TPU v7x, 32 devices: a whole 2x2x4 slice. The times are simulated.
32 devices in a mesh: crop: 2 (over x), row: 16 (over z, y, core).
Axes of the slice: x: 2, y: 2, z: 4, core: 2. Of those that a mesh axis runs over, the one named last changes fastest.
Arguments:
- pair_feats: bfloat16 [256, 2, 256, 128], P('row', 'crop'), may hold values from -6 to 6
- node_feats: bfloat16 [256, 2, 256], P('row', 'crop'), may hold values from -6 to 6
- chain_ids: int32 [2, 256], P('crop'), may hold values from 0 to 3, never falling along the last dimension, each value on 1 to 192 neighbouring positions
- out_grad: bfloat16 [256, 2, 256, 128], P('row', 'crop'), may hold values from -6 to 6
- node_out_grad: bfloat16 [256, 2, 256], P('row', 'crop'), may hold values from -6 to 6
- w_attend: float32 [256, 1024], replicated, may hold values from -0.375 to 0.375
- w_pairbias: float32 [128, 8], replicated, may hold values from -0.5 to 0.5
- w_attout: float32 [256, 256], replicated, may hold values from -1 to 1
- w_nodeup: float32 [256, 1024], replicated, may hold values from -0.375 to 0.375
- w_nodedown: float32 [1024, 256], replicated, may hold values from -0.1875 to 0.1875
- w_node: float32 [256, 64], replicated, may hold values from -0.375 to 0.375
- w_outer: float32 [1024, 128], replicated, may hold values from -0.1875 to 0.1875
- w_in: float32 [128, 1152], replicated, may hold values from -0.5 to 0.5
- w_z: float32 [256, 128], replicated, may hold values from -0.375 to 0.375
- w_up: float32 [128, 512], replicated, may hold values from -0.5 to 0.5
- w_down: float32 [512, 128], replicated, may hold values from -0.25 to 0.25
- ln_gains: float32 [1408], replicated, may hold values from 0.5 to 1.5
- m_attend: float32 [256, 1024], replicated
- m_pairbias: float32 [128, 8], replicated
- m_attout: float32 [256, 256], replicated
- m_nodeup: float32 [256, 1024], replicated
- m_nodedown: float32 [1024, 256], replicated
- m_node: float32 [256, 64], replicated
- m_outer: float32 [1024, 128], replicated
- m_in: float32 [128, 1152], replicated
- m_z: float32 [256, 128], replicated
- m_up: float32 [128, 512], replicated
- m_down: float32 [512, 128], replicated
- m_gains: float32 [1408], replicated
- v_attend: float32 [256, 1024], replicated, as said below
- v_pairbias: float32 [128, 8], replicated, as said below
- v_attout: float32 [256, 256], replicated, as said below
- v_nodeup: float32 [256, 1024], replicated, as said below
- v_nodedown: float32 [1024, 256], replicated, as said below
- v_node: float32 [256, 64], replicated, as said below
- v_outer: float32 [1024, 128], replicated, as said below
- v_in: float32 [128, 1152], replicated, as said below
- v_z: float32 [256, 128], replicated, as said below
- v_up: float32 [128, 512], replicated, as said below
- v_down: float32 [512, 128], replicated, as said below
- v_gains: float32 [1408], replicated, as said below
Outputs:
- pair_out: bfloat16 [256, 2, 256, 128], P('row', 'crop')
- node_out: bfloat16 [256, 2, 256], P('row', 'crop')
- pair_grad: float32 [256, 2, 256, 128], P('row', 'crop')
- node_grad: float32 [256, 2, 256], P('row', 'crop')
- attend_first: float32 [256, 1024], replicated
- attend_second: float32 [256, 1024], replicated
- attend_master: float32 [256, 1024], replicated
- pairbias_first: float32 [128, 8], replicated
- pairbias_second: float32 [128, 8], replicated
- pairbias_master: float32 [128, 8], replicated
- attout_first: float32 [256, 256], replicated
- attout_second: float32 [256, 256], replicated
- attout_master: float32 [256, 256], replicated
- nodeup_first: float32 [256, 1024], replicated
- nodeup_second: float32 [256, 1024], replicated
- nodeup_master: float32 [256, 1024], replicated
- nodedown_first: float32 [1024, 256], replicated
- nodedown_second: float32 [1024, 256], replicated
- nodedown_master: float32 [1024, 256], replicated
- node_first: float32 [256, 64], replicated
- node_second: float32 [256, 64], replicated
- node_master: float32 [256, 64], replicated
- outer_first: float32 [1024, 128], replicated
- outer_second: float32 [1024, 128], replicated
- outer_master: float32 [1024, 128], replicated
- inproj_first: float32 [128, 1152], replicated
- inproj_second: float32 [128, 1152], replicated
- inproj_master: float32 [128, 1152], replicated
- zproj_first: float32 [256, 128], replicated
- zproj_second: float32 [256, 128], replicated
- zproj_master: float32 [256, 128], replicated
- upproj_first: float32 [128, 512], replicated
- upproj_second: float32 [128, 512], replicated
- upproj_master: float32 [128, 512], replicated
- downproj_first: float32 [512, 128], replicated
- downproj_second: float32 [512, 128], replicated
- downproj_master: float32 [512, 128], replicated
- gains_first: float32 [1408], replicated
- gains_second: float32 [1408], replicated
- gains_master: float32 [1408], replicated
Inputs may be any that keep to these rules, and one draw needn't show every extreme that they name: `chain_ids`: along each crop the chain index never falls; each chain has at most 192 residues and one has exactly that many. `v_attend`: positive. `v_pairbias`: positive. `v_attout`: positive. `v_nodeup`: positive. `v_nodedown`: positive. `v_node`: positive. `v_outer`: positive. `v_in`: positive. `v_z`: positive. `v_up`: positive. `v_down`: positive. `v_gains`: positive.
All inputs are finite; a program needn't handle non-finite values.
Results may differ from a plain program's by a relative error of at most 0.017.
Values may be sent and summed in bfloat16 or wider, within the bound.
No kernel may reach another device: no remote copies, remote signals or barrier semaphores. Data moves between devices by JAX's collectives and lax.ppermute only.
A program may use at most 256 MiB of HBM per device.

v0:
```python
import jax
import jax.numpy as jnp
from jax import lax
from jax.sharding import PartitionSpec as P

ADAM_STEP = 4


def layer_norm(values, gain_vec):
    centred = values - jnp.mean(values, axis=-1, keepdims=True)
    spread = jnp.mean(centred * centred, axis=-1, keepdims=True)
    return centred * lax.rsqrt(spread + 1e-05) * gain_vec


def gelu_tanh(values):
    return jax.nn.gelu(values, approximate=True)


def back_dot(left, weight):
    return lax.dot_general(
        left, weight, (((left.ndim - 1,), (1,)), ((), ())), preferred_element_type=jnp.float32
    )


def cross_sum(left, right):
    left_flat = left.reshape(-1, left.shape[-1])
    right_flat = right.reshape(-1, right.shape[-1])
    return lax.dot_general(
        left_flat, right_flat, (((0,), (0,)), ((), ())), preferred_element_type=jnp.float32
    )


def adam_step(master, first_old, second_old, grad_total, rate, decay):
    first_new = 0.9 * first_old + 0.1 * grad_total
    second_new = 0.999 * second_old + 0.001 * grad_total * grad_total
    first_hat = first_new / (1.0 - 0.9**ADAM_STEP)
    second_hat = second_new / (1.0 - 0.999**ADAM_STEP)
    master_new = master - rate * (first_hat / (jnp.sqrt(second_hat) + 1e-08) + decay * master)
    return (first_new, second_new, master_new)


def shards(
    pair_feats,
    node_feats,
    chain_ids,
    out_grad,
    node_out_grad,
    w_attend,
    w_pairbias,
    w_attout,
    w_nodeup,
    w_nodedown,
    w_node,
    w_outer,
    w_in,
    w_z,
    w_up,
    w_down,
    ln_gains,
    m_attend,
    m_pairbias,
    m_attout,
    m_nodeup,
    m_nodedown,
    m_node,
    m_outer,
    m_in,
    m_z,
    m_up,
    m_down,
    m_gains,
    v_attend,
    v_pairbias,
    v_attout,
    v_nodeup,
    v_nodedown,
    v_node,
    v_outer,
    v_in,
    v_z,
    v_up,
    v_down,
    v_gains,
):
    row_count, crop_count, residues, width_z = pair_feats.shape
    width_s = node_feats.shape[2]
    head_count = w_pairbias.shape[1]
    head_dim = width_s // head_count
    score_scale = 1.0 / head_dim**0.5
    outer_dim = w_node.shape[1] // 2
    hidden = (w_in.shape[1] - width_z) // 8
    first_row = lax.axis_index("row") * row_count
    own_chain = lax.dynamic_slice_in_dim(chain_ids, first_row, row_count, 1)
    chain_equal = jnp.transpose(own_chain)[:, :, None] == chain_ids[None, :, :]
    pair_mask = chain_equal.astype(jnp.float32)[..., None]
    offset_n = width_s + width_z
    offset_s = offset_n + width_s
    offset_x = offset_s + width_s
    offset_t = offset_x + width_z
    offset_h = offset_t + 2 * hidden
    gain_a = ln_gains[:width_s]
    gain_b = ln_gains[width_s:offset_n]
    gain_n = ln_gains[offset_n:offset_s]
    gain_s = ln_gains[offset_s:offset_x]
    gain_x = ln_gains[offset_x:offset_t]
    gain_t = ln_gains[offset_t:offset_h]
    gain_h = ln_gains[offset_h:]
    att_wb = w_attend.astype(jnp.bfloat16)
    bias_wb = w_pairbias.astype(jnp.bfloat16)
    attout_wb = w_attout.astype(jnp.bfloat16)
    nodeup_wb = w_nodeup.astype(jnp.bfloat16)
    nodedown_wb = w_nodedown.astype(jnp.bfloat16)
    node_wb = w_node.astype(jnp.bfloat16)
    outer_wb = w_outer.astype(jnp.bfloat16).reshape(outer_dim, outer_dim * width_z)
    in_wb = w_in.astype(jnp.bfloat16)
    z_wb = w_z.astype(jnp.bfloat16)
    up_wb = w_up.astype(jnp.bfloat16)
    down_wb = w_down.astype(jnp.bfloat16)
    node_f32 = node_feats.astype(jnp.float32)
    pair_f32 = pair_feats.astype(jnp.float32)
    att_hat, att_back = jax.vjp(layer_norm, node_f32, gain_a)
    att_norm = att_hat.astype(jnp.bfloat16)
    qkvg = jnp.dot(att_norm, att_wb, preferred_element_type=jnp.float32)
    query = qkvg[..., :width_s].astype(jnp.bfloat16)
    key_own = qkvg[..., width_s : 2 * width_s].astype(jnp.bfloat16)
    value_own = qkvg[..., 2 * width_s : 3 * width_s].astype(jnp.bfloat16)
    att_gate = jax.nn.sigmoid(qkvg[..., 3 * width_s :])
    keys_all, values_all = (
        lax.all_gather(key_own, "row", axis=0, tiled=True),
        lax.all_gather(value_own, "row", axis=0, tiled=True),
    )
    query_heads = query.reshape(row_count, crop_count, head_count, head_dim)
    keys_heads = keys_all.reshape(residues, crop_count, head_count, head_dim)
    values_heads = values_all.reshape(residues, crop_count, head_count, head_dim)
    bias_hat, bias_back = jax.vjp(layer_norm, pair_f32, gain_b)
    bias_norm = bias_hat.astype(jnp.bfloat16)
    pair_bias = jnp.dot(bias_norm, bias_wb, preferred_element_type=jnp.float32)
    raw_scores = jnp.einsum(
        "ichd,jchd->ichj", query_heads, keys_heads, preferred_element_type=jnp.float32
    ) * score_scale + jnp.transpose(pair_bias, (0, 1, 3, 2))
    masked_scores = jnp.where(chain_equal[:, :, None, :], raw_scores, -1000000000.0)
    att_weights = jax.nn.softmax(masked_scores, axis=-1)
    weights_low = att_weights.astype(jnp.bfloat16)
    attn = jnp.einsum(
        "ichj,jchd->ichd", weights_low, values_heads, preferred_element_type=jnp.float32
    ).reshape(row_count, crop_count, width_s)
    gated = (att_gate * attn).astype(jnp.bfloat16)
    node_mid = node_f32 + jnp.dot(gated, attout_wb, preferred_element_type=jnp.float32)
    ntrans_hat, ntrans_back = jax.vjp(layer_norm, node_mid, gain_n)
    trans_node = ntrans_hat.astype(jnp.bfloat16)
    node_upv = jnp.dot(trans_node, nodeup_wb, preferred_element_type=jnp.float32)
    nact_val, nact_back = jax.vjp(gelu_tanh, node_upv)
    node_act = nact_val.astype(jnp.bfloat16)
    node_next = node_mid + jnp.dot(node_act, nodedown_wb, preferred_element_type=jnp.float32)
    node_out = node_next.astype(jnp.bfloat16)
    node_hat, node_back = jax.vjp(layer_norm, node_next, gain_s)
    node_norm = node_hat.astype(jnp.bfloat16)
    node_proj = jnp.dot(node_norm, node_wb, preferred_element_type=jnp.float32).astype(jnp.bfloat16)
    left_vec = node_proj[..., :outer_dim]
    right_vec = node_proj[..., outer_dim:]
    right_all = lax.all_gather(right_vec, "row", axis=0, tiled=True)
    outer_mix = jnp.dot(left_vec, outer_wb, preferred_element_type=jnp.float32).astype(jnp.bfloat16)
    outer_mix = outer_mix.reshape(row_count, crop_count, outer_dim, width_z)
    outer_out = jnp.einsum(
        "jcb,icbe->icje", right_all, outer_mix, preferred_element_type=jnp.float32
    )
    first_sum = pair_f32 + outer_out
    pair_hat, pair_back = jax.vjp(layer_norm, first_sum, gain_x)
    pair_norm = pair_hat.astype(jnp.bfloat16)
    projected = jnp.dot(pair_norm, in_wb, preferred_element_type=jnp.float32)
    values_part = projected[..., : 4 * hidden]
    gate_sig = jax.nn.sigmoid(projected[..., 4 * hidden : 8 * hidden])
    out_gate = jax.nn.sigmoid(projected[..., 8 * hidden :])
    gated_acts = (gate_sig * values_part * pair_mask).astype(jnp.bfloat16)
    left_out = gated_acts[..., :hidden]
    right_out = gated_acts[..., hidden : 2 * hidden]
    left_in = gated_acts[..., 2 * hidden : 3 * hidden]
    right_in = gated_acts[..., 3 * hidden :]
    columns_in = lax.all_to_all(left_in, "row", split_axis=2, concat_axis=0, tiled=True)
    piece_out = lax.all_gather(right_out, "row", axis=0, tiled=True)
    piece_in = lax.all_gather(right_in, "row", axis=0, tiled=True)
    block_out = jnp.einsum(
        "ickh,jckh->icjh", left_out, piece_out, preferred_element_type=jnp.float32
    )
    tri_out = block_out
    tri_in = jnp.einsum("kcih,kcjh->icjh", columns_in, piece_in, preferred_element_type=jnp.float32)
    tri_out, tri_in = (tri_out, tri_in)
    combined = jnp.concatenate([tri_out, tri_in], axis=-1)
    tri_hat, tri_back = jax.vjp(layer_norm, combined, gain_t)
    tri_norm = tri_hat.astype(jnp.bfloat16)
    tri_proj = jnp.dot(tri_norm, z_wb, preferred_element_type=jnp.float32)
    second_sum = first_sum + out_gate * tri_proj * pair_mask
    trans_hat, trans_back = jax.vjp(layer_norm, second_sum, gain_h)
    trans_in = trans_hat.astype(jnp.bfloat16)
    up_proj = jnp.dot(trans_in, up_wb, preferred_element_type=jnp.float32)
    act_val, act_back = jax.vjp(gelu_tanh, up_proj)
    activated = act_val.astype(jnp.bfloat16)
    down_proj = jnp.dot(activated, down_wb, preferred_element_type=jnp.float32)
    pair_out = (second_sum + down_proj).astype(jnp.bfloat16)
    grad_three = out_grad.astype(jnp.float32)
    grad_down = cross_sum(activated, out_grad)
    (grad_act,) = act_back(back_dot(out_grad, down_wb))
    grad_upin = grad_act.astype(jnp.bfloat16)
    grad_up = cross_sum(trans_in, grad_upin)
    trans_grad, gain_h_grad = trans_back(back_dot(grad_upin, up_wb))
    grad_two = grad_three + trans_grad
    grad_triproj = (grad_two * out_gate * pair_mask).astype(jnp.bfloat16)
    grad_outgate = grad_two * tri_proj * pair_mask * out_gate * (1.0 - out_gate)
    grad_z = cross_sum(tri_norm, grad_triproj)
    comb_grad, gain_t_grad = tri_back(back_dot(grad_triproj, z_wb))
    comb_low = comb_grad.astype(jnp.bfloat16)
    tri_grad_out = comb_low[..., :hidden]
    tri_grad_in = comb_low[..., hidden:]
    grad_rows = lax.all_to_all(tri_grad_out, "row", split_axis=2, concat_axis=0, tiled=True)
    piece_out = lax.all_gather(right_out, "row", axis=0, tiled=True)
    piece_in = lax.all_gather(right_in, "row", axis=0, tiled=True)
    piece_left = lax.all_gather(left_out, "row", axis=0, tiled=True)
    full_piece_grad = lax.all_gather(tri_grad_in, "row", axis=0, tiled=True)
    left_acc = jnp.einsum(
        "icjh,jckh->ickh", tri_grad_out, piece_out, preferred_element_type=jnp.float32
    )
    col_block = jnp.einsum(
        "kcjh,icjh->kcih", piece_in, tri_grad_in, preferred_element_type=jnp.float32
    )
    right_acc = jnp.einsum(
        "icjh,ickh->jckh", grad_rows, piece_left, preferred_element_type=jnp.float32
    )
    rin_acc = jnp.einsum(
        "kcih,icjh->kcjh", left_in, full_piece_grad, preferred_element_type=jnp.float32
    )
    left_in_grad = lax.all_to_all(
        col_block.astype(jnp.bfloat16), "row", split_axis=0, concat_axis=2, tiled=True
    )
    acts_grad = jnp.concatenate(
        [
            left_acc.astype(jnp.bfloat16),
            right_acc.astype(jnp.bfloat16),
            left_in_grad,
            rin_acc.astype(jnp.bfloat16),
        ],
        axis=-1,
    ).astype(jnp.float32)
    grad_proj = jnp.concatenate(
        [
            acts_grad * gate_sig * pair_mask,
            acts_grad * values_part * pair_mask * gate_sig * (1.0 - gate_sig),
            grad_outgate,
        ],
        axis=-1,
    ).astype(jnp.bfloat16)
    grad_in = cross_sum(pair_norm, grad_proj)
    pnorm_grad, gain_x_grad = pair_back(back_dot(grad_proj, in_wb))
    first_grad = grad_two + pnorm_grad
    first_low = first_grad.astype(jnp.bfloat16)
    mix_grad = jnp.einsum(
        "jcb,icje->icbe", right_all, first_low, preferred_element_type=jnp.float32
    ).astype(jnp.bfloat16)
    right_part = jnp.einsum(
        "icbe,icje->jcb", outer_mix, first_low, preferred_element_type=jnp.float32
    )
    right_grad = lax.psum_scatter(right_part, "row", scatter_dimension=0, tiled=True)
    mix_flat = mix_grad.reshape(row_count, crop_count, outer_dim * width_z)
    left_grad = back_dot(mix_flat, outer_wb)
    grad_outer = cross_sum(left_vec, mix_flat).reshape(outer_dim * outer_dim, width_z)
    proj_grad = jnp.concatenate([left_grad, right_grad], axis=-1).astype(jnp.bfloat16)
    grad_node = cross_sum(node_norm, proj_grad)
    outer_node_grad, gain_s_grad = node_back(back_dot(proj_grad, node_wb))
    grad_next = node_out_grad.astype(jnp.float32) + outer_node_grad
    next_low = grad_next.astype(jnp.bfloat16)
    grad_nodedown = cross_sum(node_act, next_low)
    (nact_grad,) = nact_back(back_dot(next_low, nodedown_wb))
    nodeup_low = nact_grad.astype(jnp.bfloat16)
    grad_nodeup = cross_sum(trans_node, nodeup_low)
    ntrans_grad, gain_n_grad = ntrans_back(back_dot(nodeup_low, nodeup_wb))
    grad_mid = grad_next + ntrans_grad
    mid_low = grad_mid.astype(jnp.bfloat16)
    grad_attout = cross_sum(gated, mid_low)
    gated_grad = back_dot(mid_low, attout_wb)
    attn_grad = (gated_grad * att_gate).astype(jnp.bfloat16)
    gate_logit_grad = gated_grad * attn * att_gate * (1.0 - att_gate)
    attn_grad_heads = attn_grad.reshape(row_count, crop_count, head_count, head_dim)
    weight_grad = jnp.einsum(
        "ichd,jchd->ichj", attn_grad_heads, values_heads, preferred_element_type=jnp.float32
    )
    score_grad = (
        att_weights * (weight_grad - jnp.sum(weight_grad * att_weights, axis=-1, keepdims=True))
    ).astype(jnp.bfloat16)
    query_grad = (
        jnp.einsum("ichj,jchd->ichd", score_grad, keys_heads, preferred_element_type=jnp.float32)
        * score_scale
    )
    key_term = (
        jnp.einsum("ichj,ichd->jchd", score_grad, query_heads, preferred_element_type=jnp.float32)
        * score_scale
    )
    value_term = jnp.einsum(
        "ichj,ichd->jchd", weights_low, attn_grad_heads, preferred_element_type=jnp.float32
    )
    key_grad, value_grad = (
        lax.psum_scatter(
            key_term.reshape(residues, crop_count, width_s), "row", scatter_dimension=0, tiled=True
        ),
        lax.psum_scatter(
            value_term.reshape(residues, crop_count, width_s),
            "row",
            scatter_dimension=0,
            tiled=True,
        ),
    )
    qkvg_grad = jnp.concatenate(
        [query_grad.reshape(row_count, crop_count, width_s), key_grad, value_grad, gate_logit_grad],
        axis=-1,
    ).astype(jnp.bfloat16)
    grad_attend = cross_sum(att_norm, qkvg_grad)
    att_in_grad, gain_a_grad = att_back(back_dot(qkvg_grad, att_wb))
    node_grad = grad_mid + att_in_grad
    bias_grad = jnp.transpose(score_grad, (0, 1, 3, 2))
    grad_pairbias = cross_sum(bias_norm, bias_grad)
    bias_in_grad, gain_b_grad = bias_back(back_dot(bias_grad, bias_wb))
    pair_grad = first_grad + bias_in_grad
    gain_grad = jnp.concatenate(
        [gain_a_grad, gain_b_grad, gain_n_grad, gain_s_grad, gain_x_grad, gain_t_grad, gain_h_grad]
    )
    local_grads = [
        grad_attend,
        grad_pairbias,
        grad_attout,
        grad_nodeup,
        grad_nodedown,
        grad_node,
        grad_outer,
        grad_in,
        grad_z,
        grad_up,
        grad_down,
        gain_grad,
    ]
    flat_grads = jnp.concatenate([piece_grad.reshape(-1) for piece_grad in local_grads])
    summed_grads = lax.psum(flat_grads, ("crop", "row"))
    masters = [
        w_attend,
        w_pairbias,
        w_attout,
        w_nodeup,
        w_nodedown,
        w_node,
        w_outer,
        w_in,
        w_z,
        w_up,
        w_down,
        ln_gains,
    ]
    firsts = [
        m_attend,
        m_pairbias,
        m_attout,
        m_nodeup,
        m_nodedown,
        m_node,
        m_outer,
        m_in,
        m_z,
        m_up,
        m_down,
        m_gains,
    ]
    seconds = [
        v_attend,
        v_pairbias,
        v_attout,
        v_nodeup,
        v_nodedown,
        v_node,
        v_outer,
        v_in,
        v_z,
        v_up,
        v_down,
        v_gains,
    ]
    rates = [0.1] * 11 + [1.0]
    decays = [0.1] * 11 + [0.0]
    results = [pair_out, node_out, pair_grad, node_grad]
    offset = 0
    for master, first_old, second_old, local_grad, rate, decay in zip(
        masters, firsts, seconds, local_grads, rates, decays
    ):
        count_here = local_grad.size
        total_grad = summed_grads[offset : offset + count_here].reshape(master.shape)
        offset = offset + count_here
        first_new, second_new, master_new = adam_step(
            master, first_old, second_old, total_grad, rate, decay
        )
        results.append(first_new)
        results.append(second_new)
        results.append(master_new)
    return tuple(results)


def solution(mesh):
    return jax.shard_map(
        shards,
        mesh=mesh,
        in_specs=(
            P("row", "crop", None, None),
            P("row", "crop", None),
            P("crop", None),
            P("row", "crop", None, None),
            P("row", "crop", None),
            P(),
            P(),
            P(),
            P(),
            P(),
            P(),
            P(),
            P(),
            P(),
            P(),
            P(),
            P(),
            P(),
            P(),
            P(),
            P(),
            P(),
            P(),
            P(),
            P(),
            P(),
            P(),
            P(),
            P(),
            P(),
            P(),
            P(),
            P(),
            P(),
            P(),
            P(),
            P(),
            P(),
            P(),
            P(),
            P(),
        ),
        out_specs=(
            P("row", "crop", None, None),
            P("row", "crop", None),
            P("row", "crop", None, None),
            P("row", "crop", None),
            P(),
            P(),
            P(),
            P(),
            P(),
            P(),
            P(),
            P(),
            P(),
            P(),
            P(),
            P(),
            P(),
            P(),
            P(),
            P(),
            P(),
            P(),
            P(),
            P(),
            P(),
            P(),
            P(),
            P(),
            P(),
            P(),
            P(),
            P(),
            P(),
            P(),
            P(),
            P(),
            P(),
            P(),
            P(),
            P(),
        ),
        check_vma=False,
    )
```

profile of v0, /device:TPU:0, one launch (start us, length us, event | category | flops | bytes accessed | tf_op | source)
XLA Modules:
  0.0 1104.6 jit_solution(18278463742426891686)
XLA Ops:
  13.5 23.4 %all_gather.24 = bf16[256,1,256]{2,0,1:T(8,128)(2,1)S(1)} all-gather(bf16[16,1,256]{2,0,1:T(8,128)(2,1)S(1)} %get-tuple-element.320), channel_id=1, replica_groups=mesh['crop'=2,'row'=16] {'row'}, dimensions={0}, use_global_device_ids=true | all-gather | bytes 139264 | tf_op jit(solution)/shard_map/all_gather | solution.py:129
  37.1 17.8 %all_gather.23 = bf16[256,1,256]{2,0,1:T(8,128)(2,1)S(1)} all-gather(bf16[16,1,256]{2,0,1:T(8,128)(2,1)S(1)} %get-tuple-element.321), channel_id=1, replica_groups=mesh['crop'=2,'row'=16] {'row'}, dimensions={0}, use_global_device_ids=true | all-gather | bytes 139264 | tf_op jit(solution)/shard_map/all_gather | solution.py:130
  65.3 18.9 %all_gather.25 = bf16[256,1,32]{2,0,1:T(8,128)(2,1)S(1)} all-gather(bf16[16,1,32]{2,0,1:T(8,128)(2,1)S(1)} %slice.193), channel_id=1, replica_groups=mesh['crop'=2,'row'=16] {'row'}, dimensions={0}, use_global_device_ids=true | all-gather | bytes 17408 | tf_op jit(solution)/shard_map/all_gather | solution.py:161
  109.3 38.3 %all-to-all-done = bf16[16,1,256,128]{3,0,1,2:T(8,128)(2,1)S(1)} async-done(((bf16[16,1,256,128]{3,0,1,2:T(8,128)(2,1)}), bf16[16,1,256,128]{3,0,1,2:T(8,128)(2,1)S(1)}, u32[]{:S(2)}, u32[]{:S(2)}) %all-to-all-start) | async-done | bytes 1048608 | tf_op jit(solution)/shard_map/all_to_all | solution.py:179
  150.2 95.0 %all-gather.5.cloned.1.call-done = bf16[256,1,256,128]{3,2,1,0:T(8,128)(2,1)} async-done(((bf16[16,1,256,128]{3,2,1,0:T(8,128)(2,1)}), bf16[256,1,256,128]{3,2,1,0:T(8,128)(2,1)}) %all-gather.5.cloned.1.call-update) | async-done | bytes 16777232 | tf_op jit(solution)/shard_map/all_gather | solution.py:180
  245.2 23.6 %copy.397 = bf16[256,1,256,128]{2,0,3,1:T(8,128)(2,1)} copy(bf16[256,1,256,128]{3,2,1,0:T(8,128)(2,1)} %all-gather.5.cloned.1.call-done) | data formatting | bytes 33554432 | tf_op jit(solution)/shard_map/all_gather | solution.py:180
  268.7 104.3 %all-gather.7.cloned.1.call-done = bf16[256,1,256,128]{3,2,1,0:T(8,128)(2,1)} async-done(((bf16[16,1,256,128]{3,2,1,0:T(8,128)(2,1)}), bf16[256,1,256,128]{3,2,1,0:T(8,128)(2,1)}) %all-gather.7.cloned.1.call-update) | async-done | bytes 16777232 | tf_op jit(solution)/shard_map/all_gather | solution.py:181
  373.0 22.1 %copy.400 = bf16[256,1,256,128]{2,0,3,1:T(8,128)(2,1)} copy(bf16[256,1,256,128]{3,2,1,0:T(8,128)(2,1)} %all-gather.7.cloned.1.call-done) | data formatting | bytes 33554432 | tf_op jit(solution)/shard_map/all_gather | solution.py:181
  395.1 10.6 bitcast_reduce_fusion
  406.9 7.7 bitcast_reduce_fusion.1
  457.1 8.9 fusion.47
  477.0 11.6 %fusion.68 = bf16[256,1,16,128]{0,2,3,1:T(8,128)(2,1)} fusion(bf16[256,1,256,128]{2,0,3,1:T(8,128)(2,1)} %copy.400, bf16[16,1,256,256]{2,0,3,1:T(8,128)(2,1)} %copy-done.13), kind=kOutput, calls=%fused_computation.115 | convolution fusion | flops 268959744 | bytes 18874368 | tf_op jit(solution)/shard_map/kcjh,icjh->kcih/dot_general | solution.py:222
  491.8 9.4 fusion.8
  501.2 14.9 %all-to-all-done.1 = bf16[16,1,256,128]{3,0,1,2:T(8,128)(2,1)} async-done(((bf16[16,1,256,128]{3,0,1,2:T(8,128)(2,1)}), bf16[16,1,256,128]{3,0,1,2:T(8,128)(2,1)}, u32[]{:S(2)}, u32[]{:S(2)}) %all-to-all-start.1) | async-done | bytes 1048608 | tf_op jit(solution)/shard_map/all_to_all | solution.py:214
  516.2 8.4 all-to-all-start.2
  529.7 22.4 %copy.414 = bf16[256,1,256,128]{2,0,3,1:T(8,128)(2,1)} copy(bf16[256,1,256,128]{3,2,1,0:T(8,128)(2,1)} %all-gather.9.cloned.1.call-done) | data formatting | bytes 33554432 | tf_op jit(solution)/shard_map/all_gather | solution.py:217
  559.2 8.1 fusion.2
  573.4 96.1 %all-gather.11.cloned.1.call-done = bf16[256,1,256,128]{2,0,3,1:T(8,128)(2,1)} async-done(((bf16[16,1,256,128]{2,0,3,1:T(8,128)(2,1)}), bf16[256,1,256,128]{2,0,3,1:T(8,128)(2,1)}) %all-gather.11.cloned.1.call-update) | async-done | bytes 16777232 | tf_op jit(solution)/shard_map/all_gather | solution.py:218
  669.5 8.4 fusion
  687.0 7.8 fusion.40
  704.3 50.3 %reduce-scatter.4.cloned.1.call-done = f32[16,1,32]{2,0,1:T(8,128)} async-done(((f32[256,1,32]{2,0,1:T(8,128)}), f32[16,1,32]{2,0,1:T(8,128)}) %reduce-scatter.4.cloned.1.call-update) | async-done | bytes 2064 | tf_op jit(solution)/shard_map/reduce_scatter | solution.py:261
  793.7 38.5 %reduce-scatter.6.cloned.1.call-done = f32[16,1,256]{2,0,1:T(8,128)} async-done(((f32[256,1,256]{2,0,1:T(8,128)}), f32[16,1,256]{2,0,1:T(8,128)}) %reduce-scatter.6.cloned.1.call-update) | async-done | bytes 16400 | tf_op jit(solution)/shard_map/reduce_scatter | solution.py:300
  832.9 57.8 %reduce-scatter.8.cloned.1.call-done = f32[16,1,256]{2,0,1:T(8,128)} async-done(((f32[256,1,256]{2,0,1:T(8,128)}), f32[16,1,256]{2,0,1:T(8,128)}) %reduce-scatter.8.cloned.1.call-update) | async-done | bytes 16400 | tf_op jit(solution)/shard_map/reduce_scatter | solution.py:303
  935.9 130.7 %all-reduce.2.cloned.1.call-done = f32[1313152]{0:T(1024)} async-done(((f32[1313152]{0:T(1024)}), f32[1313152]{0:T(1024)}) %all-reduce.2.cloned.1.call-update) | async-done | bytes 5252624 | tf_op jit(solution)/shard_map/psum | solution.py:339
  (592 shorter events, 252.8 us)
Async XLA Ops:
  7.3 237.9 %all-gather.5.cloned.1.call-start = ((), (), s32[]{:S(2)}) async-start(), calls=%async_computation.6 | async-start | bytes 17825792 | tf_op jit(solution)/shard_map/all_gather | solution.py:180
  11.5 72.8 %copy-start.6 = (bf16[16,1,256,128]{2,3,0,1:T(8,128)(2,1)}, bf16[16,1,256,128]{2,3,0,1:T(8,128)(2,1)S(1)}, u32[]{:S(2)}) copy-start(bf16[16,1,256,128]{2,3,0,1:T(8,128)(2,1)S(1)} %copy.386) | copy-start | bytes 3145732
  98.6 274.4 %all-gather.7.cloned.1.call-start = ((), (), s32[]{:S(2)}) async-start(), calls=%async_computation.7 | async-start | bytes 17825792 | tf_op jit(solution)/shard_map/all_gather | solution.py:181
  100.9 428.8 %all-gather.9.cloned.1.call-start = ((), (), s32[]{:S(2)}) async-start(), calls=%async_computation.8 | async-start | bytes 17825792 | tf_op jit(solution)/shard_map/all_gather | solution.py:217
  104.1 43.5 %all-to-all-start = ((bf16[16,1,256,128]{3,0,1,2:T(8,128)(2,1)}), bf16[16,1,256,128]{3,0,1,2:T(8,128)(2,1)S(1)}, u32[]{:S(2)}, u32[]{:S(2)}) async-start(bf16[16,1,256,128]{3,0,1,2:T(8,128)(2,1)} %copy.401), calls=%async_computation | async-start | bytes 2097152 | tf_op jit(solution)/shard_map/all_to_all | solution.py:179
  107.7 561.8 %all-gather.11.cloned.1.call-start = ((), (), s32[]{:S(2)}) async-start(), calls=%async_computation.9 | async-start | bytes 17825792 | tf_op jit(solution)/shard_map/all_gather | solution.py:218
  425.3 99.3 %copy-start.3 = (f32[16,1,256,128]{2,3,0,1:T(8,128)}, f32[16,1,256,128]{2,3,0,1:T(8,128)S(1)}, u32[]{:S(2)}) copy-start(f32[16,1,256,128]{2,3,0,1:T(8,128)S(1)} %get-tuple-element.299) | copy-start | bytes 6291460
  472.7 43.5 %all-to-all-start.1 = ((bf16[16,1,256,128]{3,0,1,2:T(8,128)(2,1)}), bf16[16,1,256,128]{3,0,1,2:T(8,128)(2,1)}, u32[]{:S(2)}, u32[]{:S(2)}) async-start(bf16[16,1,256,128]{3,0,1,2:T(8,128)(2,1)} %copy.415), calls=%async_computation.1 | async-start | bytes 2097152 | tf_op jit(solution)/shard_map/all_to_all | solution.py:214
  516.2 52.4 %all-to-all-start.2 = ((bf16[256,1,16,128]{3,2,1,0:T(8,128)(2,1)}), bf16[256,1,16,128]{3,2,1,0:T(8,128)(2,1)}, u32[]{:S(2)}, u32[]{:S(2)}) async-start(bf16[256,1,16,128]{3,2,1,0:T(8,128)(2,1)} %copy.420), calls=%async_computation.2 | async-start | bytes 2097152 | tf_op jit(solution)/shard_map/all_to_all | solution.py:231
  524.5 230.1 %reduce-scatter.4.cloned.1.call-start = ((), (), s32[]{:S(2)}) async-start(), calls=%async_computation.10 | async-start | bytes 139264 | tf_op jit(solution)/shard_map/reduce_scatter | solution.py:261
  571.0 107.3 %slice-start = ((s8[18874368]{0:T(1024)(128)(4,1)}), s8[2097152]{0:T(1024)(128)(4,1)S(1)}, s32[]{:S(2)}) async-start(s8[18874368]{0:T(1024)(128)(4,1)} %bitcast.508), calls=%async_computation.14 | async-start | bytes 4194304
  699.4 59.1 %copy-start.22 = (f32[1024,256]{1,0:T(8,128)S(1)}, f32[1024,256]{1,0:T(8,128)}, u32[]{:S(2)}) copy-start(f32[1024,256]{1,0:T(8,128)} %param.50) | copy-start | bytes 3145732
  699.4 59.1 %copy-start.63 = (f32[16,1024]{1,0:T(8,128)S(1)}, f32[16,1024]{1,0:T(8,128)}, u32[]{:S(2)}) copy-start(f32[16,1024]{1,0:T(8,128)} %copy-done.62) | copy-start | bytes 196612
  699.4 59.4 %copy-start.20 = (f32[256,1024]{1,0:T(8,128)S(1)}, f32[256,1024]{1,0:T(8,128)}, u32[]{:S(2)}) copy-start(f32[256,1024]{1,0:T(8,128)} %param.49) | copy-start | bytes 3145732
  699.4 59.4 %copy-start.71 = (f32[16,1,256]{2,0,1:T(8,128)S(1)}, f32[16,1,256]{2,0,1:T(8,128)}, u32[]{:S(2)}) copy-start(f32[16,1,256]{2,0,1:T(8,128)} %copy-done.70) | copy-start | bytes 49156
  699.4 63.2 %copy-start.43 = (f32[256,256]{1,0:T(8,128)S(1)}, f32[256,256]{1,0:T(8,128)}, u32[]{:S(2)}) copy-start(f32[256,256]{1,0:T(8,128)} %param.48) | copy-start | bytes 786436
  701.0 67.3 %copy-start.55 = (bf16[256,1,256]{0,2,1:T(8,128)(2,1)S(1)}, bf16[256,1,256]{0,2,1:T(8,128)(2,1)}, u32[]{:S(2)}) copy-start(bf16[256,1,256]{0,2,1:T(8,128)(2,1)} %copy-done.54) | copy-start | bytes 393220
  701.2 131.0 %reduce-scatter.6.cloned.1.call-start = ((), (), s32[]{:S(2)}) async-start(), calls=%async_computation.11 | async-start | bytes 278528 | tf_op jit(solution)/shard_map/reduce_scatter | solution.py:300
  777.7 113.0 %reduce-scatter.8.cloned.1.call-start = ((), (), s32[]{:S(2)}) async-start(), calls=%async_computation.12 | async-start | bytes 278528 | tf_op jit(solution)/shard_map/reduce_scatter | solution.py:303
  789.3 102.2 %copy-start.79 = (bf16[16,1,256]{2,0,1:T(8,128)(2,1)S(1)}, bf16[16,1,256]{2,0,1:T(8,128)(2,1)}, u32[]{:S(2)}) copy-start(bf16[16,1,256]{2,0,1:T(8,128)(2,1)} %param.42) | copy-start | bytes 24580
  789.3 102.2 %copy-start.123 = (bf16[16,256]{1,0:T(8,128)(2,1)S(1)}, bf16[16,256]{1,0:T(8,128)(2,1)}, u32[]{:S(2)}) copy-start(bf16[16,256]{1,0:T(8,128)(2,1)} %get-tuple-element.317) | copy-start | bytes 24580
  791.4 104.3 %copy-start.15 = (f32[16,256,128]{1,2,0:T(8,128)}, f32[16,256,128]{1,2,0:T(8,128)S(1)}, u32[]{:S(2)}) copy-start(f32[16,256,128]{1,2,0:T(8,128)S(1)} %get-tuple-element.354) | copy-start | bytes 6291460
  791.4 275.2 %all-reduce.2.cloned.1.call-start = ((), (), s32[]{:S(2)}) async-start(), calls=%async_computation.13 | async-start | bytes 10510336 | tf_op jit(solution)/shard_map/psum | solution.py:339
  832.9 58.6 %copy-start.124 = (bf16[16,256]{1,0:T(8,128)(2,1)}, bf16[16,256]{1,0:T(8,128)(2,1)S(1)}, u32[]{:S(2)}) copy-start(bf16[16,256]{1,0:T(8,128)(2,1)S(1)} %convert_bitcast_fusion.1) | copy-start | bytes 24580
  (174 other events, 1963.1 us)
Sparse Core Ops, SparseCore 0:
  98.7 146.4 all-gather.4
  247.9 125.0 all-gather.6
  375.7 145.6 all-gather.8
  524.0 145.4 all-gather.10
  701.3 53.2 reduce-scatter.3
  777.8 54.3 reduce-scatter.5
  836.3 54.3 reduce-scatter.7
  919.2 147.3 all-reduce.1
where the time goes:
time: 1120 us; the launch traced here: 1100 us
  waiting for transfers between devices  626 us (56%)
  local copies, waits for them, and re-layouts  175 us (16%)
  matrix products  128 us (11%)
  other arithmetic  81.2 us (7%)
  blocking collectives  60.2 us (5%)
  between operations  17 us (2%)
  starting transfers between devices  16.9 us (2%)
    psum x1, waiting for transfers between devices, shards(): summed_grads = lax.psum(flat_grads, ('crop', 'row'))  131 us
    all_gather x1, waiting for transfers between devices, shards(): piece_in = lax.all_gather(right_in, 'row', axis=0, tiled=True)  104 us
    all_gather x1, waiting for transfers between devices, shards(): full_piece_grad = lax.all_gather(tri_grad_in, 'row', axis=0, tiled=True)  96.1 us
    all_gather x1, waiting for transfers between devices, shards(): piece_out = lax.all_gather(right_out, 'row', axis=0, tiled=True)  95 us
    reduce_scatter x1, waiting for transfers between devices, shards(): lax.psum_scatter(value_term.reshape(residues, crop_count, width_s), 'row'...  57.8 us
    reduce_scatter x1, waiting for transfers between devices, shards(): lax.psum_scatter(right_part, 'row', scatter_dimension=0, tiled=True)  50.3 us
    unnamed x395, local copies, waits for them, and re-layouts  47.4 us
    reduce_scatter x1, waiting for transfers between devices, shards(): lax.psum_scatter(key_term.reshape(residues, crop_count, width_s), 'row',...  38.5 us
  transfers between devices with their start and end apart: 11, of which 9 were waited for; matrix products, arithmetic and copies ran while one was open for 21% of the time, Pallas kernels for 0%

commit v1 on v0

v1 whole, which is shorter than its diff:
```python
import functools
import jax
import jax.numpy as jnp
from jax import lax
from jax.experimental import pallas as pl
from jax.experimental.pallas import tpu as pltpu
from jax.sharding import PartitionSpec as P

ADAM_STEP = 4
EPS = 1e-05
BF = jnp.bfloat16
F32 = jnp.float32
LANES = 128
HALF = 64
BOTH = ("crop", "row")
NN = (((1,), (0,)), ((), ()))
NT = (((1,), (1,)), ((), ()))
TN = (((0,), (0,)), ((), ()))


def mm(left, right, dims=NN):
    return lax.dot_general(left, right, dims, preferred_element_type=F32)


def layer_norm(values, gain_vec):
    centred = values - jnp.mean(values, axis=-1, keepdims=True)
    spread = jnp.mean(centred * centred, axis=-1, keepdims=True)
    return centred * lax.rsqrt(spread + EPS) * gain_vec


def gelu_tanh(values):
    return jax.nn.gelu(values, approximate=True)


def back_dot(left, weight):
    return mm(left, weight, NT)


def cross_sum(left, right):
    return mm(left, right, TN)


def adam_step(master, first_old, second_old, grad_total, rate, decay):
    first_new = 0.9 * first_old + 0.1 * grad_total
    second_new = 0.999 * second_old + 0.001 * grad_total * grad_total
    first_hat = first_new / (1.0 - 0.9**ADAM_STEP)
    second_hat = second_new / (1.0 - 0.999**ADAM_STEP)
    master_new = master - rate * (first_hat / (jnp.sqrt(second_hat) + 1e-08) + decay * master)
    return (first_new, second_new, master_new)


def gather_all(part, row_devices):
    every = 2 * row_devices
    groups = [[d for d in range(every) if d % 2 == k] for k in range(2)]
    spread = jnp.broadcast_to(part[None], (every // 2,) + part.shape)
    got = lax.all_to_all(
        spread, BOTH, split_axis=0, concat_axis=0, tiled=True, axis_index_groups=groups
    )
    other = lax.ppermute(got, "row", [(d, d ^ 1) for d in range(row_devices)])
    odd = lax.axis_index("row") % 2 == 1
    pair = [jnp.where(odd, other, got), jnp.where(odd, got, other)]
    return jnp.stack(pair, axis=1).reshape((every,) + part.shape)


def scatter_sum(flat, row_devices):
    every = 2 * row_devices
    unit = every * 16 * LANES
    sent = jnp.pad(flat, (0, -flat.shape[0] % unit)).astype(BF).reshape(every, -1, LANES)
    parts = lax.all_to_all(sent, BOTH, split_axis=0, concat_axis=0, tiled=True)
    return jnp.sum(parts.astype(F32), axis=0).astype(BF)


def after(value, event):
    return lax.optimization_barrier((value, event))[0]


def join_flat(parts):
    return jnp.concatenate([part.reshape(-1) for part in parts])


def split_flat(flat, parts):
    found, start = [], 0
    for part in parts:
        found.append(flat[start : start + part.size].reshape(part.shape))
        start = start + part.size
    return found


def lanes_sum(acc):
    return jnp.sum(acc, axis=1)


def norm_rows(values):
    centred = values - jnp.mean(values, axis=0, keepdims=True)
    inv = lax.rsqrt(jnp.mean(centred * centred, axis=0, keepdims=True) + EPS)
    return centred * inv, inv


def norm_rows_back(scaled, hat, inv):
    return inv * (
        scaled
        - jnp.mean(scaled, axis=0, keepdims=True)
        - hat * jnp.mean(scaled * hat, axis=0, keepdims=True)
    )


def turn(values):
    return pltpu.roll(values, HALF, values.ndim - 1)


def low_lanes(shape):
    return lax.broadcasted_iota(jnp.int32, shape, len(shape) - 1) < HALF


def fold_pair(first, second):
    low = low_lanes((first.shape[0], LANES))
    f_lo, f_hi = first[:, :LANES], first[:, LANES:]
    s_lo, s_hi = second[:, :LANES], second[:, LANES:]
    f_turn, s_turn = turn(f_hi), turn(s_hi)
    main_f = f_lo + jnp.where(low, f_turn, 0.0)
    main_s = s_lo + jnp.where(low, s_turn, 0.0)
    return main_f, main_s, jnp.where(low, f_hi, s_turn)


def unfold_pair(main_f, main_s, tail):
    low = low_lanes(tail.shape)
    first = jnp.concatenate([main_f, jnp.where(low, tail, turn(main_f))], axis=1)
    second = jnp.concatenate([main_s, jnp.where(low, turn(tail), turn(main_s))], axis=1)
    return first, second


def put_tile(stage_ref, tile, row, rows, values):
    high = values.shape[0]
    stage_ref[pl.ds(tile * high * rows + row, high, stride=rows), :] = values


def get_tile(stage_ref, tile, row, rows, high):
    return stage_ref[pl.ds(tile * high * rows + row, high, stride=rows), :]


def ship(stage_ref, send_ref, tiles, share, rows):
    devices = send_ref.shape[0]
    span = share * rows
    for t in range(tiles):
        block = stage_ref[t * devices * span : (t + 1) * devices * span]
        send_ref[:, t * span : (t + 1) * span] = block.reshape(devices, span, LANES).astype(BF)


def unship(got_ref, stage_ref, tiles, share, rows):
    devices = got_ref.shape[0]
    span = share * rows
    for t in range(tiles):
        block = got_ref[:, t * span : (t + 1) * span].astype(F32)
        stage_ref[t * devices * span : (t + 1) * devices * span] = block.reshape(-1, LANES)


def bias_kernel(x_ref, gain_ref, weight_ref, xt_ref, bias_ref):
    for r in range(x_ref.shape[0]):
        xt = x_ref[r].astype(F32).T
        xt_ref[r] = xt.astype(BF)
        hat, _ = norm_rows(xt)
        bias_ref[r] = mm(weight_ref[...], (hat * gain_ref[...]).astype(BF))


def first_kernel(
    share, rows, xt_ref, mix_ref, right_ref, mask_ref, gain_ref, weight_ref, ride_ref,
    sum_ref, send_ref, *stage,
):
    hidden = weight_ref.shape[0] // 9
    for r in range(xt_ref.shape[0]):
        row = pl.program_id(0) * xt_ref.shape[0] + r
        total = xt_ref[r].astype(F32) + mm(mix_ref[r], right_ref[...], TN)
        sum_ref[r] = total
        hat, _ = norm_rows(total)
        norm = (hat * gain_ref[...]).astype(BF)
        mask = mask_ref[r]
        acts = []
        for block in range(4):
            value = mm(weight_ref[block * hidden : (block + 1) * hidden], norm)
            gate = mm(weight_ref[(block + 4) * hidden : (block + 5) * hidden], norm)
            acts.append(jax.nn.sigmoid(gate) * value * mask)
        for pair in range(2):
            tiles = fold_pair(acts[2 * pair], acts[2 * pair + 1])
            for t in range(3):
                if stage:
                    put_tile(stage[0], 3 * pair + t, row, rows, tiles[t])
                else:
                    send_ref[r, 3 * pair + t] = tiles[t].astype(BF)
    if stage:

        @pl.when(pl.program_id(0) == pl.num_programs(0) - 1)
        def _():
            ship(stage[0], send_ref, 6, share, rows)
            send_ref[:, 6 * share * rows :] = ride_ref[...]


def chain_mask(col_ref, row_ref):
    return col_ref[...] == row_ref[...]


def channel_rows(dims, tile):
    share, rows = dims
    return pl.ds(pl.multiple_of((tile * share + pl.program_id(0)) * rows, rows), rows)


def flat_rows(ref, tile, dims):
    block = ref[:, channel_rows(dims, tile)] if dims else ref[:, tile, 0]
    return block.reshape(-1, block.shape[-1])


def slot_operands(ref, pair, dims):
    main_f, main_s, tail = (flat_rows(ref, 3 * pair + t, dims).astype(F32) for t in range(3))
    low = low_lanes(tail.shape)
    zero = jnp.zeros_like(tail)
    first = jnp.concatenate([main_f, jnp.where(low, tail, zero)], axis=1).astype(BF)
    second = jnp.concatenate([main_s, jnp.where(low, turn(tail), zero)], axis=1).astype(BF)
    return first, second


def raw_columns(slots, same):
    values = slots.astype(F32)
    main, tail = values[:, :LANES], values[:, LANES:]
    wide = jnp.concatenate(
        [main, jnp.where(low_lanes(tail.shape), tail, turn(main))], axis=1
    )
    return jnp.where(same, wide, 0.0).astype(BF)


def store_tiles(out_ref, pair, dims, tiles):
    for t in range(3):
        block = tiles[t].astype(BF).reshape(out_ref.shape[0], -1, LANES)
        if dims:
            out_ref[:, channel_rows(dims, 3 * pair + t)] = block
        else:
            out_ref[:, 3 * pair + t, 0] = block


def tri_kernel(dims, col_ref, row_ref, acts_ref, out_ref):
    same = chain_mask(col_ref, row_ref)
    left_out, right_out = slot_operands(acts_ref, 0, dims)
    left_in, right_in = slot_operands(acts_ref, 1, dims)
    outgoing = jnp.where(same, mm(left_out, right_out, NT), 0.0)
    incoming = mm(raw_columns(left_in, same), right_in, TN)
    low = low_lanes((outgoing.shape[0], LANES))
    o_lo, o_hi = outgoing[:, :LANES], outgoing[:, LANES:]
    main_o = o_lo + jnp.where(low, turn(o_hi), 0.0)
    tail = jnp.where(low, o_hi, turn(incoming[:, LANES:]))
    store_tiles(out_ref, 0, dims, (main_o, incoming[:, :LANES], tail))


def tri_back_kernel(dims, col_ref, row_ref, acts_ref, grad_ref, out_ref):
    same = chain_mask(col_ref, row_ref)
    left_out, right_out = slot_operands(acts_ref, 0, dims)
    left_in, right_in = slot_operands(acts_ref, 1, dims)
    grad_out, grad_in = slot_operands(grad_ref, 0, dims)
    raw_out = raw_columns(grad_out, same)
    d_left = mm(raw_out, right_out)
    d_right = mm(raw_out, left_out, TN)
    low = low_lanes((d_left.shape[0], LANES))
    tail = jnp.where(low, d_left[:, LANES:], turn(d_right[:, LANES:]))
    store_tiles(out_ref, 0, dims, (d_left[:, :LANES], d_right[:, :LANES], tail))
    d_left = jnp.where(same, mm(right_in, grad_in, NT), 0.0)
    d_right = mm(raw_columns(left_in, same), grad_in)
    l_lo, l_hi = d_left[:, :LANES], d_left[:, LANES:]
    main_l = l_lo + jnp.where(low, turn(l_hi), 0.0)
    tail = jnp.where(low, l_hi, turn(d_right[:, LANES:]))
    store_tiles(out_ref, 1, dims, (main_l, d_right[:, :LANES], tail))


def second_kernel(
    share, rows, sum_ref, tri_ref, grad_ref, mask_ref, gx_ref, gt_ref, gh_ref,
    wgate_ref, wzt_ref, wz_ref, wut_ref, wu_ref, wdt_ref, wd_ref,
    out_ref, ds_ref, dlogit_ref, send_ref, gd_ref, gu_ref, gz_ref, gaint_ref, gainh_ref,
    *stage,
):
    @pl.when(pl.program_id(0) == 0)
    def _():
        for acc in (gd_ref, gu_ref, gz_ref, gaint_ref, gainh_ref):
            acc[...] = jnp.zeros_like(acc)
        if stage:
            unship(tri_ref, stage[0], 3, share, rows)

    for r in range(sum_ref.shape[0]):
        row = pl.program_id(0) * sum_ref.shape[0] + r
        total = sum_ref[r]
        mask = mask_ref[r]
        hat_x, _ = norm_rows(total)
        norm = (hat_x * gx_ref[...]).astype(BF)
        out_gate = jax.nn.sigmoid(mm(wgate_ref[...], norm))
        if stage:
            tiles = [get_tile(stage[0], t, row, rows, total.shape[0]) for t in range(3)]
        else:
            tiles = [tri_ref[r, t].astype(F32) for t in range(3)]
        tri_out, tri_in = unfold_pair(*tiles)
        hat_t, inv_t = norm_rows(jnp.concatenate([tri_out, tri_in], axis=0))
        tri_norm = (hat_t * gt_ref[...]).astype(BF)
        tri_proj = mm(wzt_ref[...], tri_norm)
        second = total + out_gate * tri_proj * mask
        hat_h, inv_h = norm_rows(second)
        trans_in = (hat_h * gh_ref[...]).astype(BF)
        up = mm(wut_ref[...], trans_in)
        square = up * up
        curve = jnp.tanh(0.7978845608 * up * (1.0 + 0.044715 * square))
        half = 0.5 * (1.0 + curve)
        act = (up * half).astype(BF)
        slope = half + up * (1.0 - curve * curve) * (0.3989422804 + 0.05351611220 * square)
        out_ref[r] = (second + mm(wdt_ref[...], act)).T.astype(BF)
        grad_low = grad_ref[r].astype(F32).T.astype(BF)
        gd_ref[...] += mm(act, grad_low, NT)
        d_up = (mm(wd_ref[...], grad_low) * slope).astype(BF)
        gu_ref[...] += mm(d_up, trans_in, NT)
        back = mm(wu_ref[...], d_up)
        gainh_ref[...] += back * hat_h
        d_second = grad_low.astype(F32) + norm_rows_back(back * gh_ref[...], hat_h, inv_h)
        ds_ref[r] = d_second
        gated = d_second * mask * out_gate
        d_tri = gated.astype(BF)
        dlogit_ref[r] = (gated * tri_proj * (1.0 - out_gate)).astype(BF)
        gz_ref[...] += mm(tri_norm, d_tri, NT)
        back = mm(wz_ref[...], d_tri)
        gaint_ref[...] += back * hat_t
        comb = norm_rows_back(back * gt_ref[...], hat_t, inv_t)
        hidden = comb.shape[0] // 2
        tiles = fold_pair(comb[:hidden], comb[hidden:])
        for t in range(3):
            if stage:
                put_tile(stage[1], t, row, rows, tiles[t])
            else:
                send_ref[r, t] = tiles[t].astype(BF)
    if stage:

        @pl.when(pl.program_id(0) == pl.num_programs(0) - 1)
        def _():
            ship(stage[1], send_ref, 3, share, rows)
            at = 3 * share * rows
            for acc in (gd_ref, gu_ref, gz_ref):
                part = acc.shape[0] // send_ref.shape[0]
                block = acc[...].reshape(send_ref.shape[0], part, LANES)
                send_ref[:, at : at + part] = block.astype(BF)
                at = at + part


def third_kernel(
    share, rows, sum_ref, acts_ref, ds_ref, dlogit_ref, mask_ref, mix_ref, right_ref, gx_ref, wt_ref, w_ref,
    fg_ref, dmix_ref, dright_ref, gin_ref, gainx_ref, dproj_ref, *stage,
):
    @pl.when(pl.program_id(0) == 0)
    def _():
        for acc in (dright_ref, gin_ref, gainx_ref):
            acc[...] = jnp.zeros_like(acc)
        if stage:
            unship(acts_ref, stage[0], 6, share, rows)

    hidden = wt_ref.shape[0] // 9
    for r in range(sum_ref.shape[0]):
        row = pl.program_id(0) * sum_ref.shape[0] + r
        hat, inv = norm_rows(sum_ref[r])
        norm = (hat * gx_ref[...]).astype(BF)
        mask = mask_ref[r]
        for pair in range(2):
            tiles = range(3 * pair, 3 * pair + 3)
            if stage:
                tiles = [get_tile(stage[0], t, row, rows, hidden) for t in tiles]
            else:
                tiles = [acts_ref[r, t].astype(F32) for t in tiles]
            both = unfold_pair(*tiles)
            for side in range(2):
                block = 2 * pair + side
                value = mm(wt_ref[block * hidden : (block + 1) * hidden], norm)
                gate = mm(wt_ref[(block + 4) * hidden : (block + 5) * hidden], norm)
                sig = jax.nn.sigmoid(gate)
                d_value = both[side] * mask * sig
                d_gate = d_value * value * (1.0 - sig)
                dproj_ref[block * hidden : (block + 1) * hidden] = d_value.astype(BF)
                dproj_ref[(block + 4) * hidden : (block + 5) * hidden] = d_gate.astype(BF)
        dproj_ref[8 * hidden :] = dlogit_ref[r]
        d_proj = dproj_ref[...]
        gin_ref[...] += mm(d_proj, norm, NT)
        back = mm(w_ref[...], d_proj)
        gainx_ref[...] += back * hat
        first = ds_ref[r] + norm_rows_back(back * gx_ref[...], hat, inv)
        fg_ref[r] = first
        low = first.astype(BF)
        dmix_ref[r] = mm(right_ref[...], low, NT).astype(BF)
        dright_ref[...] += mm(mix_ref[r], low)


def last_kernel(xt_ref, fg_ref, ds_ref, gain_ref, w_ref, out_ref, gw_ref, gainb_ref):
    @pl.when(pl.program_id(0) == 0)
    def _():
        for acc in (gw_ref, gainb_ref):
            acc[...] = jnp.zeros_like(acc)

    for r in range(xt_ref.shape[0]):
        hat, inv = norm_rows(xt_ref[r].astype(F32))
        norm = (hat * gain_ref[...]).astype(BF)
        d_bias = ds_ref[r]
        gw_ref[...] += mm(d_bias, norm, NT)
        back = mm(w_ref[...], d_bias)
        gainb_ref[...] += back * hat
        out_ref[r] = (fg_ref[r] + norm_rows_back(back * gain_ref[...], hat, inv)).T


def whole(shape):
    return pl.BlockSpec(shape, lambda i: (0,) * len(shape))


def by_row(step, shape):
    return pl.BlockSpec((step,) + shape, lambda i: (i,) + (0,) * len(shape))


def pair_call(kernel, steps, ins, outs, args, scratch=(), flops=0, moved=0):
    return pl.pallas_call(
        kernel,
        grid=(steps,),
        in_specs=ins,
        out_specs=[spec for spec, _ in outs],
        out_shape=[shape for _, shape in outs],
        scratch_shapes=list(scratch),
        compiler_params=pltpu.CompilerParams(vmem_limit_bytes=48 * 1024 * 1024),
        cost_estimate=pl.CostEstimate(flops=flops, bytes_accessed=moved, transcendentals=0),
    )(*args)


def shards(row_devices, *arrays):
    (pair_feats, node_feats, chain_ids, out_grad, node_out_grad) = arrays[:5]
    masters, firsts, seconds = arrays[5:17], arrays[17:29], arrays[29:41]
    w_attend, w_pairbias, w_attout, w_nodeup, w_nodedown = masters[:5]
    w_node, w_outer, w_in, w_z, w_up, w_down, ln_gains = masters[5:]
    count, _, residues, width_z = pair_feats.shape
    width_s = node_feats.shape[2]
    heads = w_pairbias.shape[1]
    depth = width_s // heads
    scale = 1.0 / depth**0.5
    outer_dim = w_node.shape[1] // 2
    hidden = (w_in.shape[1] - width_z) // 8
    expand = w_up.shape[1]
    every = 2 * row_devices
    shape_of = jax.ShapeDtypeStruct
    cuts = [width_s, width_z, width_s, width_s, width_z, 2 * hidden, width_z]
    gains, at = [], 0
    for cut in cuts:
        gains.append(ln_gains[at : at + cut])
        at = at + cut
    gain_a, gain_b, gain_n, gain_s, gain_x, gain_t, gain_h = gains
    column = lambda gain: gain.reshape(-1, 1)
    crop_index, row_index = lax.axis_index("crop"), lax.axis_index("row")
    first_row = row_index * count
    chains = chain_ids[0]
    own_chain = lax.dynamic_slice_in_dim(chains, first_row, count, 0)
    same_own = own_chain[:, None] == chains[None, :]
    mask = same_own.astype(F32)[:, None, :]
    chain_col, chain_row = chains.reshape(-1, 1), chains.reshape(1, -1)

    att_wb, attout_wb = w_attend.astype(BF), w_attout.astype(BF)
    nodeup_wb, nodedown_wb, node_wb = w_nodeup.astype(BF), w_nodedown.astype(BF), w_node.astype(BF)
    outer_wb = w_outer.astype(BF).reshape(outer_dim, outer_dim * width_z)
    bias_wb, in_wb, z_wb = w_pairbias.astype(BF), w_in.astype(BF), w_z.astype(BF)
    up_wb, down_wb = w_up.astype(BF), w_down.astype(BF)
    bias_wt, in_wt, z_wt, up_wt, down_wt = bias_wb.T, in_wb.T, z_wb.T, up_wb.T, down_wb.T

    step = 2 if count % 2 == 0 else 1
    steps = count // step
    pairs = count * residues

    node_both = jnp.concatenate([node_feats[:, 0], node_out_grad[:, 0]], axis=1)
    node_both = gather_all(node_both, row_devices).reshape(2 * residues, 2 * width_s)
    node_all, cot_all = node_both[:, :width_s], node_both[:, width_s:]
    node_f32 = node_all.astype(F32)

    pair_x = pair_feats[:, 0]
    xt, pair_bias = pair_call(
        bias_kernel, steps,
        [by_row(step, (residues, width_z)), whole((width_z, 1)), whole((heads, width_z))],
        [(by_row(step, (width_z, residues)), shape_of((count, width_z, residues), BF)),
         (by_row(step, (heads, residues)), shape_of((count, heads, residues), F32))],
        [pair_x, column(gain_b), bias_wt],
        flops=2 * pairs * width_z * heads, moved=4 * pairs * width_z,
    )

    def own_rows(values):
        return lax.dynamic_slice_in_dim(values, crop_index * residues + first_row, count, 0)

    def own_crop(values):
        return lax.dynamic_slice_in_dim(values, crop_index * residues, residues, 0)

    att_hat, att_back = jax.vjp(layer_norm, node_f32, gain_a)
    att_norm = att_hat.astype(BF)
    qkvg = mm(att_norm, att_wb)
    gate_all = jax.nn.sigmoid(qkvg[:, 3 * width_s :])
    qkv_crop = own_crop(qkvg[:, : 3 * width_s]).astype(BF)
    query_crop, keys, values = (
        qkv_crop[:, k * width_s : (k + 1) * width_s].reshape(residues, heads, depth)
        for k in range(3)
    )
    own_row_of = lambda v: lax.dynamic_slice_in_dim(v, first_row, count, 0)
    query = own_row_of(query_crop)
    raw_scores = jnp.einsum("ihd,jhd->ihj", query, keys, preferred_element_type=F32) * scale
    scores = jnp.where(same_own[:, None, :], raw_scores + pair_bias, -1000000000.0)
    att_weights = jax.nn.softmax(scores, axis=-1)
    weights_low = att_weights.astype(BF)
    attn = jnp.einsum("ihj,jhd->ihd", weights_low, values, preferred_element_type=F32)
    gated_own = (own_rows(gate_all) * attn.reshape(count, width_s)).astype(BF)
    gated = gather_all(gated_own, row_devices).reshape(2 * residues, width_s)

    node_mid = node_f32 + mm(gated, attout_wb)
    ntrans_hat, ntrans_back = jax.vjp(layer_norm, node_mid, gain_n)
    trans_node = ntrans_hat.astype(BF)
    node_upv = mm(trans_node, nodeup_wb)
    nact_val, nact_back = jax.vjp(gelu_tanh, node_upv)
    node_act = nact_val.astype(BF)
    node_next = node_mid + mm(node_act, nodedown_wb)
    node_out = own_rows(node_next).astype(BF)[:, None]
    node_hat, node_back = jax.vjp(layer_norm, node_next, gain_s)
    node_norm = node_hat.astype(BF)
    node_proj = mm(node_norm, node_wb).astype(BF)
    left_vec = own_rows(node_proj[:, :outer_dim])
    right_t = own_crop(node_proj[:, outer_dim:]).T
    outer_mix = mm(left_vec, outer_wb).astype(BF).reshape(count, outer_dim, width_z)

    share = hidden // row_devices
    direct = count % 16 == 0
    dims = (share, count) if direct else None
    weights_cut = weights_low.reshape(count, heads, row_devices, count).transpose(2, 0, 1, 3)

    def sent_block(tiles, extra=0):
        if direct:
            shape = (row_devices, tiles * share * count + extra, LANES)
            return whole(shape), shape_of(shape, BF)
        return by_row(step, (tiles, hidden, LANES)), shape_of((count, tiles, hidden, LANES), BF)

    def stage(tiles):
        return [pltpu.VMEM((tiles * hidden * count, LANES), F32)] if direct else []

    def swap(block):
        return lax.all_to_all(block, "row", split_axis=0, concat_axis=0, tiled=True)

    def to_channels(block):
        if direct:
            return swap(block)
        tiles = block.shape[1]
        cut = block.reshape(count, tiles, row_devices, share, LANES)
        sent = swap(cut.transpose(2, 1, 3, 0, 4))
        return sent.transpose(1, 2, 0, 3, 4).reshape(1, tiles, share, residues, LANES)

    def to_rows(block):
        if direct:
            return swap(block)
        tiles = block.shape[1]
        cut = block.reshape(tiles, share, row_devices, count, LANES)
        got = swap(cut.transpose(2, 0, 1, 3, 4))
        return got.transpose(3, 1, 0, 2, 4).reshape(count, tiles, hidden, LANES)

    def tri_block(tiles, extra=0):
        if direct:
            return sent_block(tiles, extra)
        shape = (1, tiles, share, residues, LANES)
        spec = pl.BlockSpec((1, tiles, 1, residues, LANES), lambda i: (0, 0, i, 0, 0))
        return spec, shape_of(shape, BF)

    ride = weights_cut.reshape(row_devices, -1, LANES) if direct else jnp.zeros((1, 1, LANES), BF)
    extra = ride.shape[1]
    first_sum, acts_own = pair_call(
        functools.partial(first_kernel, share, count), steps,
        [by_row(step, (width_z, residues)), by_row(step, (outer_dim, width_z)),
         whole((outer_dim, residues)), by_row(step, (1, residues)), whole((width_z, 1)),
         whole(in_wt.shape), whole(ride.shape)],
        [(by_row(step, (width_z, residues)), shape_of((count, width_z, residues), F32)),
         sent_block(6, extra)],
        [xt, outer_mix, right_t, mask, column(gain_x), in_wt, ride],
        scratch=stage(6),
        flops=16 * pairs * width_z * hidden, moved=12 * pairs * width_z,
    )

    chain_specs = [whole((residues, 1)), whole((1, residues))]
    product = 2 * share * residues**3
    acts = to_channels(acts_own)
    if direct:
        weights_col = acts[:, 6 * share * count :].reshape(residues, heads, count)
    else:
        weights_col = swap(weights_cut).reshape(residues, heads, count)
    (tri,) = pair_call(
        functools.partial(tri_kernel, dims), share, chain_specs + [tri_block(6, extra)[0]],
        [tri_block(3)], [chain_col, chain_row, acts],
        flops=2 * product, moved=share * residues * 9 * 256,
    )
    tri_rows = to_rows(tri)

    slab = by_row(step, (width_z, residues))
    second_args = [
        (by_row(step, (width_z, residues)), first_sum),
        (sent_block(3)[0], tri_rows),
        (by_row(step, (residues, width_z)), out_grad[:, 0]),
        (by_row(step, (1, residues)), mask),
    ]
    second_args += [
        (whole(v.shape), v)
        for v in (
            column(gain_x), column(gain_t), column(gain_h),
            in_wt[8 * hidden :], z_wt, z_wb, up_wt, up_wb, down_wt, down_wb,
        )
    ]
    grad_rows = 2 * expand + 2 * hidden
    carried = grad_rows // row_devices if direct else 0
    acc_shapes = [
        (expand, width_z), (expand, width_z), (2 * hidden, width_z),
        (2 * hidden, residues), (width_z, residues),
    ]
    pair_out, d_second, d_logit, dtri_own, g_down, g_up_t, g_z, gain_t_acc, gain_h_acc = pair_call(
        functools.partial(second_kernel, share, count), steps,
        [spec for spec, _ in second_args],
        [(by_row(step, (residues, width_z)), shape_of((count, residues, width_z), BF)),
         (slab, shape_of((count, width_z, residues), F32)),
         (slab, shape_of((count, width_z, residues), BF)),
         sent_block(3, carried)]
        + [(whole(s), shape_of(s, F32)) for s in acc_shapes],
        [arg for _, arg in second_args],
        scratch=stage(3) + stage(3),
        flops=12 * pairs * width_z * expand, moved=20 * pairs * width_z,
    )

    dtri = to_channels(dtri_own)
    if direct:
        grad_parts = dtri[:, 3 * share * count :]
    else:
        cut = lambda g: g.reshape(row_devices, -1, LANES)
        grad_parts = swap(jnp.concatenate([cut(g) for g in (g_down, g_up_t, g_z)], 1).astype(BF))
    row_sum = jnp.sum(grad_parts.astype(F32), axis=0)
    half_rows = row_sum.shape[0] // 2
    lower, upper = row_sum[:half_rows], row_sum[half_rows:]
    low_crop = crop_index == 0
    theirs = lax.ppermute(jnp.where(low_crop, upper, lower), "crop", [(0, 1), (1, 0)])
    pair_own = (jnp.where(low_crop, lower, upper) + theirs).astype(BF)
    (dacts,) = pair_call(
        functools.partial(tri_back_kernel, dims), share,
        chain_specs + [tri_block(6, extra)[0], tri_block(3, carried)[0]],
        [tri_block(6)], [chain_col, chain_row, acts, dtri],
        flops=4 * product, moved=share * residues * 15 * 256,
    )
    dacts_rows = to_rows(dacts)

    first_grad, d_mix, d_right, g_in_t, gain_x_acc = pair_call(
        functools.partial(third_kernel, share, count), steps,
        [slab, sent_block(6)[0], slab, slab, by_row(step, (1, residues)),
         by_row(step, (outer_dim, width_z)), whole((outer_dim, residues)), whole((width_z, 1)),
         whole(in_wt.shape), whole(in_wb.shape)],
        [(slab, shape_of((count, width_z, residues), F32)),
         (by_row(step, (outer_dim, width_z)), shape_of((count, outer_dim, width_z), BF)),
         (whole((outer_dim, residues)), shape_of((outer_dim, residues), F32)),
         (whole(in_wt.shape), shape_of(in_wt.shape, F32)),
         (whole((width_z, residues)), shape_of((width_z, residues), F32))],
        [first_sum, dacts_rows, d_second, d_logit, mask, outer_mix, right_t, column(gain_x),
         in_wt, in_wb],
        scratch=[pltpu.VMEM((9 * hidden, residues), BF)] + stage(6),
        flops=54 * pairs * width_z * hidden, moved=20 * pairs * width_z,
    )

    mix_flat = d_mix.reshape(count, outer_dim * width_z)
    d_left = back_dot(mix_flat, outer_wb)
    packed = jnp.concatenate([d_right.reshape(-1), d_left.reshape(-1)]).astype(BF)
    size = packed.shape[0]
    unit = 16 * LANES
    packed = jnp.pad(packed, (0, -size % unit)).reshape(-1, LANES)
    got = gather_all(packed, row_devices)
    g_outer = cross_sum(left_vec, mix_flat)
    gain_accs = [gain_x_acc, gain_t_acc, gain_h_acc]
    late_flat = join_flat([g_in_t, g_outer] + [lanes_sum(acc) for acc in gain_accs])
    late_own = scatter_sum(after(late_flat, got), row_devices)
    got = got.reshape(2, row_devices, -1)[:, :, :size].astype(F32)
    right_sum = jnp.sum(got[:, :, : outer_dim * residues], axis=1)
    right_sum = right_sum.reshape(2, outer_dim, residues).transpose(0, 2, 1)
    left_all = got[:, :, outer_dim * residues :].reshape(2, residues, outer_dim)
    proj_grad = jnp.concatenate([left_all, right_sum], axis=-1).astype(BF)
    proj_grad = proj_grad.reshape(2 * residues, 2 * outer_dim)

    g_node = cross_sum(node_norm, proj_grad)
    outer_node_grad, gain_s_grad = node_back(back_dot(proj_grad, node_wb))
    grad_next = cot_all.astype(F32) + outer_node_grad
    next_low = grad_next.astype(BF)
    g_nodedown = cross_sum(node_act, next_low)
    (nact_grad,) = nact_back(back_dot(next_low, nodedown_wb))
    nodeup_low = nact_grad.astype(BF)
    g_nodeup = cross_sum(trans_node, nodeup_low)
    ntrans_grad, gain_n_grad = ntrans_back(back_dot(nodeup_low, nodeup_wb))
    grad_mid = grad_next + ntrans_grad
    mid_low = grad_mid.astype(BF)
    g_attout = cross_sum(gated, mid_low)
    gated_grad = back_dot(mid_low, attout_wb)
    attn_grad = (gated_grad * gate_all).astype(BF)
    gate_grad = (gated_grad * gated.astype(F32) * (1.0 - gate_all)).astype(BF)

    attn_grad_crop = own_crop(attn_grad).reshape(residues, heads, depth)
    attn_grad_own = own_row_of(attn_grad_crop)
    weight_grad = jnp.einsum("ihd,jhd->ihj", attn_grad_own, values, preferred_element_type=F32)
    inner = jnp.sum(weight_grad * att_weights, axis=-1, keepdims=True)
    score_grad = (att_weights * (weight_grad - inner)).astype(BF)
    query_grad = jnp.einsum("ihj,jhd->ihd", score_grad, keys, preferred_element_type=F32) * scale

    values_own = own_row_of(values)
    inner_crop = jnp.sum(
        (own_crop(gated_grad) * own_crop(gated).astype(F32)).reshape(residues, heads, depth),
        axis=-1, keepdims=True,
    )
    weight_grad_col = jnp.einsum(
        "ihd,jhd->ihj", attn_grad_crop, values_own, preferred_element_type=F32
    )
    score_grad_col = (weights_col.astype(F32) * (weight_grad_col - inner_crop)).astype(BF)
    key_grad = (
        jnp.einsum("ihj,ihd->jhd", score_grad_col, query_crop, preferred_element_type=F32) * scale
    )
    value_grad = jnp.einsum("ihj,ihd->jhd", weights_col, attn_grad_crop, preferred_element_type=F32)
    qkv_grad = jnp.concatenate(
        [v.reshape(count, width_s) for v in (query_grad, key_grad, value_grad)], axis=-1
    ).astype(BF)

    pair_grad, g_bias_t, gain_b_acc = pair_call(
        last_kernel, steps,
        [slab, slab, by_row(step, (heads, residues)), whole((width_z, 1)), whole((width_z, heads))],
        [(by_row(step, (residues, width_z)), shape_of((count, residues, width_z), F32)),
         (whole((heads, width_z)), shape_of((heads, width_z), F32)),
         (whole((width_z, residues)), shape_of((width_z, residues), F32))],
        [xt, first_grad, score_grad, column(gain_b), bias_wb],
        flops=4 * pairs * width_z * heads, moved=10 * pairs * width_z,
    )

    bias_flat = join_flat([g_bias_t, lanes_sum(gain_b_acc)]).astype(BF)
    pieces = [qkv_grad.reshape(-1, LANES), late_own, pair_own, bias_flat.reshape(-1, LANES)]
    highs = [piece.shape[0] for piece in pieces]
    tail = jnp.zeros((-sum(highs) % 16, LANES), BF)
    last = gather_all(jnp.concatenate(pieces + [tail]), row_devices)
    ends = [sum(highs[: k + 1]) for k in range(len(highs))]
    qkv_grad_all = last[:, : ends[0]].reshape(2 * residues, 3 * width_s)
    late_sums = last[:, ends[0] : ends[1]].reshape(-1).astype(F32)
    pair_sums = last[:, ends[1] : ends[2]].astype(F32).reshape(2, row_devices, -1, LANES)
    bias_parts = last[:, ends[2] : ends[3]].astype(F32)
    qkvg_grad = jnp.concatenate([qkv_grad_all, gate_grad], axis=-1)
    g_attend = cross_sum(att_norm, qkvg_grad)
    att_in_grad, gain_a_grad = att_back(back_dot(qkvg_grad, att_wb))
    node_grad = own_rows(grad_mid + att_in_grad)[:, None]

    g_in_t, g_outer, gain_x_grad, gain_t_grad, gain_h_grad = split_flat(
        late_sums, [g_in_t, w_outer, gain_x, gain_t, gain_h]
    )
    g_bias_t, gain_b_grad = split_flat(jnp.sum(bias_parts, axis=0).reshape(-1), [g_bias_t, gain_b])
    pair_sums = pair_sums.transpose(1, 0, 2, 3).reshape(row_devices, 2 * half_rows, LANES)
    found, start = [], 0
    for total in (g_down, g_up_t, g_z):
        part = total.shape[0] // row_devices
        found.append(pair_sums[:, start : start + part].reshape(total.shape))
        start = start + part
    g_down, g_up_t, g_z = found
    gain_grad = jnp.concatenate(
        [gain_a_grad, gain_b_grad, gain_n_grad, gain_s_grad, gain_x_grad, gain_t_grad, gain_h_grad]
    )
    grads = [
        g_attend, g_bias_t.T, g_attout, g_nodeup, g_nodedown, g_node, g_outer, g_in_t.T, g_z,
        g_up_t.T, g_down, gain_grad,
    ]
    results = [pair_out[:, None], node_out, pair_grad[:, None], node_grad]
    rates = [0.1] * 11 + [1.0]
    decays = [0.1] * 11 + [0.0]
    for master, first_old, second_old, grad, rate, decay in zip(
        masters, firsts, seconds, grads, rates, decays
    ):
        results.extend(adam_step(master, first_old, second_old, grad, rate, decay))
    return tuple(results)


def solution(mesh):
    rows4, rows3 = P("row", "crop", None, None), P("row", "crop", None)
    return jax.shard_map(
        functools.partial(shards, mesh.shape["row"]),
        mesh=mesh,
        in_specs=(rows4, rows3, P("crop", None), rows4, rows3) + (P(),) * 36,
        out_specs=(rows4, rows3, rows4, rows3) + (P(),) * 36,
        check_vma=False,
    )
```

time: 1120 us -> 510 us (0.46); the launches traced: 1100 us -> 508 us
  waiting for transfers between devices: 626 us -> 177 us
  local copies, waits for them, and re-layouts: 175 us -> 62 us
  matrix products: 128 us -> 38.6 us
  Pallas kernels: 0 us -> 73.3 us
  starting transfers between devices: 16.9 us -> 63.2 us
  other arithmetic: 81.2 us -> 38 us
  between operations: 17 us -> 2.58 us
    all_gather x4 -> x0, waiting for transfers between devices: 295 us -> none  [the longest x1 104 us: shards(): piece_in = lax.all_gather(right_in, 'row', axis=0, tiled=True)]
    reduce_scatter x3 -> x0, waiting for transfers between devices: 147 us -> none  [the longest x1 57.8 us: shards(): lax.psum_scatter(value_term.reshape(residues, crop_count, width_s), 'row'...]
    psum x1 -> x0, waiting for transfers between devices: 131 us -> none  [shards(): summed_grads = lax.psum(flat_grads, ('crop', 'row'))]
    all_to_all x3 -> x8, waiting for transfers between devices: 53.2 us -> 177 us  [the longest x3 140 us: swap(): return lax.all_to_all(block, 'row', split_axis=0, concat_axis=0, tiled=True)]
    dot_general x48 -> x24, matrix products: 128 us -> 38.6 us  [the longest x18 33.6 us: mm(): return lax.dot_general(left, right, dims, preferred_element_type=F32)]
    pallas_call x0 -> x7, Pallas kernels: none -> 73.3 us  [pair_call(): pl.pallas_call(kernel, grid=(steps,), in_specs=ins, out_specs=[spec for s...]
    all_gather x5 -> x0, local copies, waits for them, and re-layouts: 68.3 us -> none  [the longest x1 23.6 us: shards(): piece_out = lax.all_gather(right_out, 'row', axis=0, tiled=True)]
    all_gather x3 -> x0, blocking collectives: 60.2 us -> none  [the longest x1 23.4 us: shards(): lax.all_gather(key_own, 'row', axis=0, tiled=True)]
  transfers between devices with their start and end apart: 11 -> 13, of which waited for: 9 -> 8; matrix products, arithmetic and copies ran while one was open for 21% -> 15% of each run, Pallas kernels for 0% -> 1%
where the time goes in v1:
time: 510 us; the launch traced here: 508 us
  waiting for transfers between devices  177 us (35%)
  Pallas kernels  73.3 us (14%)
  starting transfers between devices  63.2 us (12%)
  local copies, waits for them, and re-layouts  62 us (12%)
  blocking collectives  53 us (10%)
  matrix products  38.6 us (8%)
  other arithmetic  38 us (7%)
    all_to_all x3, waiting for transfers between devices, swap(): return lax.all_to_all(block, 'row', split_axis=0, concat_axis=0, tiled=True)  140 us
    pallas_call x7, Pallas kernels, pair_call(): pl.pallas_call(kernel, grid=(steps,), in_specs=ins, out_specs=[spec for s...  73.3 us
    all_to_all x1, blocking collectives, swap(): return lax.all_to_all(block, 'row', split_axis=0, concat_axis=0, tiled=True)  53 us
    all_to_all x4, waiting for transfers between devices, gather_all(): lax.all_to_all(spread, BOTH, split_axis=0, concat_axis=0, tiled=True, axi...  36.8 us
    all_to_all x4, starting transfers between devices, gather_all(): lax.all_to_all(spread, BOTH, split_axis=0, concat_axis=0, tiled=True, axi...  34.7 us
    unnamed x271, local copies, waits for them, and re-layouts  34.3 us
    dot_general x18, matrix products, mm(): return lax.dot_general(left, right, dims, preferred_element_type=F32)  33.6 us
    all_to_all x3, starting transfers between devices, swap(): return lax.all_to_all(block, 'row', split_axis=0, concat_axis=0, tiled=True)  24 us
  transfers between devices with their start and end apart: 13, of which 8 were waited for; matrix products, arithmetic and copies ran while one was open for 15% of the time, Pallas kernels for 1%

profile of v1, /device:TPU:0, one launch (start us, length us, event | category | flops | bytes accessed | tf_op | source)
XLA Modules:
  0.0 507.7 jit_solution(7857376964981414414)
XLA Ops:
  2.2 8.3 %all-to-all-start = ((bf16[16,16,512]{2,1,0:T(8,128)(2,1)}), bf16[16,16,512]{2,1,0:T(8,128)(2,1)S(1)}, u32[]{:S(2)}, u32[]{:S(2)}) async-start(bf16[16,16,512]{2,1,0:T(8,128)(2,1)} %broadcast_in_dim.44), calls=%async_computation | async-start | bytes 524288 | tf_op jit(solution)/shard_map/all_to_all | solution.py:56
  12.6 7.9 %all-to-all-done = bf16[16,16,512]{2,1,0:T(8,128)(2,1)S(1)} async-done(((bf16[16,16,512]{2,1,0:T(8,128)(2,1)}), bf16[16,16,512]{2,1,0:T(8,128)(2,1)S(1)}, u32[]{:S(2)}, u32[]{:S(2)}) %all-to-all-start) | async-done | bytes 262176 | tf_op jit(solution)/shard_map/all_to_all | solution.py:56
  37.7 3.5 all-to-all-start.1
  41.6 7.9 %all-to-all-done.1 = bf16[16,16,256]{2,1,0:T(8,128)(2,1)S(1)} async-done(((bf16[16,16,256]{2,1,0:T(8,128)(2,1)}), bf16[16,16,256]{2,1,0:T(8,128)(2,1)S(1)}, u32[]{:S(2)}, u32[]{:S(2)}) %all-to-all-start.1) | async-done | bytes 131104 | tf_op jit(solution)/shard_map/all_to_all | solution.py:56
  57.1 11.6 %shard_map.697 = (f32[16,128,256]{2,1,0:T(8,128)S(1)}, bf16[16,784,128]{2,1,0:T(8,128)(2,1)}) custom-call(bf16[16,128,256]{2,1,0:T(8,128)(2,1)S(1)} %get-tuple-element.58.xt_ref, bf16[16,32,128]{2,1,0:T(8,128)(2,1)S(1)} %bitcast.214, bf16[32,256]{1,0:T(8,128)(2,1)S(1)} %dynamic-slice_bitcast_fusion.right_ref, ...), custom_call_target="tpu_custom_call" | custom-call | flops 1073741824 | bytes 6291456 | tf_op jit(solution)/shard_map/pallas_call | solution.py:413
  70.1 3.7 all-to-all-start.2
  74.0 60.3 %all-to-all-done.2.acts_ref = bf16[16,784,128]{2,1,0:T(8,128)(2,1)S(1)} async-done(((bf16[16,784,128]{2,1,0:T(8,128)(2,1)}), bf16[16,784,128]{2,1,0:T(8,128)(2,1)S(1)}, u32[]{:S(2)}, u32[]{:S(2)}) %all-to-all-start.2) | async-done | bytes 3211296 | tf_op jit(solution)/shard_map/all_to_all | solution.py:536
  134.3 3.5 shard_map.698
  139.0 15.7 %all-to-all-start.3 = ((bf16[16,384,128]{2,1,0:T(8,128)(2,1)}), bf16[16,384,128]{2,1,0:T(8,128)(2,1)S(1)}, u32[]{:S(2)}, u32[]{:S(2)}) async-start(bf16[16,384,128]{2,1,0:T(8,128)(2,1)} %copy-done.1), calls=%async_computation.3 | async-start | bytes 3145728 | tf_op jit(solution)/shard_map/all_to_all | solution.py:536
  161.6 25.1 %all-to-all-done.3.tri_ref = bf16[16,384,128]{2,1,0:T(8,128)(2,1)S(1)} async-done(((bf16[16,384,128]{2,1,0:T(8,128)(2,1)}), bf16[16,384,128]{2,1,0:T(8,128)(2,1)S(1)}, u32[]{:S(2)}, u32[]{:S(2)}) %all-to-all-start.3) | async-done | bytes 1572896 | tf_op jit(solution)/shard_map/all_to_all | solution.py:536
  187.9 25.6 %shard_map.699 = (bf16[16,256,128]{2,1,0:T(8,128)(2,1)}, f32[16,128,256]{2,1,0:T(8,128)}, bf16[16,128,256]{2,1,0:T(8,128)(2,1)S(1)}, bf16[16,464,128]{2,1,0:T(8,...) custom-call(f32[16,128,256]{2,1,0:T(8,128)} %copy-done.13, ...), custom_call_target="tpu_custom_call" | custom-call | flops 3221225472 | bytes 10485760 | tf_op jit(solution)/shard_map/pallas_call | solution.py:413
  214.5 53.0 %all_to_all.45.grad_ref = bf16[16,464,128]{2,1,0:T(8,128)(2,1)S(1)} all-to-all(bf16[16,464,128]{2,1,0:T(8,128)(2,1)} %get-tuple-element.63), channel_id=1, replica_groups=mesh['crop'=2,'row'=16] {'row'}, dimensions={0} | all-to-all | bytes 3801088 | tf_op jit(solution)/shard_map/all_to_all | solution.py:536
  267.5 8.2 %shard_map.700 = bf16[16,768,128]{2,1,0:T(8,128)(2,1)} custom-call(s32[256,1]{1,0:T(8,128)S(1)} %copy.263.col_ref, s32[1,256]{1,0:T(1,128)S(1)} %copy-done.11, bf16[16,784,128]{2,1,0:T(8,128)(2,1)} %copy-done, bf16[16,464,128]{2,1,0:T(8,128)(2,1)S(1)} %all_to_all.45.grad_ref), custom_call_target="tpu_custom_call" | custom-call | flops 1073741824 | bytes 7864320 | tf_op jit(solution)/shard_map/pallas_call | solution.py:413
  275.7 4.6 all-to-all-start.5
  285.2 54.4 %all-to-all-done.5.acts_ref = bf16[16,768,128]{2,1,0:T(8,128)(2,1)} async-done(((bf16[16,768,128]{2,1,0:T(8,128)(2,1)}), bf16[16,768,128]{2,1,0:T(8,128)(2,1)}, u32[]{:S(2)}, u32[]{:S(2)}) %all-to-all-start.5) | async-done | bytes 3145760 | tf_op jit(solution)/shard_map/all_to_all | solution.py:536
  341.8 17.2 %shard_map.701 = (f32[16,128,256]{2,1,0:T(8,128)S(1)}, bf16[16,32,128]{2,1,0:T(8,128)(2,1)S(1)}, f32[32,256]{1,0:T(8,128)S(1)}, f32[1152,128]{1,0:T(8,128)S(1)}, f32[128,256]{1,0:T(8,128)S(1)}) custom-call(f32[16,128,256]{2,1,0:T(8,128)} %copy-done.13, bf16[16,768,128]{2,1,0:T(8,128)(2,1)} %all-to-all-done.5.acts_ref, ...), custom_call_target="tpu_custom_call" | custom-call | flops 3623878656 | bytes 10485760 | tf_op jit(solution)/shard_map/pallas_call | solution.py:413
  362.6 16.0 %all-to-all-start.6 = ((bf16[16,80,128]{2,1,0:T(8,128)(2,1)}), bf16[16,80,128]{2,1,0:T(8,128)(2,1)}, u32[]{:S(2)}, u32[]{:S(2)}) async-start(bf16[16,80,128]{2,1,0:T(8,128)(2,1)} %broadcast_in_dim.93), calls=%async_computation.6 | async-start | bytes 655360 | tf_op jit(solution)/shard_map/all_to_all | solution.py:56
  381.5 8.9 %all-to-all-done.6 = bf16[16,80,128]{2,1,0:T(8,128)(2,1)} async-done(((bf16[16,80,128]{2,1,0:T(8,128)(2,1)}), bf16[16,80,128]{2,1,0:T(8,128)(2,1)}, u32[]{:S(2)}, u32[]{:S(2)}) %all-to-all-start.6) | async-done | bytes 327712 | tf_op jit(solution)/shard_map/all_to_all | solution.py:56
  396.5 3.3 all-to-all-start.7
  428.2 4.6 shard_map.702
  435.5 6.9 %all-to-all-start.8 = ((bf16[16,240,128]{2,1,0:T(8,128)(2,1)}), bf16[16,240,128]{2,1,0:T(8,128)(2,1)S(1)}, u32[]{:S(2)}, u32[]{:S(2)}) async-start(bf16[16,240,128]{2,1,0:T(8,128)(2,1)} %broadcast_in_dim.100), calls=%async_computation.8 | async-start | bytes 1966080 | tf_op jit(solution)/shard_map/all_to_all | solution.py:56
  455.2 12.1 %all-to-all-done.8 = bf16[16,240,128]{2,1,0:T(8,128)(2,1)S(1)} async-done(((bf16[16,240,128]{2,1,0:T(8,128)(2,1)}), bf16[16,240,128]{2,1,0:T(8,128)(2,1)S(1)}, u32[]{:S(2)}, u32[]{:S(2)}) %all-to-all-start.8) | async-done | bytes 983072 | tf_op jit(solution)/shard_map/all_to_all | solution.py:56
  467.4 5.0 multiply_subtract_fusion.1
  500.9 4.3 multiply_subtract_fusion.2
  (449 shorter events, 133.3 us)
Async XLA Ops:
  0.7 25.9 %copy-start.89 = (f32[1408]{0:T(1024)S(1)}, f32[1408]{0:T(1024)}, u32[]{:S(2)}) copy-start(f32[1408]{0:T(1024)} %param.57) | copy-start | bytes 16900
  0.7 23.5 %copy-start.4 = (bf16[16,1,256,128]{3,2,1,0:T(8,128)(2,1)S(1)}, bf16[16,1,256,128]{3,2,1,0:T(8,128)(2,1)}, u32[]{:S(2)}) copy-start(bf16[16,1,256,128]{3,2,1,0:T(8,128)(2,1)} %param.41) | copy-start | bytes 3145732
  2.2 18.2 %all-to-all-start = ((bf16[16,16,512]{2,1,0:T(8,128)(2,1)}), bf16[16,16,512]{2,1,0:T(8,128)(2,1)S(1)}, u32[]{:S(2)}, u32[]{:S(2)}) async-start(bf16[16,16,512]{2,1,0:T(8,128)(2,1)} %broadcast_in_dim.44), calls=%async_computation | async-start | bytes 524288 | tf_op jit(solution)/shard_map/all_to_all | solution.py:56
  20.4 6.8 %collective-permute-start = (bf16[16,16,512]{2,1,0:T(8,128)(2,1)S(1)}, bf16[16,16,512]{2,1,0:T(8,128)(2,1)}, u32[]{:S(2)}, u32[]{:S(2)}) collective-permute-start(bf16[16,16,512]{2,1,0:T(8,128)(2,1)S(1)} %all-to-all-done), channel_id=1, source_target_pairs={{0,1},{1,0},{2,3},{3,2},{4,5},{5,4},{6,7},{7,6},{8,9},{9,8},{10,11... | collective-permute-start | bytes 786440 | tf_op jit(solution)/shard_map/ppermute | solution.py:59
  26.6 30.5 %copy-start.2 = (bf16[16,128,256]{2,1,0:T(8,128)(2,1)}, bf16[16,128,256]{2,1,0:T(8,128)(2,1)S(1)}, u32[]{:S(2)}) copy-start(bf16[16,128,256]{2,1,0:T(8,128)(2,1)S(1)} %get-tuple-element.58.xt_ref) | copy-start | bytes 3145732
  27.2 25.4 %copy-start.100 = (f32[256]{0:T(256)}, f32[256]{0:T(256)S(1)}, u32[]{:S(2)}) copy-start(f32[256]{0:T(256)S(1)} %get-tuple-element.306) | copy-start | bytes 3076
  27.2 29.0 %copy-start.102 = (f32[256]{0:T(256)}, f32[256]{0:T(256)S(1)}, u32[]{:S(2)}) copy-start(f32[256]{0:T(256)S(1)} %get-tuple-element.305) | copy-start | bytes 3076
  28.3 22.6 %copy-start.19 = (bf16[16,2,16,512]{3,2,1,0:T(8,128)(2,1)}, bf16[16,2,16,512]{3,2,1,0:T(8,128)(2,1)S(1)}, u32[]{:S(2)}) copy-start(bf16[16,2,16,512]{3,2,1,0:T(8,128)(2,1)S(1)} %pad_maximum_fusion.5) | copy-start | bytes 1572868
  37.7 11.7 %all-to-all-start.1 = ((bf16[16,16,256]{2,1,0:T(8,128)(2,1)}), bf16[16,16,256]{2,1,0:T(8,128)(2,1)S(1)}, u32[]{:S(2)}, u32[]{:S(2)}) async-start(bf16[16,16,256]{2,1,0:T(8,128)(2,1)} %broadcast_in_dim.47), calls=%async_computation.1 | async-start | bytes 262144 | tf_op jit(solution)/shard_map/all_to_all | solution.py:56
  49.5 1.3 collective-permute-start.1
  70.1 64.2 %all-to-all-start.2 = ((bf16[16,784,128]{2,1,0:T(8,128)(2,1)}), bf16[16,784,128]{2,1,0:T(8,128)(2,1)S(1)}, u32[]{:S(2)}, u32[]{:S(2)}) async-start(bf16[16,784,128]{2,1,0:T(8,128)(2,1)} %get-tuple-element.61), calls=%async_computation.2 | async-start | bytes 6422528 | tf_op jit(solution)/shard_map/all_to_all | solution.py:536
  139.0 47.7 %all-to-all-start.3 = ((bf16[16,384,128]{2,1,0:T(8,128)(2,1)}), bf16[16,384,128]{2,1,0:T(8,128)(2,1)S(1)}, u32[]{:S(2)}, u32[]{:S(2)}) async-start(bf16[16,384,128]{2,1,0:T(8,128)(2,1)} %copy-done.1), calls=%async_computation.3 | async-start | bytes 3145728 | tf_op jit(solution)/shard_map/all_to_all | solution.py:536
  275.7 64.0 %all-to-all-start.5 = ((bf16[16,768,128]{2,1,0:T(8,128)(2,1)}), bf16[16,768,128]{2,1,0:T(8,128)(2,1)}, u32[]{:S(2)}, u32[]{:S(2)}) async-start(bf16[16,768,128]{2,1,0:T(8,128)(2,1)} %shard_map.700), calls=%async_computation.5 | async-start | bytes 6291456 | tf_op jit(solution)/shard_map/all_to_all | solution.py:536
  280.3 59.3 %copy-start.6 = (bf16[1152,128]{1,0:T(8,128)(2,1)S(1)}, bf16[1152,128]{1,0:T(8,128)(2,1)}, u32[]{:S(2)}) copy-start(bf16[1152,128]{1,0:T(8,128)(2,1)} %copy-done.5) | copy-start | bytes 884740
  280.4 4.2 collective-permute-start.3
  361.8 19.6 %copy-start.10 = (f32[128,256]{1,0:T(8,128)S(1)}, f32[128,256]{1,0:T(8,128)}, u32[]{:S(2)}) copy-start(f32[128,256]{1,0:T(8,128)} %copy-done.9) | copy-start | bytes 393220
  362.6 30.4 %copy-start.115 = (f32[128]{0:T(128)S(1)}, f32[128]{0:T(128)}, u32[]{:S(2)}) copy-start(f32[128]{0:T(128)} %reduce_sum.289) | copy-start | bytes 1540
  362.6 27.8 %all-to-all-start.6 = ((bf16[16,80,128]{2,1,0:T(8,128)(2,1)}), bf16[16,80,128]{2,1,0:T(8,128)(2,1)}, u32[]{:S(2)}, u32[]{:S(2)}) async-start(bf16[16,80,128]{2,1,0:T(8,128)(2,1)} %broadcast_in_dim.93), calls=%async_computation.6 | async-start | bytes 655360 | tf_op jit(solution)/shard_map/all_to_all | solution.py:56
  390.4 9.4 %collective-permute-start.2 = (bf16[16,80,128]{2,1,0:T(8,128)(2,1)}, bf16[16,80,128]{2,1,0:T(8,128)(2,1)S(1)}, u32[]{:S(2)}, u32[]{:S(2)}) collective-permute-start(bf16[16,80,128]{2,1,0:T(8,128)(2,1)} %all-to-all-done.6), channel_id=1, source_target_pairs={{0,1},{1,0},{2,3},{3,2},{4,5},{5,4},{6,7},{7,6},{8,9},{9,8},{10,11... | collective-permute-start | bytes 983048 | tf_op jit(solution)/shard_map/ppermute | solution.py:59
  396.5 36.5 %all-to-all-start.7 = ((bf16[32,80,128]{2,1,0:T(8,128)(2,1)}), bf16[32,80,128]{2,1,0:T(8,128)(2,1)}, u32[]{:S(2)}, u32[]{:S(2)}) async-start(bf16[32,80,128]{2,1,0:T(8,128)(2,1)} %bitcast.50), calls=%async_computation.7 | async-start | bytes 1310720 | tf_op jit(solution)/shard_map/all_to_all | solution.py:69
  435.5 31.8 %all-to-all-start.8 = ((bf16[16,240,128]{2,1,0:T(8,128)(2,1)}), bf16[16,240,128]{2,1,0:T(8,128)(2,1)S(1)}, u32[]{:S(2)}, u32[]{:S(2)}) async-start(bf16[16,240,128]{2,1,0:T(8,128)(2,1)} %broadcast_in_dim.100), calls=%async_computation.8 | async-start | bytes 1966080 | tf_op jit(solution)/shard_map/all_to_all | solution.py:56
  448.1 19.3 %copy-start.18 = (f32[512,256]{1,0:T(8,128)S(1)}, f32[512,256]{1,0:T(8,128)}, u32[]{:S(2)}) copy-start(f32[512,256]{1,0:T(8,128)} %copy-done.16) | copy-start | bytes 1572868
  448.1 19.3 %copy-start.28 = (f32[256,1024]{1,0:T(8,128)S(1)}, f32[256,1024]{1,0:T(8,128)}, u32[]{:S(2)}) copy-start(f32[256,1024]{1,0:T(8,128)} %param.49) | copy-start | bytes 3145732
  467.3 8.2 %collective-permute-start.4 = (bf16[16,240,128]{2,1,0:T(8,128)(2,1)S(1)}, bf16[16,240,128]{2,1,0:T(8,128)(2,1)S(1)}, u32[]{:S(2)}, u32[]{:S(2)}) collective-permute-start(bf16[16,240,128]{2,1,0:T(8,128)(2,1)S(1)} %all-to-all-done.8), channel_id=1, source_target_pairs={{0,1},{1,0},{2,3},{3,2},{4,5},{5,4},{6,7},{7,6},{8,9},{9,8},{10,11... | collective-permute-start | bytes 2949128 | tf_op jit(solution)/shard_map/ppermute | solution.py:59
  (114 other events, 601.4 us)

commit v2 on v1

--- a/solution.py
+++ b/solution.py
@@ -22,24 +22,6 @@
     return lax.dot_general(left, right, dims, preferred_element_type=F32)
 
 
-def layer_norm(values, gain_vec):
-    centred = values - jnp.mean(values, axis=-1, keepdims=True)
-    spread = jnp.mean(centred * centred, axis=-1, keepdims=True)
-    return centred * lax.rsqrt(spread + EPS) * gain_vec
-
-
-def gelu_tanh(values):
-    return jax.nn.gelu(values, approximate=True)
-
-
-def back_dot(left, weight):
-    return mm(left, weight, NT)
-
-
-def cross_sum(left, right):
-    return mm(left, right, TN)
-
-
 def adam_step(master, first_old, second_old, grad_total, rate, decay):
     first_new = 0.9 * first_old + 0.1 * grad_total
     second_new = 0.999 * second_old + 0.001 * grad_total * grad_total
@@ -49,45 +31,27 @@
     return (first_new, second_new, master_new)
 
 
-def gather_all(part, row_devices):
+def after(value, event):
+    return lax.optimization_barrier((value, event))[0]
+
+
+def gather_all(part, row_devices, during=()):
     every = 2 * row_devices
     groups = [[d for d in range(every) if d % 2 == k] for k in range(2)]
     spread = jnp.broadcast_to(part[None], (every // 2,) + part.shape)
     got = lax.all_to_all(
         spread, BOTH, split_axis=0, concat_axis=0, tiled=True, axis_index_groups=groups
     )
+    got = after(got, during)
     other = lax.ppermute(got, "row", [(d, d ^ 1) for d in range(row_devices)])
     odd = lax.axis_index("row") % 2 == 1
     pair = [jnp.where(odd, other, got), jnp.where(odd, got, other)]
     return jnp.stack(pair, axis=1).reshape((every,) + part.shape)
 
 
-def scatter_sum(flat, row_devices):
-    every = 2 * row_devices
-    unit = every * 16 * LANES
-    sent = jnp.pad(flat, (0, -flat.shape[0] % unit)).astype(BF).reshape(every, -1, LANES)
+def scatter_sum(sent):
     parts = lax.all_to_all(sent, BOTH, split_axis=0, concat_axis=0, tiled=True)
     return jnp.sum(parts.astype(F32), axis=0).astype(BF)
-
-
-def after(value, event):
-    return lax.optimization_barrier((value, event))[0]
-
-
-def join_flat(parts):
-    return jnp.concatenate([part.reshape(-1) for part in parts])
-
-
-def split_flat(flat, parts):
-    found, start = [], 0
-    for part in parts:
-        found.append(flat[start : start + part.size].reshape(part.shape))
-        start = start + part.size
-    return found
-
-
-def lanes_sum(acc):
-    return jnp.sum(acc, axis=1)
 
 
 def norm_rows(values):
@@ -154,12 +118,25 @@
         stage_ref[t * devices * span : (t + 1) * devices * span] = block.reshape(-1, LANES)
 
 
-def bias_kernel(x_ref, gain_ref, weight_ref, xt_ref, bias_ref):
+def lane_sums(ref):
+    count = ref.shape[0] // LANES
+    cut = [ref[k * LANES : (k + 1) * LANES].T for k in range(count)]
+    return jnp.concatenate([jnp.sum(part, axis=0, keepdims=True) for part in cut], axis=0)
+
+
+def turn_blocks(ref):
+    count = ref.shape[0] // LANES
+    return jnp.concatenate([ref[k * LANES : (k + 1) * LANES].T for k in range(count)], axis=0)
+
+
+def bias_kernel(x_ref, gain_ref, weight_ref, xt_ref, norm_ref, bias_ref):
     for r in range(x_ref.shape[0]):
         xt = x_ref[r].astype(F32).T
         xt_ref[r] = xt.astype(BF)
         hat, _ = norm_rows(xt)
-        bias_ref[r] = mm(weight_ref[...], (hat * gain_ref[...]).astype(BF))
+        norm = (hat * gain_ref[...]).astype(BF)
+        norm_ref[r] = norm
+        bias_ref[r] = mm(weight_ref[...], norm)
 
 
 def first_kernel(
@@ -270,7 +247,7 @@
 def second_kernel(
     share, rows, sum_ref, tri_ref, grad_ref, mask_ref, gx_ref, gt_ref, gh_ref,
     wgate_ref, wzt_ref, wz_ref, wut_ref, wu_ref, wdt_ref, wd_ref,
-    out_ref, ds_ref, dlogit_ref, send_ref, gd_ref, gu_ref, gz_ref, gaint_ref, gainh_ref,
+    out_ref, ds_ref, dlogit_ref, send_ref, gd_ref, gu_ref, gz_ref, gains_ref, gaint_ref, gainh_ref,
     *stage,
 ):
     @pl.when(pl.program_id(0) == 0)
@@ -298,12 +275,8 @@
         second = total + out_gate * tri_proj * mask
         hat_h, inv_h = norm_rows(second)
         trans_in = (hat_h * gh_ref[...]).astype(BF)
-        up = mm(wut_ref[...], trans_in)
-        square = up * up
-        curve = jnp.tanh(0.7978845608 * up * (1.0 + 0.044715 * square))
-        half = 0.5 * (1.0 + curve)
-        act = (up * half).astype(BF)
-        slope = half + up * (1.0 - curve * curve) * (0.3989422804 + 0.05351611220 * square)
+        act, slope = gelu_parts(mm(wut_ref[...], trans_in))
+        act = act.astype(BF)
         out_ref[r] = (second + mm(wdt_ref[...], act)).T.astype(BF)
         grad_low = grad_ref[r].astype(F32).T.astype(BF)
         gd_ref[...] += mm(act, grad_low, NT)
@@ -327,26 +300,30 @@
                 put_tile(stage[1], t, row, rows, tiles[t])
             else:
                 send_ref[r, t] = tiles[t].astype(BF)
-    if stage:
-
-        @pl.when(pl.program_id(0) == pl.num_programs(0) - 1)
-        def _():
+
+    @pl.when(pl.program_id(0) == pl.num_programs(0) - 1)
+    def _():
+        gains_ref[...] = jnp.concatenate([lane_sums(gaint_ref), lane_sums(gainh_ref)], axis=0)
+        if stage:
             ship(stage[1], send_ref, 3, share, rows)
+            devices = send_ref.shape[0]
             at = 3 * share * rows
-            for acc in (gd_ref, gu_ref, gz_ref):
-                part = acc.shape[0] // send_ref.shape[0]
-                block = acc[...].reshape(send_ref.shape[0], part, LANES)
-                send_ref[:, at : at + part] = block.astype(BF)
+            for acc, turned in ((gd_ref, False), (gu_ref, True), (gz_ref, False)):
+                part = acc.shape[0] // devices
+                block = turn_blocks(acc) if turned else acc[...]
+                send_ref[:, at : at + part] = block.reshape(devices, part, LANES).astype(BF)
                 at = at + part
+            spare = send_ref.shape[1] - at
+            send_ref[:, at:] = jnp.zeros((devices, spare, LANES), BF)
 
 
 def third_kernel(
     share, rows, sum_ref, acts_ref, ds_ref, dlogit_ref, mask_ref, mix_ref, right_ref, gx_ref, wt_ref, w_ref,
-    fg_ref, dmix_ref, dright_ref, gin_ref, gainx_ref, dproj_ref, *stage,
+    fg_ref, dmix_ref, dright_ref, gin_ref, gains_ref, gainx_ref, dproj_ref, acc_ref, *stage,
 ):
     @pl.when(pl.program_id(0) == 0)
     def _():
-        for acc in (dright_ref, gin_ref, gainx_ref):
+        for acc in (dright_ref, acc_ref, gainx_ref):
             acc[...] = jnp.zeros_like(acc)
         if stage:
             unship(acts_ref, stage[0], 6, share, rows)
@@ -375,30 +352,318 @@
                 dproj_ref[(block + 4) * hidden : (block + 5) * hidden] = d_gate.astype(BF)
         dproj_ref[8 * hidden :] = dlogit_ref[r]
         d_proj = dproj_ref[...]
-        gin_ref[...] += mm(d_proj, norm, NT)
+        acc_ref[...] += mm(d_proj, norm, NT)
         back = mm(w_ref[...], d_proj)
         gainx_ref[...] += back * hat
         first = ds_ref[r] + norm_rows_back(back * gx_ref[...], hat, inv)
         fg_ref[r] = first
         low = first.astype(BF)
         dmix_ref[r] = mm(right_ref[...], low, NT).astype(BF)
-        dright_ref[...] += mm(mix_ref[r], low)
-
-
-def last_kernel(xt_ref, fg_ref, ds_ref, gain_ref, w_ref, out_ref, gw_ref, gainb_ref):
+        right = mm(mix_ref[r], low)
+        for half in range(dright_ref.shape[0]):
+            dright_ref[half] += right[:, half * LANES : (half + 1) * LANES]
+
+    @pl.when(pl.program_id(0) == pl.num_programs(0) - 1)
+    def _():
+        gin_ref[...] = turn_blocks(acc_ref).astype(BF)
+        gains_ref[...] = lane_sums(gainx_ref)
+
+
+def last_kernel(xt_ref, fg_ref, ds_ref, gain_ref, w_ref, out_ref):
+    for r in range(xt_ref.shape[0]):
+        hat, inv = norm_rows(xt_ref[r].astype(F32))
+        back = mm(w_ref[...], ds_ref[r])
+        out_ref[r] = (fg_ref[r] + norm_rows_back(back * gain_ref[...], hat, inv)).T
+
+
+def norm_lanes(values):
+    centred = values - jnp.mean(values, axis=1, keepdims=True)
+    inv = lax.rsqrt(jnp.mean(centred * centred, axis=1, keepdims=True) + EPS)
+    return centred * inv, inv
+
+
+def norm_lanes_back(scaled, hat, inv):
+    return inv * (
+        scaled
+        - jnp.mean(scaled, axis=1, keepdims=True)
+        - hat * jnp.mean(scaled * hat, axis=1, keepdims=True)
+    )
+
+
+def head_lanes(heads, width):
+    depth = width // heads
+    lane = lax.broadcasted_iota(jnp.int32, (heads, width), 1)
+    head = lax.broadcasted_iota(jnp.int32, (heads, width), 0)
+    return ((lane >= head * depth) & (lane < (head + 1) * depth)).astype(F32)
+
+
+def rows_by_head(values, lanes):
+    spread = values[:, None, :] * lanes[None]
+    return spread.reshape(-1, values.shape[1])
+
+
+def heads_by_row(values, lanes):
+    spread = values[None] * lanes[:, None, :]
+    return spread.reshape(-1, values.shape[1])
+
+
+def crop_rows(residues):
+    return pl.ds(pl.multiple_of(lax.axis_index("crop") * residues, residues), residues)
+
+
+def attend_kernel(
+    both_ref, own_ref, gain_ref, w_ref, bias_ref, mask_ref,
+    norm_ref, gate_ref, qkv_ref, weights_ref, low_ref, gated_ref,
+):
+    width = own_ref.shape[1]
+    residues = mask_ref.shape[2]
+    heads = bias_ref.shape[1]
+    rows = own_ref.shape[0]
+    scale = 1.0 / (width // heads) ** 0.5
+    hat, _ = norm_lanes(both_ref[:, :width].astype(F32))
+    norm_ref[...] = (hat * gain_ref[...]).astype(BF)
+    gate_ref[...] = jax.nn.sigmoid(mm(norm_ref[...], w_ref[:, 3 * width :]))
+    qkv_ref[...] = mm(norm_ref[crop_rows(residues), :], w_ref[:, : 3 * width]).astype(BF)
+    keys, values = qkv_ref[:, width : 2 * width], qkv_ref[:, 2 * width :]
+    hat, _ = norm_lanes(own_ref[...].astype(F32))
+    own = (hat * gain_ref[...]).astype(BF)
+    query = mm(own, w_ref[:, :width]).astype(BF).astype(F32)
+    gate = jax.nn.sigmoid(mm(own, w_ref[:, 3 * width :]))
+    lanes = head_lanes(heads, width)
+    query = rows_by_head(query, lanes).astype(BF)
+    scores = mm(query, keys, NT) * scale + bias_ref[...].reshape(rows * heads, residues)
+    mask = jnp.broadcast_to(mask_ref[...], bias_ref.shape).reshape(rows * heads, residues)
+    scores = jnp.where(mask > 0.5, scores, -1000000000.0)
+    powers = jnp.exp(scores - jnp.max(scores, axis=1, keepdims=True))
+    weights = powers / jnp.sum(powers, axis=1, keepdims=True)
+    weights_ref[...] = weights
+    low = weights.astype(BF)
+    low_ref[...] = low
+    attn = mm(low, values).reshape(rows, heads, width)
+    attn = jnp.sum(attn * lanes[None], axis=1)
+    gated_ref[...] = (gate * attn).astype(BF)
+
+
+def node_chunks(rows):
+    size = min(rows, LANES)
+    return [slice(k * size, (k + 1) * size) for k in range(rows // size)]
+
+
+def gelu_parts(up):
+    square = up * up
+    curve = jnp.tanh(0.7978845608 * up * (1.0 + 0.044715 * square))
+    half = 0.5 * (1.0 + curve)
+    slope = half + up * (1.0 - curve * curve) * (0.3989422804 + 0.05351611220 * square)
+    return up * half, slope
+
+
+def node_kernel(
+    both_ref, gated_ref, gn_ref, gs_ref, wo_ref, wu_ref, wd_ref, wn_ref, wr_ref,
+    mid_ref, next_ref, proj_ref, right_ref, norm_ref,
+):
+    width = gated_ref.shape[1]
+    residues = right_ref.shape[1]
+    for rows in node_chunks(gated_ref.shape[0]):
+        mid = both_ref[rows, :width].astype(F32) + mm(gated_ref[rows], wo_ref[...])
+        mid_ref[rows] = mid
+        hat, _ = norm_lanes(mid)
+        act, _ = gelu_parts(mm((hat * gn_ref[...]).astype(BF), wu_ref[...]))
+        following = mid + mm(act.astype(BF), wd_ref[...])
+        next_ref[rows] = following
+        hat, _ = norm_lanes(following)
+        norm = (hat * gs_ref[...]).astype(BF)
+        norm_ref[rows] = norm
+        proj_ref[rows] = mm(norm, wn_ref[...]).astype(BF)
+    right_ref[...] = mm(wr_ref[...], norm_ref[crop_rows(residues), :], NT).astype(BF)
+
+
+def sublane_sum(values):
+    return jnp.sum(values, axis=0, keepdims=True)
+
+
+def node_back_kernel(
+    outer_dim, got_ref, left_ref, both_ref, mid_ref, next_ref, gated_ref, gate_ref,
+    gn_ref, gs_ref, wo_ref, wu_ref, wd_ref, wn_ref,
+    gnode_ref, gd_ref, gu_ref, gout_ref, gains_ref, gainn_ref,
+    dmid_ref, dattn_ref, dgate_ref, inner_ref,
+    proj_ref, norm_ref, act_ref, low_ref, trans_ref, up_ref, midlow_ref,
+):
+    width = gated_ref.shape[1]
+    devices = got_ref.shape[0] // 2
+    halves = gated_ref.shape[0] // 2 // LANES
+    at = 0
+    for crop in range(2):
+        for half in range(halves):
+            total = jnp.zeros((outer_dim, LANES), F32)
+            for d in range(devices):
+                part = got_ref[crop * devices + d, half * outer_dim : (half + 1) * outer_dim]
+                total += part.astype(F32)
+            above = jnp.zeros((outer_dim, LANES), F32)
+            below = jnp.zeros((LANES - 2 * outer_dim, LANES), F32)
+            turned = jnp.concatenate([above, total, below], axis=0).T
+            if left_ref.shape[0] == gated_ref.shape[0]:
+                left = left_ref[at : at + LANES].astype(F32)
+            else:
+                rows = gated_ref.shape[0] // got_ref.shape[0]
+                own = slice(halves * outer_dim, halves * outer_dim + rows)
+                left = got_ref[at // rows : (at + LANES) // rows, own].astype(F32)
+                left = left.reshape(LANES, LANES)
+            proj_ref[at : at + LANES] = (turned + left).astype(BF)
+            at = at + LANES
+    gains, gainn = jnp.zeros((1, width), F32), jnp.zeros((1, width), F32)
+    for rows in node_chunks(gated_ref.shape[0]):
+        hat, inv = norm_lanes(next_ref[rows])
+        norm_ref[rows] = (hat * gs_ref[...]).astype(BF)
+        back = mm(proj_ref[rows], wn_ref[...], NT)
+        gains += sublane_sum(back * hat)
+        d_next = both_ref[rows, width:].astype(F32)
+        d_next += norm_lanes_back(back * gs_ref[...], hat, inv)
+        low = d_next.astype(BF)
+        low_ref[rows] = low
+        hat, inv = norm_lanes(mid_ref[rows])
+        trans = (hat * gn_ref[...]).astype(BF)
+        trans_ref[rows] = trans
+        act, slope = gelu_parts(mm(trans, wu_ref[...]))
+        act_ref[rows] = act.astype(BF)
+        d_up = (mm(low, wd_ref[...], NT) * slope).astype(BF)
+        up_ref[rows] = d_up
+        back = mm(d_up, wu_ref[...], NT)
+        gainn += sublane_sum(back * hat)
+        d_mid = d_next + norm_lanes_back(back * gn_ref[...], hat, inv)
+        dmid_ref[rows] = d_mid
+        low = d_mid.astype(BF)
+        midlow_ref[rows] = low
+        d_gated = mm(low, wo_ref[...], NT)
+        gate = gate_ref[rows]
+        product = d_gated * gated_ref[rows].astype(F32)
+        inner_ref[rows] = product
+        dattn_ref[rows] = (d_gated * gate).astype(BF)
+        dgate_ref[rows] = (product * (1.0 - gate)).astype(BF)
+    gains_ref[...] = gains
+    gainn_ref[...] = gainn
+    gnode_ref[...] = mm(proj_ref[...], norm_ref[...], TN)[: 2 * outer_dim]
+    gd_ref[...] = mm(act_ref[...], low_ref[...], TN)
+    gu_ref[...] = mm(trans_ref[...], up_ref[...], TN)
+    gout_ref[...] = mm(gated_ref[...], midlow_ref[...], TN)
+
+
+def attend_back_kernel(
+    own_ref, dattn_ref, inner_ref, qkv_ref, values_ref, weights_ref, column_ref, norm_ref,
+    ds_ref, grad_ref, bias_ref,
+):
+    width = own_ref.shape[1]
+    residues = qkv_ref.shape[0]
+    rows, _, _ = norm_ref.shape
+    heads = ds_ref.shape[0] // rows
+    scale = 1.0 / (width // heads) ** 0.5
+    lanes = head_lanes(heads, width)
+    query, keys = qkv_ref[:, :width], qkv_ref[:, width : 2 * width]
+    own = rows_by_head(own_ref[...].astype(F32), lanes).astype(BF)
+    d_weights = mm(own, qkv_ref[:, 2 * width :], NT)
+    weights = weights_ref[...]
+    inner = jnp.sum(d_weights * weights, axis=1, keepdims=True)
+    d_scores = (weights * (d_weights - inner)).astype(BF)
+    ds_ref[...] = d_scores
+    d_query = mm(d_scores, keys).reshape(rows, heads, width)
+    d_query = jnp.sum(d_query * lanes[None], axis=1) * scale
+    total = jnp.zeros(bias_ref.shape, F32)
+    for r in range(rows):
+        total += mm(d_scores[r * heads : (r + 1) * heads], norm_ref[r], NT)
+    bias_ref[...] = total
+    crop = crop_rows(residues)
+    d_attn = dattn_ref[crop, :]
+    spread = heads_by_row(values_ref[...].astype(F32), lanes).astype(BF)
+    ones = heads_by_row(jnp.ones(values_ref.shape, F32), lanes).astype(BF)
+    product = inner_ref[crop, :]
+    high = product.astype(BF)
+    rest = (product - high.astype(F32)).astype(BF)
+    inner = mm(high, ones, NT) + mm(rest, ones, NT)
+    column = column_ref[...]
+    d_column = (column.astype(F32) * (mm(d_attn, spread, NT) - inner)).astype(BF)
+    d_key = mm(d_column, query, TN).reshape(heads, rows, width)
+    d_key = jnp.sum(d_key * lanes[:, None, :], axis=0) * scale
+    d_value = mm(column, d_attn, TN).reshape(heads, rows, width)
+    d_value = jnp.sum(d_value * lanes[:, None, :], axis=0)
+    at = 0
+    for part in (d_query, d_key, d_value):
+        for half in range(width // LANES):
+            grad_ref[at] = part[:, half * LANES : (half + 1) * LANES].astype(BF)
+            at = at + 1
+
+
+def adam_refs(master_ref, first_ref, second_ref, grad, outs):
+    for ref, value in zip(
+        outs, adam_step(master_ref[...], first_ref[...], second_ref[...], grad, 0.1, 0.1)
+    ):
+        ref[...] = value
+
+
+def adam_kernel(count, *refs):
+    for k in range(count):
+        master, first, second, grad = refs[4 * k : 4 * k + 4]
+        outs = refs[4 * count + 3 * k : 4 * count + 3 * k + 3]
+        adam_refs(master, first, second, grad[...], outs)
+
+
+def unpack(take, every, layout):
+    count, late_rows, half_rows, part_up, part_z, in_blocks, outer_rows, small_rows = layout
+    blocks, at = [], 0
+    for _ in range(6):
+        blocks.append(take(at, at + count).reshape(-1, LANES))
+        at = at + count
+    late = take(at, at + late_rows).reshape(-1, LANES)
+    at = at + late_rows
+    pair = take(at, at + half_rows)
+    small = jnp.sum(take(at + half_rows, at + half_rows + small_rows), axis=0)
+    lower, upper = pair[: every // 2], pair[every // 2 :]
+    over = 2 * part_up - half_rows
+    g_up = jnp.concatenate([lower[:, part_up:], upper[:, :over]], axis=1).reshape(-1, LANES)
+    across = lambda g: jnp.concatenate(
+        [g[k * LANES : (k + 1) * LANES] for k in range(g.shape[0] // LANES)], axis=1
+    )
+    g_in = across(late[: in_blocks * LANES])
+    g_outer = late[in_blocks * LANES : in_blocks * LANES + outer_rows]
+    g_down = lower[:, :part_up].reshape(-1, LANES)
+    g_z = upper[:, over : over + part_z].reshape(-1, LANES)
+    return blocks, (g_outer, g_in, g_z, across(g_up), g_down), small
+
+
+def final_kernel(
+    layout, dgate_ref, norm_ref, both_ref, dmid_ref, gain_ref, w_ref, *refs
+):
+    n_got = 1 if layout else 12
+    got, refs = refs[:n_got], refs[n_got:]
+    olds, refs = refs[:18], refs[18:]
+    news, (dnode_ref, gaina_ref, small_ref, grad_ref), sums = refs[:18], refs[18:22], refs[22:]
+    width = dmid_ref.shape[1]
+
     @pl.when(pl.program_id(0) == 0)
     def _():
-        for acc in (gw_ref, gainb_ref):
-            acc[...] = jnp.zeros_like(acc)
-
-    for r in range(xt_ref.shape[0]):
-        hat, inv = norm_rows(xt_ref[r].astype(F32))
-        norm = (hat * gain_ref[...]).astype(BF)
-        d_bias = ds_ref[r]
-        gw_ref[...] += mm(d_bias, norm, NT)
-        back = mm(w_ref[...], d_bias)
-        gainb_ref[...] += back * hat
-        out_ref[r] = (fg_ref[r] + norm_rows_back(back * gain_ref[...], hat, inv)).T
+        if layout:
+            take = lambda start, stop: got[0][:, start:stop].astype(F32)
+            blocks, grads, small = unpack(take, got[0].shape[0], layout)
+        else:
+            values = [ref[...] for ref in got]
+            blocks, grads, small = values[:6], values[6:11], values[11]
+        small_ref[...] = small
+        for ref, grad in zip(sums[1:], grads):
+            ref[...] = grad
+        for k, block in enumerate(blocks):
+            grad_ref[:, k * LANES : (k + 1) * LANES] = block.astype(BF)
+        grad_ref[:, 3 * width :] = dgate_ref[...]
+        sums[0][...] = mm(norm_ref[...], grad_ref[...], TN)
+        total = jnp.zeros((1, width), F32)
+        for rows in node_chunks(dmid_ref.shape[0]):
+            hat, inv = norm_lanes(both_ref[rows, :width].astype(F32))
+            back = mm(grad_ref[rows], w_ref[...], NT)
+            total += sublane_sum(back * hat)
+            dnode_ref[rows] = dmid_ref[rows] + norm_lanes_back(back * gain_ref[...], hat, inv)
+        gaina_ref[...] = total
+
+    for k in range(6):
+        height = olds[3 * k].shape[0]
+        start = pl.multiple_of(pl.program_id(0) * height, height)
+        adam_refs(*olds[3 * k : 3 * k + 3], sums[k][pl.ds(start, height), :], news[3 * k : 3 * k + 3])
 
 
 def whole(shape):
@@ -430,8 +695,6 @@
     count, _, residues, width_z = pair_feats.shape
     width_s = node_feats.shape[2]
     heads = w_pairbias.shape[1]
-    depth = width_s // heads
-    scale = 1.0 / depth**0.5
     outer_dim = w_node.shape[1] // 2
     hidden = (w_in.shape[1] - width_z) // 8
     expand = w_up.shape[1]
@@ -444,6 +707,8 @@
         at = at + cut
     gain_a, gain_b, gain_n, gain_s, gain_x, gain_t, gain_h = gains
     column = lambda gain: gain.reshape(-1, 1)
+    line = lambda gain: gain.reshape(1, -1)
+    nodes = 2 * residues
     crop_index, row_index = lax.axis_index("crop"), lax.axis_index("row")
     first_row = row_index * count
     chains = chain_ids[0]
@@ -459,20 +724,18 @@
     up_wb, down_wb = w_up.astype(BF), w_down.astype(BF)
     bias_wt, in_wt, z_wt, up_wt, down_wt = bias_wb.T, in_wb.T, z_wb.T, up_wb.T, down_wb.T
 
+    direct = count % 16 == 0
     step = 2 if count % 2 == 0 else 1
     steps = count // step
     pairs = count * residues
 
     node_both = jnp.concatenate([node_feats[:, 0], node_out_grad[:, 0]], axis=1)
-    node_both = gather_all(node_both, row_devices).reshape(2 * residues, 2 * width_s)
-    node_all, cot_all = node_both[:, :width_s], node_both[:, width_s:]
-    node_f32 = node_all.astype(F32)
-
     pair_x = pair_feats[:, 0]
-    xt, pair_bias = pair_call(
+    xt, bias_norm, pair_bias = pair_call(
         bias_kernel, steps,
         [by_row(step, (residues, width_z)), whole((width_z, 1)), whole((heads, width_z))],
         [(by_row(step, (width_z, residues)), shape_of((count, width_z, residues), BF)),
+         (by_row(step, (width_z, residues)), shape_of((count, width_z, residues), BF)),
          (by_row(step, (heads, residues)), shape_of((count, heads, residues), F32))],
         [pair_x, column(gain_b), bias_wt],
         flops=2 * pairs * width_z * heads, moved=4 * pairs * width_z,
@@ -481,47 +744,46 @@
     def own_rows(values):
         return lax.dynamic_slice_in_dim(values, crop_index * residues + first_row, count, 0)
 
-    def own_crop(values):
-        return lax.dynamic_slice_in_dim(values, crop_index * residues, residues, 0)
-
-    att_hat, att_back = jax.vjp(layer_norm, node_f32, gain_a)
-    att_norm = att_hat.astype(BF)
-    qkvg = mm(att_norm, att_wb)
-    gate_all = jax.nn.sigmoid(qkvg[:, 3 * width_s :])
-    qkv_crop = own_crop(qkvg[:, : 3 * width_s]).astype(BF)
-    query_crop, keys, values = (
-        qkv_crop[:, k * width_s : (k + 1) * width_s].reshape(residues, heads, depth)
-        for k in range(3)
-    )
-    own_row_of = lambda v: lax.dynamic_slice_in_dim(v, first_row, count, 0)
-    query = own_row_of(query_crop)
-    raw_scores = jnp.einsum("ihd,jhd->ihj", query, keys, preferred_element_type=F32) * scale
-    scores = jnp.where(same_own[:, None, :], raw_scores + pair_bias, -1000000000.0)
-    att_weights = jax.nn.softmax(scores, axis=-1)
-    weights_low = att_weights.astype(BF)
-    attn = jnp.einsum("ihj,jhd->ihd", weights_low, values, preferred_element_type=F32)
-    gated_own = (own_rows(gate_all) * attn.reshape(count, width_s)).astype(BF)
-    gated = gather_all(gated_own, row_devices).reshape(2 * residues, width_s)
-
-    node_mid = node_f32 + mm(gated, attout_wb)
-    ntrans_hat, ntrans_back = jax.vjp(layer_norm, node_mid, gain_n)
-    trans_node = ntrans_hat.astype(BF)
-    node_upv = mm(trans_node, nodeup_wb)
-    nact_val, nact_back = jax.vjp(gelu_tanh, node_upv)
-    node_act = nact_val.astype(BF)
-    node_next = node_mid + mm(node_act, nodedown_wb)
+    def single(kernel, outs, args, scratch=(), flops=0):
+        moved = sum(arg.size * 4 for arg in args)
+        return pair_call(
+            kernel, 1, [whole(arg.shape) for arg in args],
+            [(whole(shape), shape_of(shape, kind)) for shape, kind in outs],
+            args, scratch, flops, moved,
+        )
+
+    columns = [column(gain) for gain in (gain_x, gain_t, gain_h)]
+    ready = [att_wb, attout_wb, nodeup_wb, nodedown_wb, mask]
+    node_both = gather_all(node_both, row_devices, [xt, pair_bias] + ready)
+    node_both = node_both.reshape(nodes, 2 * width_s)
+    square = (nodes, width_s)
+    att_norm, gate_all, qkv_crop, att_weights, weights_low, gated_own = single(
+        attend_kernel,
+        [(square, BF), (square, F32), ((residues, 3 * width_s), BF),
+         ((count * heads, residues), F32), ((count * heads, residues), BF),
+         ((count, width_s), BF)],
+        [node_both, node_feats[:, 0], line(gain_a), att_wb, pair_bias, mask],
+        flops=8 * nodes * width_s * width_s,
+    )
+    weights_cut = weights_low.reshape(count, heads, row_devices, count).transpose(2, 0, 1, 3)
+    if direct:
+        weights_cut = weights_cut.reshape(row_devices, -1, LANES)
+    ready = [weights_cut, node_wb, outer_wb, in_wt, chain_col, columns[0]]
+    gated = gather_all(gated_own, row_devices, ready).reshape(nodes, width_s)
+
+    node_mid, node_next, node_proj, right_t = single(
+        node_kernel,
+        [(square, F32), (square, F32), ((nodes, 2 * outer_dim), BF), ((outer_dim, residues), BF)],
+        [node_both, gated, line(gain_n), line(gain_s), attout_wb, nodeup_wb, nodedown_wb, node_wb,
+         node_wb[:, outer_dim:].T],
+        scratch=[pltpu.VMEM(square, BF)], flops=18 * nodes * width_s * width_s,
+    )
     node_out = own_rows(node_next).astype(BF)[:, None]
-    node_hat, node_back = jax.vjp(layer_norm, node_next, gain_s)
-    node_norm = node_hat.astype(BF)
-    node_proj = mm(node_norm, node_wb).astype(BF)
     left_vec = own_rows(node_proj[:, :outer_dim])
-    right_t = own_crop(node_proj[:, outer_dim:]).T
     outer_mix = mm(left_vec, outer_wb).astype(BF).reshape(count, outer_dim, width_z)
 
     share = hidden // row_devices
-    direct = count % 16 == 0
     dims = (share, count) if direct else None
-    weights_cut = weights_low.reshape(count, heads, row_devices, count).transpose(2, 0, 1, 3)
 
     def sent_block(tiles, extra=0):
         if direct:
@@ -558,7 +820,7 @@
         spec = pl.BlockSpec((1, tiles, 1, residues, LANES), lambda i: (0, 0, i, 0, 0))
         return spec, shape_of(shape, BF)
 
-    ride = weights_cut.reshape(row_devices, -1, LANES) if direct else jnp.zeros((1, 1, LANES), BF)
+    ride = weights_cut if direct else jnp.zeros((1, 1, LANES), BF)
     extra = ride.shape[1]
     first_sum, acts_own = pair_call(
         functools.partial(first_kernel, share, count), steps,
@@ -574,11 +836,10 @@
 
     chain_specs = [whole((residues, 1)), whole((1, residues))]
     product = 2 * share * residues**3
-    acts = to_channels(acts_own)
-    if direct:
-        weights_col = acts[:, 6 * share * count :].reshape(residues, heads, count)
-    else:
-        weights_col = swap(weights_cut).reshape(residues, heads, count)
+    ready = [in_wb, z_wb, up_wb, down_wb, z_wt, up_wt, down_wt] + columns
+    acts = after(to_channels(acts_own), ready)
+    weights_col = acts[:, 6 * share * count :] if direct else swap(weights_cut)
+    weights_col = weights_col.reshape(residues, heads * count)
     (tri,) = pair_call(
         functools.partial(tri_kernel, dims), share, chain_specs + [tri_block(6, extra)[0]],
         [tri_block(3)], [chain_col, chain_row, acts],
@@ -600,13 +861,14 @@
             in_wt[8 * hidden :], z_wt, z_wb, up_wt, up_wb, down_wt, down_wb,
         )
     ]
-    grad_rows = 2 * expand + 2 * hidden
-    carried = grad_rows // row_devices if direct else 0
+    part_up, part_z = expand // row_devices, 2 * hidden // row_devices
+    half_rows = part_up + part_up // 2
+    carried = 2 * half_rows if direct else 0
     acc_shapes = [
         (expand, width_z), (expand, width_z), (2 * hidden, width_z),
-        (2 * hidden, residues), (width_z, residues),
+        ((2 * hidden + width_z) // LANES, LANES),
     ]
-    pair_out, d_second, d_logit, dtri_own, g_down, g_up_t, g_z, gain_t_acc, gain_h_acc = pair_call(
+    pair_out, d_second, d_logit, dtri_own, g_down, g_up_t, g_z, gains_th = pair_call(
         functools.partial(second_kernel, share, count), steps,
         [spec for spec, _ in second_args],
         [(by_row(step, (residues, width_z)), shape_of((count, residues, width_z), BF)),
@@ -615,7 +877,8 @@
          sent_block(3, carried)]
         + [(whole(s), shape_of(s, F32)) for s in acc_shapes],
         [arg for _, arg in second_args],
-        scratch=stage(3) + stage(3),
+        scratch=[pltpu.VMEM((2 * hidden, residues), F32), pltpu.VMEM((width_z, residues), F32)]
+        + stage(3) + stage(3),
         flops=12 * pairs * width_z * expand, moved=20 * pairs * width_z,
     )
 
@@ -623,10 +886,11 @@
     if direct:
         grad_parts = dtri[:, 3 * share * count :]
     else:
-        cut = lambda g: g.reshape(row_devices, -1, LANES)
-        grad_parts = swap(jnp.concatenate([cut(g) for g in (g_down, g_up_t, g_z)], 1).astype(BF))
+        turned = g_up_t.reshape(-1, LANES, LANES).transpose(0, 2, 1)
+        parts = [g.reshape(row_devices, -1, LANES) for g in (g_down, turned, g_z)]
+        spare = jnp.zeros((row_devices, part_up - part_z, LANES), F32)
+        grad_parts = swap(jnp.concatenate(parts + [spare], axis=1).astype(BF))
     row_sum = jnp.sum(grad_parts.astype(F32), axis=0)
-    half_rows = row_sum.shape[0] // 2
     lower, upper = row_sum[:half_rows], row_sum[half_rows:]
     low_crop = crop_index == 0
     theirs = lax.ppermute(jnp.where(low_crop, upper, lower), "crop", [(0, 1), (1, 0)])
@@ -637,132 +901,138 @@
         [tri_block(6)], [chain_col, chain_row, acts, dtri],
         flops=4 * product, moved=share * residues * 15 * 256,
     )
-    dacts_rows = to_rows(dacts)
-
-    first_grad, d_mix, d_right, g_in_t, gain_x_acc = pair_call(
+    dacts_rows = after(to_rows(dacts), pair_own)
+
+    first_grad, d_mix, d_right, g_in_blocks, gains_x = pair_call(
         functools.partial(third_kernel, share, count), steps,
         [slab, sent_block(6)[0], slab, slab, by_row(step, (1, residues)),
          by_row(step, (outer_dim, width_z)), whole((outer_dim, residues)), whole((width_z, 1)),
          whole(in_wt.shape), whole(in_wb.shape)],
         [(slab, shape_of((count, width_z, residues), F32)),
          (by_row(step, (outer_dim, width_z)), shape_of((count, outer_dim, width_z), BF)),
-         (whole((outer_dim, residues)), shape_of((outer_dim, residues), F32)),
-         (whole(in_wt.shape), shape_of(in_wt.shape, F32)),
-         (whole((width_z, residues)), shape_of((width_z, residues), F32))],
+         (whole((residues // LANES, outer_dim, LANES)),
+          shape_of((residues // LANES, outer_dim, LANES), F32)),
+         (whole(in_wt.shape), shape_of(in_wt.shape, BF)),
+         (whole((width_z // LANES, LANES)), shape_of((width_z // LANES, LANES), F32))],
         [first_sum, dacts_rows, d_second, d_logit, mask, outer_mix, right_t, column(gain_x),
          in_wt, in_wb],
-        scratch=[pltpu.VMEM((9 * hidden, residues), BF)] + stage(6),
+        scratch=[pltpu.VMEM((width_z, residues), F32), pltpu.VMEM((9 * hidden, residues), BF),
+                 pltpu.VMEM(in_wt.shape, F32)] + stage(6),
         flops=54 * pairs * width_z * hidden, moved=20 * pairs * width_z,
     )
 
     mix_flat = d_mix.reshape(count, outer_dim * width_z)
-    d_left = back_dot(mix_flat, outer_wb)
-    packed = jnp.concatenate([d_right.reshape(-1), d_left.reshape(-1)]).astype(BF)
-    size = packed.shape[0]
-    unit = 16 * LANES
-    packed = jnp.pad(packed, (0, -size % unit)).reshape(-1, LANES)
-    got = gather_all(packed, row_devices)
-    g_outer = cross_sum(left_vec, mix_flat)
-    gain_accs = [gain_x_acc, gain_t_acc, gain_h_acc]
-    late_flat = join_flat([g_in_t, g_outer] + [lanes_sum(acc) for acc in gain_accs])
-    late_own = scatter_sum(after(late_flat, got), row_devices)
-    got = got.reshape(2, row_devices, -1)[:, :, :size].astype(F32)
-    right_sum = jnp.sum(got[:, :, : outer_dim * residues], axis=1)
-    right_sum = right_sum.reshape(2, outer_dim, residues).transpose(0, 2, 1)
-    left_all = got[:, :, outer_dim * residues :].reshape(2, residues, outer_dim)
-    proj_grad = jnp.concatenate([left_all, right_sum], axis=-1).astype(BF)
-    proj_grad = proj_grad.reshape(2 * residues, 2 * outer_dim)
-
-    g_node = cross_sum(node_norm, proj_grad)
-    outer_node_grad, gain_s_grad = node_back(back_dot(proj_grad, node_wb))
-    grad_next = cot_all.astype(F32) + outer_node_grad
-    next_low = grad_next.astype(BF)
-    g_nodedown = cross_sum(node_act, next_low)
-    (nact_grad,) = nact_back(back_dot(next_low, nodedown_wb))
-    nodeup_low = nact_grad.astype(BF)
-    g_nodeup = cross_sum(trans_node, nodeup_low)
-    ntrans_grad, gain_n_grad = ntrans_back(back_dot(nodeup_low, nodeup_wb))
-    grad_mid = grad_next + ntrans_grad
-    mid_low = grad_mid.astype(BF)
-    g_attout = cross_sum(gated, mid_low)
-    gated_grad = back_dot(mid_low, attout_wb)
-    attn_grad = (gated_grad * gate_all).astype(BF)
-    gate_grad = (gated_grad * gated.astype(F32) * (1.0 - gate_all)).astype(BF)
-
-    attn_grad_crop = own_crop(attn_grad).reshape(residues, heads, depth)
-    attn_grad_own = own_row_of(attn_grad_crop)
-    weight_grad = jnp.einsum("ihd,jhd->ihj", attn_grad_own, values, preferred_element_type=F32)
-    inner = jnp.sum(weight_grad * att_weights, axis=-1, keepdims=True)
-    score_grad = (att_weights * (weight_grad - inner)).astype(BF)
-    query_grad = jnp.einsum("ihj,jhd->ihd", score_grad, keys, preferred_element_type=F32) * scale
-
-    values_own = own_row_of(values)
-    inner_crop = jnp.sum(
-        (own_crop(gated_grad) * own_crop(gated).astype(F32)).reshape(residues, heads, depth),
-        axis=-1, keepdims=True,
-    )
-    weight_grad_col = jnp.einsum(
-        "ihd,jhd->ihj", attn_grad_crop, values_own, preferred_element_type=F32
-    )
-    score_grad_col = (weights_col.astype(F32) * (weight_grad_col - inner_crop)).astype(BF)
-    key_grad = (
-        jnp.einsum("ihj,ihd->jhd", score_grad_col, query_crop, preferred_element_type=F32) * scale
-    )
-    value_grad = jnp.einsum("ihj,ihd->jhd", weights_col, attn_grad_crop, preferred_element_type=F32)
-    qkv_grad = jnp.concatenate(
-        [v.reshape(count, width_s) for v in (query_grad, key_grad, value_grad)], axis=-1
-    ).astype(BF)
-
-    pair_grad, g_bias_t, gain_b_acc = pair_call(
+    d_left = mm(mix_flat, outer_wb, NT)
+    right_rows = d_right.shape[0] * outer_dim
+    left_rows = jnp.pad(d_left, ((0, 0), (0, LANES - outer_dim)))
+    packed = jnp.concatenate([d_right.reshape(right_rows, LANES), left_rows]).astype(BF)
+
+    g_outer = mm(left_vec, mix_flat, TN).reshape(outer_dim * outer_dim, width_z).astype(BF)
+    late_rows = g_in_blocks.shape[0] + g_outer.shape[0]
+    spare = jnp.zeros((-late_rows % (every * 16), LANES), BF)
+    late = jnp.concatenate([g_in_blocks, g_outer, spare]).reshape(every, -1, LANES)
+    got = gather_all(packed, row_devices, late)
+    late_own = scatter_sum(after(late, got))
+    left_all = left_rows
+    if not direct:
+        left_all = got[:, right_rows : right_rows + count].reshape(nodes, LANES)
+
+    wide_node = jnp.pad(node_wb, ((0, 0), (0, LANES - 2 * outer_dim)))
+    tall, low_square = (nodes, w_nodeup.shape[1]), pltpu.VMEM(square, BF)
+    (g_node, g_nodedown, g_nodeup, g_attout, gain_s_grad, gain_n_grad,
+     grad_mid, d_attn, d_gate, inner) = single(
+        functools.partial(node_back_kernel, outer_dim),
+        [((2 * outer_dim, width_s), F32), (w_nodedown.shape, F32), (w_nodeup.shape, F32),
+         (w_attout.shape, F32), ((1, width_s), F32), ((1, width_s), F32),
+         (square, F32), (square, BF), (square, BF), (square, F32)],
+        [got, left_all, node_both, node_mid, node_next, gated, gate_all,
+         line(gain_n), line(gain_s), attout_wb, nodeup_wb, nodedown_wb, wide_node],
+        scratch=[pltpu.VMEM((nodes, LANES), BF), low_square, pltpu.VMEM(tall, BF), low_square,
+                 low_square, pltpu.VMEM(tall, BF), low_square],
+        flops=50 * nodes * width_s * width_s,
+    )
+
+    values_own = lax.dynamic_slice(qkv_crop, (first_row, 2 * width_s), (count, width_s))
+    score_grad, qkv_grad, g_bias_t = single(
+        attend_back_kernel,
+        [((count * heads, residues), BF), ((3 * width_s // LANES, count, LANES), BF),
+         ((heads, width_z), F32)],
+        [own_rows(d_attn), d_attn, inner, qkv_crop, values_own, att_weights, weights_col,
+         bias_norm],
+        flops=12 * count * heads * residues * width_s,
+    )
+
+    small = jnp.concatenate([g_bias_t, gains_x, gains_th]).astype(BF)
+    small = jnp.pad(small, ((0, -small.shape[0] % 16), (0, 0)))
+    pieces = [qkv_grad.reshape(-1, LANES), late_own, pair_own, small]
+    layout = (
+        count, late_own.shape[0], half_rows, part_up, part_z,
+        in_wb.shape[1] // LANES, g_outer.shape[0], small.shape[0],
+    )
+
+    (pair_grad,) = pair_call(
         last_kernel, steps,
         [slab, slab, by_row(step, (heads, residues)), whole((width_z, 1)), whole((width_z, heads))],
-        [(by_row(step, (residues, width_z)), shape_of((count, residues, width_z), F32)),
-         (whole((heads, width_z)), shape_of((heads, width_z), F32)),
-         (whole((width_z, residues)), shape_of((width_z, residues), F32))],
-        [xt, first_grad, score_grad, column(gain_b), bias_wb],
+        [(by_row(step, (residues, width_z)), shape_of((count, residues, width_z), F32))],
+        [xt, first_grad, score_grad.reshape(count, heads, residues), column(gain_b), bias_wb],
         flops=4 * pairs * width_z * heads, moved=10 * pairs * width_z,
     )
 
-    bias_flat = join_flat([g_bias_t, lanes_sum(gain_b_acc)]).astype(BF)
-    pieces = [qkv_grad.reshape(-1, LANES), late_own, pair_own, bias_flat.reshape(-1, LANES)]
-    highs = [piece.shape[0] for piece in pieces]
-    tail = jnp.zeros((-sum(highs) % 16, LANES), BF)
-    last = gather_all(jnp.concatenate(pieces + [tail]), row_devices)
-    ends = [sum(highs[: k + 1]) for k in range(len(highs))]
-    qkv_grad_all = last[:, : ends[0]].reshape(2 * residues, 3 * width_s)
-    late_sums = last[:, ends[0] : ends[1]].reshape(-1).astype(F32)
-    pair_sums = last[:, ends[1] : ends[2]].astype(F32).reshape(2, row_devices, -1, LANES)
-    bias_parts = last[:, ends[2] : ends[3]].astype(F32)
-    qkvg_grad = jnp.concatenate([qkv_grad_all, gate_grad], axis=-1)
-    g_attend = cross_sum(att_norm, qkvg_grad)
-    att_in_grad, gain_a_grad = att_back(back_dot(qkvg_grad, att_wb))
-    node_grad = own_rows(grad_mid + att_in_grad)[:, None]
-
-    g_in_t, g_outer, gain_x_grad, gain_t_grad, gain_h_grad = split_flat(
-        late_sums, [g_in_t, w_outer, gain_x, gain_t, gain_h]
-    )
-    g_bias_t, gain_b_grad = split_flat(jnp.sum(bias_parts, axis=0).reshape(-1), [g_bias_t, gain_b])
-    pair_sums = pair_sums.transpose(1, 0, 2, 3).reshape(row_devices, 2 * half_rows, LANES)
-    found, start = [], 0
-    for total in (g_down, g_up_t, g_z):
-        part = total.shape[0] // row_devices
-        found.append(pair_sums[:, start : start + part].reshape(total.shape))
-        start = start + part
-    g_down, g_up_t, g_z = found
+    parts = 8
+    split = lambda k: pl.BlockSpec((olds[k].shape[0] // parts, olds[k].shape[1]), lambda i: (i, 0))
+    updated = {}
+
+    early = {2: g_attout, 3: g_nodeup, 4: g_nodedown, 5: g_node}
+    turned = lambda k, value: value.T if k == 5 else value
+    specs, args, outs = [], [], []
+    for k, grad in early.items():
+        spec = pl.BlockSpec((grad.shape[0] // parts, grad.shape[1]), lambda i: (i, 0))
+        specs += [spec] * 4
+        args += [turned(k, old[k]) for old in (masters, firsts, seconds)] + [grad]
+        outs += [(spec, shape_of(grad.shape, F32))] * 3
+    found = pair_call(
+        functools.partial(adam_kernel, len(early)), parts, specs, outs, args,
+        moved=sum(7 * arg.size for arg in args),
+    )
+    last = gather_all(jnp.concatenate(pieces), row_devices, (pair_grad, found[0]))
+    for at, k in enumerate(early):
+        updated[k] = [turned(k, value) for value in found[3 * at : 3 * at + 3]]
+
+    late_keys = (0, 6, 7, 8, 9, 10)
+    got_last = [last]
+    if not direct:
+        blocks, sums, small = unpack(lambda a, b: last[:, a:b].astype(F32), every, layout)
+        got_last = blocks + list(sums) + [small]
+    fixed = [d_gate, att_norm, node_both, grad_mid, line(gain_a), att_wb] + got_last
+    olds, specs = [], [whole(arg.shape) for arg in fixed]
+    for k in late_keys:
+        olds += [masters[k], firsts[k], seconds[k]]
+    blocked = [split(k) for k in range(len(olds))]
+    found = pair_call(
+        functools.partial(final_kernel, layout if direct else None), parts, specs + blocked,
+        [(spec, shape_of(old.shape, F32)) for spec, old in zip(blocked, olds)]
+        + [(whole(shape), shape_of(shape, F32)) for shape in (square, (1, width_s), small.shape)],
+        fixed + olds,
+        scratch=[pltpu.VMEM((nodes, 4 * width_s), BF)]
+        + [pltpu.VMEM(masters[k].shape, F32) for k in late_keys],
+        flops=16 * nodes * width_s * width_s, moved=sum(7 * old.size for old in olds),
+    )
+    for at, k in enumerate(late_keys):
+        updated[k] = found[3 * at : 3 * at + 3]
+    d_nodes, gain_a_grad, small = found[18:]
+    node_grad = own_rows(d_nodes)[:, None]
+
+    g_bias = small[:heads].T
+    gain_b_grad = jnp.sum(bias_wb.astype(F32) * g_bias, axis=1) / gain_b
+    pair_gains = small[heads : heads + gains_x.shape[0] + gains_th.shape[0]].reshape(-1)
     gain_grad = jnp.concatenate(
-        [gain_a_grad, gain_b_grad, gain_n_grad, gain_s_grad, gain_x_grad, gain_t_grad, gain_h_grad]
-    )
-    grads = [
-        g_attend, g_bias_t.T, g_attout, g_nodeup, g_nodedown, g_node, g_outer, g_in_t.T, g_z,
-        g_up_t.T, g_down, gain_grad,
-    ]
+        [gain_a_grad[0], gain_b_grad, gain_n_grad[0], gain_s_grad[0], pair_gains]
+    )
+    updated[1] = adam_step(masters[1], firsts[1], seconds[1], g_bias, 0.1, 0.1)
+    updated[11] = adam_step(masters[11], firsts[11], seconds[11], gain_grad, 1.0, 0.0)
     results = [pair_out[:, None], node_out, pair_grad[:, None], node_grad]
-    rates = [0.1] * 11 + [1.0]
-    decays = [0.1] * 11 + [0.0]
-    for master, first_old, second_old, grad, rate, decay in zip(
-        masters, firsts, seconds, grads, rates, decays
-    ):
-        results.extend(adam_step(master, first_old, second_old, grad, rate, decay))
+    for k in range(12):
+        results.extend(updated[k])
     return tuple(results)
 
 

time: 510 us -> 471 us (0.924)
  matrix products: 38.6 us -> 1.29 us
  Pallas kernels: 73.3 us -> 106 us
  waiting for transfers between devices: 177 us -> 162 us
  other arithmetic: 38 us -> 25.1 us
  local copies, waits for them, and re-layouts: 62 us -> 53.6 us
    pallas_call x7 -> x13, Pallas kernels: 73.3 us -> 106 us  [pair_call(): pl.pallas_call(kernel, grid=(steps,), in_specs=ins, out_specs=[spec for s...]
    dot_general x18 -> x3, matrix products: 33.6 us -> 1.29 us  [mm(): return lax.dot_general(left, right, dims, preferred_element_type=F32)]
    all_to_all x4, waiting for transfers between devices: 36.8 us -> 17.2 us  [gather_all(): lax.all_to_all(spread, BOTH, split_axis=0, concat_axis=0, tiled=True, axi...]
    all_to_all x3, waiting for transfers between devices: 140 us -> 132 us  [swap(): return lax.all_to_all(block, 'row', split_axis=0, concat_axis=0, tiled=True)]
    sub x7 -> x2, other arithmetic: 8.41 us -> 1.25 us  [adam_step(): master - rate * (first_hat / (jnp.sqrt(second_hat) + 1e-08) + decay * mas...]
    all_to_all x1, waiting for transfers between devices: 0.01 us -> 6.02 us  [scatter_sum(): parts = lax.all_to_all(sent, BOTH, split_axis=0, concat_axis=0, tiled=True)]
    reduce_sum x14 -> x0, other arithmetic: 5.81 us -> none  [the longest x1 1.58 us: shards(): jnp.sum((own_crop(gated_grad) * own_crop(gated).astype(F32)).reshape(resi...]
    unnamed x271 -> x241, local copies, waits for them, and re-layouts: 34.3 us -> 32.7 us
  transfers between devices with their start and end apart: 13 -> 13, of which waited for: 8 -> 12; matrix products, arithmetic and copies ran while one was open for 15% -> 7% of each run, Pallas kernels for 1% -> 5%
where the time goes in v2:
time: 471 us; the launch traced here: 469 us
  waiting for transfers between devices  162 us (34%)
  Pallas kernels  106 us (23%)
  starting transfers between devices  64.1 us (14%)
  blocking collectives  54.3 us (12%)
  local copies, waits for them, and re-layouts  53.6 us (11%)
  other arithmetic  25.1 us (5%)
    all_to_all x3, waiting for transfers between devices, swap(): return lax.all_to_all(block, 'row', split_axis=0, concat_axis=0, tiled=True)  132 us
    pallas_call x13, Pallas kernels, pair_call(): pl.pallas_call(kernel, grid=(steps,), in_specs=ins, out_specs=[spec for s...  106 us
    all_to_all x1, blocking collectives, swap(): return lax.all_to_all(block, 'row', split_axis=0, concat_axis=0, tiled=True)  54.3 us
    all_to_all x4, starting transfers between devices, gather_all(): lax.all_to_all(spread, BOTH, split_axis=0, concat_axis=0, tiled=True, axi...  35.5 us
    unnamed x241, local copies, waits for them, and re-layouts  32.7 us
    all_to_all x3, starting transfers between devices, swap(): return lax.all_to_all(block, 'row', split_axis=0, concat_axis=0, tiled=True)  24.3 us
    all_to_all x4, waiting for transfers between devices, gather_all(): lax.all_to_all(spread, BOTH, split_axis=0, concat_axis=0, tiled=True, axi...  17.2 us
  transfers between devices with their start and end apart: 13, of which 12 were waited for; matrix products, arithmetic and copies ran while one was open for 7% of the time, Pallas kernels for 5%

profile of v2, /device:TPU:0, one launch (start us, length us, event | category | flops | bytes accessed | tf_op | source)
XLA Modules:
  0.0 468.5 jit_solution(12284184267106843957)
XLA Ops:
  2.3 8.4 %all-to-all-start = ((bf16[16,16,512]{2,1,0:T(8,128)(2,1)}), bf16[16,16,512]{2,1,0:T(8,128)(2,1)}, u32[]{:S(2)}, u32[]{:S(2)}) async-start(bf16[16,16,512]{2,1,0:T(8,128)(2,1)} %broadcast_in_dim.18), calls=%async_computation | async-start | bytes 524288 | tf_op jit(solution)/shard_map/all_to_all | solution.py:42
  29.2 6.9 %all-to-all-start.1 = ((bf16[16,16,256]{2,1,0:T(8,128)(2,1)}), bf16[16,16,256]{2,1,0:T(8,128)(2,1)S(1)}, u32[]{:S(2)}, u32[]{:S(2)}) async-start(bf16[16,16,256]{2,1,0:T(8,128)(2,1)} %broadcast_in_dim.19), calls=%async_computation.1 | async-start | bytes 262144 | tf_op jit(solution)/shard_map/all_to_all | solution.py:42
  45.6 3.9 shard_map.701
  52.0 11.8 %shard_map.702 = (f32[16,128,256]{2,1,0:T(8,128)S(1)}, bf16[16,784,128]{2,1,0:T(8,128)(2,1)}) custom-call(bf16[16,128,256]{2,1,0:T(8,128)(2,1)S(1)} %copy-done.26, bf16[16,32,128]{2,1,0:T(8,128)(2,1)S(1)} %bitcast.121, bf16[32,256]{1,0:T(8,128)(2,1)S(1)} %get-tuple-element.125.right_ref, f32[16,1,256]{2,1,0:T(1,128)S(1)} %compare_convert_fusion.mask_ref, ...), custom_call_target="tpu_custom_call" | custom-call | flops 1073741824 | bytes 6291456 | tf_op jit(solution)/shard_map/pallas_call | solution.py:678
  65.1 3.9 all-to-all-start.2
  79.0 50.4 %all-to-all-done.2.acts_ref = bf16[16,784,128]{2,1,0:T(8,128)(2,1)S(1)} async-done(((bf16[16,784,128]{2,1,0:T(8,128)(2,1)}), bf16[16,784,128]{2,1,0:T(8,128)(2,1)S(1)}, u32[]{:S(2)}, u32[]{:S(2)}) %all-to-all-start.2) | async-done | bytes 3211296 | tf_op jit(solution)/shard_map/all_to_all | solution.py:798
  131.1 3.6 shard_map.703
  135.9 15.7 %all-to-all-start.3 = ((bf16[16,384,128]{2,1,0:T(8,128)(2,1)}), bf16[16,384,128]{2,1,0:T(8,128)(2,1)S(1)}, u32[]{:S(2)}, u32[]{:S(2)}) async-start(bf16[16,384,128]{2,1,0:T(8,128)(2,1)} %copy-done.1), calls=%async_computation.3 | async-start | bytes 3145728 | tf_op jit(solution)/shard_map/all_to_all | solution.py:798
  157.0 26.5 %all-to-all-done.3.tri_ref = bf16[16,384,128]{2,1,0:T(8,128)(2,1)S(1)} async-done(((bf16[16,384,128]{2,1,0:T(8,128)(2,1)}), bf16[16,384,128]{2,1,0:T(8,128)(2,1)S(1)}, u32[]{:S(2)}, u32[]{:S(2)}) %all-to-all-start.3) | async-done | bytes 1572896 | tf_op jit(solution)/shard_map/all_to_all | solution.py:798
  188.2 25.7 %shard_map.704 = (bf16[16,256,128]{2,1,0:T(8,128)(2,1)}, f32[16,128,256]{2,1,0:T(8,128)}, bf16[16,128,256]{2,1,0:T(8,128)(2,1)S(1)}, bf16[16,480,128]{2,1,0:T(8,...) custom-call(f32[16,128,256]{2,1,0:T(8,128)} %copy-done.103, ...), custom_call_target="tpu_custom_call" | custom-call | flops 3221225472 | bytes 10485760 | tf_op jit(solution)/shard_map/pallas_call | solution.py:678
  214.9 54.3 %all_to_all.45.grad_ref = bf16[16,480,128]{2,1,0:T(8,128)(2,1)S(1)} all-to-all(bf16[16,480,128]{2,1,0:T(8,128)(2,1)} %get-tuple-element.131), channel_id=1, replica_groups=mesh['crop'=2,'row'=16] {'row'}, dimensions={0} | all-to-all | bytes 3932160 | tf_op jit(solution)/shard_map/all_to_all | solution.py:798
  269.2 8.2 %shard_map.705 = bf16[16,768,128]{2,1,0:T(8,128)(2,1)} custom-call(s32[256,1]{1,0:T(8,128)S(1)} %copy-done.16, s32[1,256]{1,0:T(1,128)S(1)} %copy-done.86, bf16[16,784,128]{2,1,0:T(8,128)(2,1)} %copy-done, bf16[16,480,128]{2,1,0:T(8,128)(2,1)S(1)} %all_to_all.45.grad_ref), custom_call_target="tpu_custom_call" | custom-call | flops 1073741824 | bytes 7864320 | tf_op jit(solution)/shard_map/pallas_call | solution.py:678
  277.3 4.7 %all-to-all-start.5 = ((bf16[16,768,128]{2,1,0:T(8,128)(2,1)}), bf16[16,768,128]{2,1,0:T(8,128)(2,1)}, u32[]{:S(2)}, u32[]{:S(2)}) async-start(bf16[16,768,128]{2,1,0:T(8,128)(2,1)} %shard_map.705), calls=%async_computation.5 | async-start | bytes 6291456 | tf_op jit(solution)/shard_map/all_to_all | solution.py:798
  286.7 54.8 %all-to-all-done.5.acts_ref = bf16[16,768,128]{2,1,0:T(8,128)(2,1)} async-done(((bf16[16,768,128]{2,1,0:T(8,128)(2,1)}), bf16[16,768,128]{2,1,0:T(8,128)(2,1)}, u32[]{:S(2)}, u32[]{:S(2)}) %all-to-all-start.5) | async-done | bytes 3145760 | tf_op jit(solution)/shard_map/all_to_all | solution.py:798
  342.8 17.4 %shard_map.706 = (f32[16,128,256]{2,1,0:T(8,128)S(1)}, bf16[16,32,128]{2,1,0:T(8,128)(2,1)S(1)}, f32[2,32,128]{2,1,0:T(8,128)S(1)}, bf16[1152,128]{1,0:T(8,128)(2,1)S(1)}, f32[1,128]{1,0:T(1,128)S(1)}) custom-call(f32[16,128,256]{2,1,0:T(8,128)} %copy-done.103, bf16[16,768,128]{2,1,0:T(8,128)(2,1)} %all-to-all-done.5.acts_ref, ...), custom_call_target="tpu_custom_call" | custom-call | flops 3623878656 | bytes 10485760 | tf_op jit(solution)/shard_map/pallas_call | solution.py:678
  363.6 15.7 %all-to-all-start.6 = ((bf16[16,80,128]{2,1,0:T(8,128)(2,1)}), bf16[16,80,128]{2,1,0:T(8,128)(2,1)S(1)}, u32[]{:S(2)}, u32[]{:S(2)}) async-start(bf16[16,80,128]{2,1,0:T(8,128)(2,1)} %broadcast_in_dim.22), calls=%async_computation.6 | async-start | bytes 655360 | tf_op jit(solution)/shard_map/all_to_all | solution.py:42
  380.5 10.5 %all-to-all-done.6 = bf16[16,80,128]{2,1,0:T(8,128)(2,1)S(1)} async-done(((bf16[16,80,128]{2,1,0:T(8,128)(2,1)}), bf16[16,80,128]{2,1,0:T(8,128)(2,1)S(1)}, u32[]{:S(2)}, u32[]{:S(2)}) %all-to-all-start.6) | async-done | bytes 327712 | tf_op jit(solution)/shard_map/all_to_all | solution.py:42
  400.4 6.2 %shard_map.707 = (f32[64,256]{1,0:T(8,128)S(1)}, f32[1024,256]{1,0:T(8,128)}, f32[256,1024]{1,0:T(8,128)}, f32[256,256]{1,0:T(8,128)S(1)}, f32[1,256]{1,0:T(1,12...) custom-call(bf16[32,80,128]{2,1,0:T(8,128)(2,1)S(1)} %bitcast.114, ...), custom_call_target="tpu_custom_call" | custom-call | flops 1677721600 | bytes 6957056 | tf_op jit(solution)/shard_map/pallas_call | solution.py:678
  409.0 6.0 %all-to-all-done.7 = bf16[32,80,128]{2,1,0:T(8,128)(2,1)} async-done(((bf16[32,80,128]{2,1,0:T(8,128)(2,1)}), bf16[32,80,128]{2,1,0:T(8,128)(2,1)}, u32[]{:S(2)}, u32[]{:S(2)}) %all-to-all-start.7) | async-done | bytes 655392 | tf_op jit(solution)/shard_map/all_to_all | solution.py:53
  418.7 4.6 all-to-all-start.8
  430.9 8.6 %shard_map.710 = (f32[256,256]{1,0:T(8,128)}, f32[256,256]{1,0:T(8,128)}, f32[256,256]{1,0:T(8,128)}, f32[256,1024]{1,0:T(8,128)}, f32[256,1024]{1,0:T(8,128)}, ...) custom-call(f32[256,256]{1,0:T(8,128)S(1)} %copy-done.23, ...), custom_call_target="tpu_custom_call" | custom-call | bytes 16973824 | tf_op jit(solution)/shard_map/pallas_call | solution.py:678
  439.5 4.6 shard_map.709
  444.1 3.4 all-to-all-done.8
  455.0 11.6 %shard_map.711 = (f32[256,1024]{1,0:T(8,128)}, f32[256,1024]{1,0:T(8,128)}, f32[256,1024]{1,0:T(8,128)}, f32[1024,128]{1,0:T(8,128)}, f32[1024,128]{1,0:T(8,128)...) custom-call(bf16[512,256]{1,0:T(8,128)(2,1)S(1)} %copy-done.54, ...), custom_call_target="tpu_custom_call" | custom-call | flops 536870912 | bytes 14794752 | tf_op jit(solution)/shard_map/pallas_call | solution.py:678
  (339 shorter events, 99.4 us)
Async XLA Ops:
  2.3 19.1 %all-to-all-start = ((bf16[16,16,512]{2,1,0:T(8,128)(2,1)}), bf16[16,16,512]{2,1,0:T(8,128)(2,1)}, u32[]{:S(2)}, u32[]{:S(2)}) async-start(bf16[16,16,512]{2,1,0:T(8,128)(2,1)} %broadcast_in_dim.18), calls=%async_computation | async-start | bytes 524288 | tf_op jit(solution)/shard_map/all_to_all | solution.py:42
  21.4 1.8 collective-permute-start
  21.6 23.9 %copy-start.28 = (bf16[256,64]{1,0:T(8,128)(2,1)}, bf16[256,64]{1,0:T(8,128)(2,1)S(1)}, u32[]{:S(2)}) copy-start(bf16[256,64]{1,0:T(8,128)(2,1)S(1)} %copy.106.wn_ref) | copy-start | bytes 98308
  22.5 28.6 %copy-start.108 = (bf16[32,4096]{1,0:T(8,128)(2,1)}, bf16[32,4096]{1,0:T(8,128)(2,1)S(1)}, u32[]{:S(2)}) copy-start(bf16[32,4096]{1,0:T(8,128)(2,1)S(1)} %reshape.234) | copy-start | bytes 786436
  23.1 22.4 %copy-start.89 = (f32[256]{0:T(256)}, f32[256]{0:T(256)S(1)}, u32[]{:S(2)}) copy-start(f32[256]{0:T(256)S(1)} %get-tuple-element.295) | copy-start | bytes 3076
  23.1 22.4 %copy-start.91 = (f32[256]{0:T(256)}, f32[256]{0:T(256)S(1)}, u32[]{:S(2)}) copy-start(f32[256]{0:T(256)S(1)} %get-tuple-element.296) | copy-start | bytes 3076
  29.2 14.9 %all-to-all-start.1 = ((bf16[16,16,256]{2,1,0:T(8,128)(2,1)}), bf16[16,16,256]{2,1,0:T(8,128)(2,1)S(1)}, u32[]{:S(2)}, u32[]{:S(2)}) async-start(bf16[16,16,256]{2,1,0:T(8,128)(2,1)} %broadcast_in_dim.19), calls=%async_computation.1 | async-start | bytes 262144 | tf_op jit(solution)/shard_map/all_to_all | solution.py:42
  44.1 1.3 collective-permute-start.1
  65.1 64.3 %all-to-all-start.2 = ((bf16[16,784,128]{2,1,0:T(8,128)(2,1)}), bf16[16,784,128]{2,1,0:T(8,128)(2,1)S(1)}, u32[]{:S(2)}, u32[]{:S(2)}) async-start(bf16[16,784,128]{2,1,0:T(8,128)(2,1)} %get-tuple-element.127), calls=%async_computation.2 | async-start | bytes 6422528 | tf_op jit(solution)/shard_map/all_to_all | solution.py:798
  135.9 47.6 %all-to-all-start.3 = ((bf16[16,384,128]{2,1,0:T(8,128)(2,1)}), bf16[16,384,128]{2,1,0:T(8,128)(2,1)S(1)}, u32[]{:S(2)}, u32[]{:S(2)}) async-start(bf16[16,384,128]{2,1,0:T(8,128)(2,1)} %copy-done.1), calls=%async_computation.3 | async-start | bytes 3145728 | tf_op jit(solution)/shard_map/all_to_all | solution.py:798
  214.9 54.3 %copy-start.16 = (s32[256,1]{1,0:T(8,128)S(1)}, s32[256,1]{1,0:T(8,128)}, u32[]{:S(2)}) copy-start(s32[256,1]{1,0:T(8,128)} %copy.111.col_ref) | copy-start | bytes 3076
  214.9 54.3 %copy-start.86 = (s32[1,256]{1,0:T(1,128)S(1)}, s32[1,256]{1,0:T(1,128)}, u32[]{:S(2)}) copy-start(s32[1,256]{1,0:T(1,128)} %row_ref.3) | copy-start | bytes 3076
  277.3 64.2 %copy-start.40 = (bf16[128,1152]{1,0:T(8,128)(2,1)S(1)}, bf16[128,1152]{1,0:T(8,128)(2,1)}, u32[]{:S(2)}) copy-start(bf16[128,1152]{1,0:T(8,128)(2,1)} %convert_element_type.86.w_ref) | copy-start | bytes 884740
  277.3 64.2 %copy-start.42 = (bf16[1152,128]{1,0:T(8,128)(2,1)S(1)}, bf16[1152,128]{1,0:T(8,128)(2,1)}, u32[]{:S(2)}) copy-start(bf16[1152,128]{1,0:T(8,128)(2,1)} %copy-done.41) | copy-start | bytes 884740
  277.3 64.2 %copy-start.69 = (bf16[2,8,32,128]{3,2,1,0:T(8,128)(2,1)S(1)}, bf16[2,8,32,128]{3,2,1,0:T(8,128)(2,1)}, u32[]{:S(2)}) copy-start(bf16[2,8,32,128]{3,2,1,0:T(8,128)(2,1)} %copy-done.68) | copy-start | bytes 393220
  277.3 64.2 %copy-start.81 = (f32[128,1]{1,0:T(8,128)S(1)}, f32[128,1]{1,0:T(8,128)}, u32[]{:S(2)}) copy-start(f32[128,1]{1,0:T(8,128)} %copy.109.gain_ref.gx_ref) | copy-start | bytes 1540
  277.3 64.2 %copy-start.102 = (bf16[32,256]{1,0:T(8,128)(2,1)S(1)}, bf16[32,256]{1,0:T(8,128)(2,1)}, u32[]{:S(2)}) copy-start(bf16[32,256]{1,0:T(8,128)(2,1)} %copy-done.101) | copy-start | bytes 49156
  277.3 64.2 %all-to-all-start.5 = ((bf16[16,768,128]{2,1,0:T(8,128)(2,1)}), bf16[16,768,128]{2,1,0:T(8,128)(2,1)}, u32[]{:S(2)}, u32[]{:S(2)}) async-start(bf16[16,768,128]{2,1,0:T(8,128)(2,1)} %shard_map.705), calls=%async_computation.5 | async-start | bytes 6291456 | tf_op jit(solution)/shard_map/all_to_all | solution.py:798
  282.2 3.9 collective-permute-start.2
  363.6 27.5 %all-to-all-start.6 = ((bf16[16,80,128]{2,1,0:T(8,128)(2,1)}), bf16[16,80,128]{2,1,0:T(8,128)(2,1)S(1)}, u32[]{:S(2)}, u32[]{:S(2)}) async-start(bf16[16,80,128]{2,1,0:T(8,128)(2,1)} %broadcast_in_dim.22), calls=%async_computation.6 | async-start | bytes 655360 | tf_op jit(solution)/shard_map/all_to_all | solution.py:42
  391.1 1.7 collective-permute-start.3
  393.0 22.0 %all-to-all-start.7 = ((bf16[32,80,128]{2,1,0:T(8,128)(2,1)}), bf16[32,80,128]{2,1,0:T(8,128)(2,1)}, u32[]{:S(2)}, u32[]{:S(2)}) async-start(bf16[32,80,128]{2,1,0:T(8,128)(2,1)} %bitcast.144), calls=%async_computation.7 | async-start | bytes 1310720 | tf_op jit(solution)/shard_map/all_to_all | solution.py:53
  418.7 28.8 %all-to-all-start.8 = ((bf16[16,240,128]{2,1,0:T(8,128)(2,1)}), bf16[16,240,128]{2,1,0:T(8,128)(2,1)}, u32[]{:S(2)}, u32[]{:S(2)}) async-start(bf16[16,240,128]{2,1,0:T(8,128)(2,1)} %broadcast_in_dim.48), calls=%async_computation.8 | async-start | bytes 1966080 | tf_op jit(solution)/shard_map/all_to_all | solution.py:42
  447.5 2.9 collective-permute-start.4
  (107 other events, 597.3 us)

commit v3 on v2

--- a/solution.py
+++ b/solution.py
@@ -144,20 +144,24 @@
     sum_ref, send_ref, *stage,
 ):
     hidden = weight_ref.shape[0] // 9
-    for r in range(xt_ref.shape[0]):
-        row = pl.program_id(0) * xt_ref.shape[0] + r
-        total = xt_ref[r].astype(F32) + mm(mix_ref[r], right_ref[...], TN)
-        sum_ref[r] = total
-        hat, _ = norm_rows(total)
-        norm = (hat * gain_ref[...]).astype(BF)
-        mask = mask_ref[r]
+    step, _, residues = xt_ref.shape
+    columns = [slice(r * residues, (r + 1) * residues) for r in range(step)]
+    mixes = [mm(mix_ref[r], right_ref[...], TN) for r in range(step)]
+    total = jnp.concatenate([xt_ref[r].astype(F32) + mixes[r] for r in range(step)], axis=1)
+    for r in range(step):
+        sum_ref[r] = total[:, columns[r]]
+    hat, _ = norm_rows(total)
+    norm = (hat * gain_ref[...]).astype(BF)
+    mask = jnp.concatenate([mask_ref[r] for r in range(step)], axis=1)
+    for pair in range(2):
         acts = []
-        for block in range(4):
+        for block in (2 * pair, 2 * pair + 1):
             value = mm(weight_ref[block * hidden : (block + 1) * hidden], norm)
             gate = mm(weight_ref[(block + 4) * hidden : (block + 5) * hidden], norm)
             acts.append(jax.nn.sigmoid(gate) * value * mask)
-        for pair in range(2):
-            tiles = fold_pair(acts[2 * pair], acts[2 * pair + 1])
+        for r in range(step):
+            row = pl.program_id(0) * step + r
+            tiles = fold_pair(*(act[:, columns[r]] for act in acts))
             for t in range(3):
                 if stage:
                     put_tile(stage[0], 3 * pair + t, row, rows, tiles[t])
@@ -175,18 +179,13 @@
     return col_ref[...] == row_ref[...]
 
 
-def channel_rows(dims, tile):
-    share, rows = dims
-    return pl.ds(pl.multiple_of((tile * share + pl.program_id(0)) * rows, rows), rows)
-
-
-def flat_rows(ref, tile, dims):
-    block = ref[:, channel_rows(dims, tile)] if dims else ref[:, tile, 0]
+def flat_rows(ref, tile, spot):
+    block = ref[:, spot(tile)] if spot else ref[:, tile, 0]
     return block.reshape(-1, block.shape[-1])
 
 
-def slot_operands(ref, pair, dims):
-    main_f, main_s, tail = (flat_rows(ref, 3 * pair + t, dims).astype(F32) for t in range(3))
+def slot_operands(ref, pair, spot):
+    main_f, main_s, tail = (flat_rows(ref, 3 * pair + t, spot).astype(F32) for t in range(3))
     low = low_lanes(tail.shape)
     zero = jnp.zeros_like(tail)
     first = jnp.concatenate([main_f, jnp.where(low, tail, zero)], axis=1).astype(BF)
@@ -194,6 +193,19 @@
     return first, second
 
 
+def channel_spots(dims):
+    if not dims:
+        return [None]
+    share, rows = dims
+    each = share // pl.num_programs(0)
+    first = pl.program_id(0) * each
+
+    def spot_of(channel):
+        return lambda tile: pl.ds(pl.multiple_of((tile * share + channel) * rows, rows), rows)
+
+    return [spot_of(first + k) for k in range(each)]
+
+
 def raw_columns(slots, same):
     values = slots.astype(F32)
     main, tail = values[:, :LANES], values[:, LANES:]
@@ -203,45 +215,47 @@
     return jnp.where(same, wide, 0.0).astype(BF)
 
 
-def store_tiles(out_ref, pair, dims, tiles):
+def store_tiles(out_ref, pair, spot, tiles):
     for t in range(3):
         block = tiles[t].astype(BF).reshape(out_ref.shape[0], -1, LANES)
-        if dims:
-            out_ref[:, channel_rows(dims, 3 * pair + t)] = block
+        if spot:
+            out_ref[:, spot(3 * pair + t)] = block
         else:
             out_ref[:, 3 * pair + t, 0] = block
 
 
 def tri_kernel(dims, col_ref, row_ref, acts_ref, out_ref):
     same = chain_mask(col_ref, row_ref)
-    left_out, right_out = slot_operands(acts_ref, 0, dims)
-    left_in, right_in = slot_operands(acts_ref, 1, dims)
-    outgoing = jnp.where(same, mm(left_out, right_out, NT), 0.0)
-    incoming = mm(raw_columns(left_in, same), right_in, TN)
-    low = low_lanes((outgoing.shape[0], LANES))
-    o_lo, o_hi = outgoing[:, :LANES], outgoing[:, LANES:]
-    main_o = o_lo + jnp.where(low, turn(o_hi), 0.0)
-    tail = jnp.where(low, o_hi, turn(incoming[:, LANES:]))
-    store_tiles(out_ref, 0, dims, (main_o, incoming[:, :LANES], tail))
+    for spot in channel_spots(dims):
+        left_out, right_out = slot_operands(acts_ref, 0, spot)
+        left_in, right_in = slot_operands(acts_ref, 1, spot)
+        outgoing = jnp.where(same, mm(left_out, right_out, NT), 0.0)
+        incoming = mm(raw_columns(left_in, same), right_in, TN)
+        low = low_lanes((outgoing.shape[0], LANES))
+        o_lo, o_hi = outgoing[:, :LANES], outgoing[:, LANES:]
+        main_o = o_lo + jnp.where(low, turn(o_hi), 0.0)
+        tail = jnp.where(low, o_hi, turn(incoming[:, LANES:]))
+        store_tiles(out_ref, 0, spot, (main_o, incoming[:, :LANES], tail))
 
 
 def tri_back_kernel(dims, col_ref, row_ref, acts_ref, grad_ref, out_ref):
     same = chain_mask(col_ref, row_ref)
-    left_out, right_out = slot_operands(acts_ref, 0, dims)
-    left_in, right_in = slot_operands(acts_ref, 1, dims)
-    grad_out, grad_in = slot_operands(grad_ref, 0, dims)
-    raw_out = raw_columns(grad_out, same)
-    d_left = mm(raw_out, right_out)
-    d_right = mm(raw_out, left_out, TN)
-    low = low_lanes((d_left.shape[0], LANES))
-    tail = jnp.where(low, d_left[:, LANES:], turn(d_right[:, LANES:]))
-    store_tiles(out_ref, 0, dims, (d_left[:, :LANES], d_right[:, :LANES], tail))
-    d_left = jnp.where(same, mm(right_in, grad_in, NT), 0.0)
-    d_right = mm(raw_columns(left_in, same), grad_in)
-    l_lo, l_hi = d_left[:, :LANES], d_left[:, LANES:]
-    main_l = l_lo + jnp.where(low, turn(l_hi), 0.0)
-    tail = jnp.where(low, l_hi, turn(d_right[:, LANES:]))
-    store_tiles(out_ref, 1, dims, (main_l, d_right[:, :LANES], tail))
+    for spot in channel_spots(dims):
+        left_out, right_out = slot_operands(acts_ref, 0, spot)
+        left_in, right_in = slot_operands(acts_ref, 1, spot)
+        grad_out, grad_in = slot_operands(grad_ref, 0, spot)
+        raw_out = raw_columns(grad_out, same)
+        d_left = mm(raw_out, right_out)
+        d_right = mm(raw_out, left_out, TN)
+        low = low_lanes((d_left.shape[0], LANES))
+        tail = jnp.where(low, d_left[:, LANES:], turn(d_right[:, LANES:]))
+        store_tiles(out_ref, 0, spot, (d_left[:, :LANES], d_right[:, :LANES], tail))
+        d_left = jnp.where(same, mm(right_in, grad_in, NT), 0.0)
+        d_right = mm(raw_columns(left_in, same), grad_in)
+        l_lo, l_hi = d_left[:, :LANES], d_left[:, LANES:]
+        main_l = l_lo + jnp.where(low, turn(l_hi), 0.0)
+        tail = jnp.where(low, l_hi, turn(d_right[:, LANES:]))
+        store_tiles(out_ref, 1, spot, (main_l, d_right[:, :LANES], tail))
 
 
 def second_kernel(
@@ -257,44 +271,56 @@
         if stage:
             unship(tri_ref, stage[0], 3, share, rows)
 
-    for r in range(sum_ref.shape[0]):
-        row = pl.program_id(0) * sum_ref.shape[0] + r
-        total = sum_ref[r]
-        mask = mask_ref[r]
-        hat_x, _ = norm_rows(total)
-        norm = (hat_x * gx_ref[...]).astype(BF)
-        out_gate = jax.nn.sigmoid(mm(wgate_ref[...], norm))
+    step, _, residues = sum_ref.shape
+    joined = lambda values: jnp.concatenate(list(values), axis=1)
+    total = joined(sum_ref[r] for r in range(step))
+    mask = joined(mask_ref[r] for r in range(step))
+    hat_x, _ = norm_rows(total)
+    norm = (hat_x * gx_ref[...]).astype(BF)
+    out_gate = jax.nn.sigmoid(mm(wgate_ref[...], norm))
+    combined = []
+    for r in range(step):
+        row = pl.program_id(0) * step + r
         if stage:
             tiles = [get_tile(stage[0], t, row, rows, total.shape[0]) for t in range(3)]
         else:
             tiles = [tri_ref[r, t].astype(F32) for t in range(3)]
-        tri_out, tri_in = unfold_pair(*tiles)
-        hat_t, inv_t = norm_rows(jnp.concatenate([tri_out, tri_in], axis=0))
-        tri_norm = (hat_t * gt_ref[...]).astype(BF)
-        tri_proj = mm(wzt_ref[...], tri_norm)
-        second = total + out_gate * tri_proj * mask
-        hat_h, inv_h = norm_rows(second)
-        trans_in = (hat_h * gh_ref[...]).astype(BF)
-        act, slope = gelu_parts(mm(wut_ref[...], trans_in))
-        act = act.astype(BF)
-        out_ref[r] = (second + mm(wdt_ref[...], act)).T.astype(BF)
-        grad_low = grad_ref[r].astype(F32).T.astype(BF)
-        gd_ref[...] += mm(act, grad_low, NT)
-        d_up = (mm(wd_ref[...], grad_low) * slope).astype(BF)
-        gu_ref[...] += mm(d_up, trans_in, NT)
-        back = mm(wu_ref[...], d_up)
-        gainh_ref[...] += back * hat_h
-        d_second = grad_low.astype(F32) + norm_rows_back(back * gh_ref[...], hat_h, inv_h)
-        ds_ref[r] = d_second
-        gated = d_second * mask * out_gate
-        d_tri = gated.astype(BF)
-        dlogit_ref[r] = (gated * tri_proj * (1.0 - out_gate)).astype(BF)
-        gz_ref[...] += mm(tri_norm, d_tri, NT)
-        back = mm(wz_ref[...], d_tri)
-        gaint_ref[...] += back * hat_t
-        comb = norm_rows_back(back * gt_ref[...], hat_t, inv_t)
-        hidden = comb.shape[0] // 2
-        tiles = fold_pair(comb[:hidden], comb[hidden:])
+        combined.append(jnp.concatenate(unfold_pair(*tiles), axis=0))
+    hat_t, inv_t = norm_rows(joined(combined))
+    tri_norm = (hat_t * gt_ref[...]).astype(BF)
+    tri_proj = mm(wzt_ref[...], tri_norm)
+    second = total + out_gate * tri_proj * mask
+    hat_h, inv_h = norm_rows(second)
+    trans_in = (hat_h * gh_ref[...]).astype(BF)
+    act, slope = gelu_parts(mm(wut_ref[...], trans_in))
+    act = act.astype(BF)
+    result = second + mm(wdt_ref[...], act)
+    for r in range(step):
+        out_ref[r] = result[:, r * residues : (r + 1) * residues].T.astype(BF)
+    grad_low = joined(grad_ref[r].astype(F32).T.astype(BF) for r in range(step))
+    gd_ref[...] += mm(act, grad_low, NT)
+    d_up = (mm(wd_ref[...], grad_low) * slope).astype(BF)
+    gu_ref[...] += mm(d_up, trans_in, NT)
+    back = mm(wu_ref[...], d_up)
+    prod = back * hat_h
+    gainh_ref[...] += sum(prod[:, r * residues : (r + 1) * residues] for r in range(step))
+    d_second = grad_low.astype(F32) + norm_rows_back(back * gh_ref[...], hat_h, inv_h)
+    gated = d_second * mask * out_gate
+    d_tri = gated.astype(BF)
+    d_logit = (gated * tri_proj * (1.0 - out_gate)).astype(BF)
+    for r in range(step):
+        ds_ref[r] = d_second[:, r * residues : (r + 1) * residues]
+        dlogit_ref[r] = d_logit[:, r * residues : (r + 1) * residues]
+    gz_ref[...] += mm(tri_norm, d_tri, NT)
+    back = mm(wz_ref[...], d_tri)
+    prod = back * hat_t
+    gaint_ref[...] += sum(prod[:, r * residues : (r + 1) * residues] for r in range(step))
+    comb = norm_rows_back(back * gt_ref[...], hat_t, inv_t)
+    hidden = comb.shape[0] // 2
+    for r in range(step):
+        row = pl.program_id(0) * step + r
+        own = comb[:, r * residues : (r + 1) * residues]
+        tiles = fold_pair(own[:hidden], own[hidden:])
         for t in range(3):
             if stage:
                 put_tile(stage[1], t, row, rows, tiles[t])
@@ -318,8 +344,10 @@
 
 
 def third_kernel(
-    share, rows, sum_ref, acts_ref, ds_ref, dlogit_ref, mask_ref, mix_ref, right_ref, gx_ref, wt_ref, w_ref,
-    fg_ref, dmix_ref, dright_ref, gin_ref, gains_ref, gainx_ref, dproj_ref, acc_ref, *stage,
+    share, rows, sum_ref, acts_ref, ds_ref, dlogit_ref, mask_ref, mix_ref, right_ref, gx_ref,
+    wt_ref, w_ref, left_ref, outer_ref, carry_ref,
+    fg_ref, packed_ref, late_ref, gains_ref,
+    gainx_ref, dproj_ref, acc_ref, dmix_ref, dright_ref, gout_ref, *stage,
 ):
     @pl.when(pl.program_id(0) == 0)
     def _():
@@ -329,44 +357,73 @@
             unship(acts_ref, stage[0], 6, share, rows)
 
     hidden = wt_ref.shape[0] // 9
-    for r in range(sum_ref.shape[0]):
-        row = pl.program_id(0) * sum_ref.shape[0] + r
-        hat, inv = norm_rows(sum_ref[r])
-        norm = (hat * gx_ref[...]).astype(BF)
-        mask = mask_ref[r]
-        for pair in range(2):
+    step, _, residues = sum_ref.shape
+    joined = lambda ref: jnp.concatenate([ref[r] for r in range(step)], axis=1)
+    hat, inv = norm_rows(joined(sum_ref))
+    norm = (hat * gx_ref[...]).astype(BF)
+    mask = joined(mask_ref)
+    for pair in range(2):
+        unfolded = []
+        for r in range(step):
+            row = pl.program_id(0) * step + r
             tiles = range(3 * pair, 3 * pair + 3)
             if stage:
                 tiles = [get_tile(stage[0], t, row, rows, hidden) for t in tiles]
             else:
                 tiles = [acts_ref[r, t].astype(F32) for t in tiles]
-            both = unfold_pair(*tiles)
-            for side in range(2):
-                block = 2 * pair + side
-                value = mm(wt_ref[block * hidden : (block + 1) * hidden], norm)
-                gate = mm(wt_ref[(block + 4) * hidden : (block + 5) * hidden], norm)
-                sig = jax.nn.sigmoid(gate)
-                d_value = both[side] * mask * sig
-                d_gate = d_value * value * (1.0 - sig)
-                dproj_ref[block * hidden : (block + 1) * hidden] = d_value.astype(BF)
-                dproj_ref[(block + 4) * hidden : (block + 5) * hidden] = d_gate.astype(BF)
-        dproj_ref[8 * hidden :] = dlogit_ref[r]
-        d_proj = dproj_ref[...]
-        acc_ref[...] += mm(d_proj, norm, NT)
-        back = mm(w_ref[...], d_proj)
-        gainx_ref[...] += back * hat
-        first = ds_ref[r] + norm_rows_back(back * gx_ref[...], hat, inv)
-        fg_ref[r] = first
-        low = first.astype(BF)
-        dmix_ref[r] = mm(right_ref[...], low, NT).astype(BF)
-        right = mm(mix_ref[r], low)
+            unfolded.append(unfold_pair(*tiles))
+        for side in range(2):
+            block = 2 * pair + side
+            value = mm(wt_ref[block * hidden : (block + 1) * hidden], norm)
+            gate = mm(wt_ref[(block + 4) * hidden : (block + 5) * hidden], norm)
+            sig = jax.nn.sigmoid(gate)
+            d_value = jnp.concatenate([both[side] for both in unfolded], axis=1) * mask * sig
+            d_gate = d_value * value * (1.0 - sig)
+            dproj_ref[block * hidden : (block + 1) * hidden] = d_value.astype(BF)
+            dproj_ref[(block + 4) * hidden : (block + 5) * hidden] = d_gate.astype(BF)
+    dproj_ref[8 * hidden :] = joined(dlogit_ref)
+    d_proj = dproj_ref[...]
+    acc_ref[...] += mm(d_proj, norm, NT)
+    back = mm(w_ref[...], d_proj)
+    prod = back * hat
+    gainx_ref[...] += sum(prod[:, r * residues : (r + 1) * residues] for r in range(step))
+    first = joined(ds_ref) + norm_rows_back(back * gx_ref[...], hat, inv)
+    low = first.astype(BF)
+    for r in range(step):
+        own = slice(r * residues, (r + 1) * residues)
+        fg_ref[r] = first[:, own]
+        outer_dim = right_ref.shape[0]
+        row = pl.program_id(0) * step + r
+        mixed = pl.ds(pl.multiple_of(row * outer_dim, outer_dim), outer_dim)
+        dmix_ref[mixed, :] = mm(right_ref[...], low[:, own], NT).astype(BF).astype(F32)
+        right = mm(mix_ref[r], low[:, own])
         for half in range(dright_ref.shape[0]):
             dright_ref[half] += right[:, half * LANES : (half + 1) * LANES]
 
     @pl.when(pl.program_id(0) == pl.num_programs(0) - 1)
     def _():
-        gin_ref[...] = turn_blocks(acc_ref).astype(BF)
         gains_ref[...] = lane_sums(gainx_ref)
+        outer_dim, count = right_ref.shape[0], left_ref.shape[0]
+        d_left = jnp.zeros((count, LANES), F32)
+        below = jnp.zeros((LANES - outer_dim, LANES), BF)
+        for b in range(outer_dim):
+            mixed = dmix_ref[pl.ds(b, count, stride=outer_dim), :].astype(BF)
+            weight = outer_ref[pl.ds(b, outer_dim, stride=outer_dim), :].astype(BF)
+            d_left += mm(mixed, jnp.concatenate([weight, below], axis=0), NT)
+            gout_ref[pl.ds(b, outer_dim, stride=outer_dim), :] = mm(left_ref[...], mixed, TN)
+        at = 0
+        for half in range(dright_ref.shape[0]):
+            packed_ref[at : at + outer_dim] = dright_ref[half].astype(BF)
+            at = at + outer_dim
+        packed_ref[at : at + count] = d_left.astype(BF)
+        if carry_ref.shape[0] > 1:
+            start = packed_ref.shape[0] - carry_ref.shape[0]
+            packed_ref[start:] = carry_ref[...]
+        in_rows, outer_rows = acc_ref.shape[0], gout_ref.shape[0]
+        late_ref[:in_rows] = turn_blocks(acc_ref).astype(BF)
+        late_ref[in_rows : in_rows + outer_rows] = gout_ref[...].astype(BF)
+        spare = late_ref.shape[0] - in_rows - outer_rows
+        late_ref[in_rows + outer_rows :] = jnp.zeros((spare, LANES), BF)
 
 
 def last_kernel(xt_ref, fg_ref, ds_ref, gain_ref, w_ref, out_ref):
@@ -598,53 +655,75 @@
         ref[...] = value
 
 
-def adam_kernel(count, *refs):
+def adam_kernel(count, layout, *refs):
+    n_pair = 1 if layout else 3
+    ins = 4 * count + 9 + n_pair
+    outs, sums = refs[ins : ins + 3 * count + 9], refs[ins + 3 * count + 9 :]
     for k in range(count):
         master, first, second, grad = refs[4 * k : 4 * k + 4]
-        outs = refs[4 * count + 3 * k : 4 * count + 3 * k + 3]
-        adam_refs(master, first, second, grad[...], outs)
-
-
-def unpack(take, every, layout):
-    count, late_rows, half_rows, part_up, part_z, in_blocks, outer_rows, small_rows = layout
+        adam_refs(master, first, second, grad[...], outs[3 * k : 3 * k + 3])
+    olds, pair = refs[4 * count : 4 * count + 9], refs[4 * count + 9 : ins]
+
+    @pl.when(pl.program_id(0) == 0)
+    def _():
+        if layout:
+            start, part_up, part_z = layout
+            values = unpack_pair(pair[0][:, start:].astype(F32), part_up, part_z)
+        else:
+            values = [ref[...] for ref in pair]
+        for ref, value in zip(sums, values):
+            ref[...] = value
+
+    for k in range(3):
+        height = olds[3 * k].shape[0]
+        start = pl.multiple_of(pl.program_id(0) * height, height)
+        at = 3 * (count + k)
+        adam_refs(*olds[3 * k : 3 * k + 3], sums[k][pl.ds(start, height), :], outs[at : at + 3])
+
+
+def across(rows):
+    count = rows.shape[0] // LANES
+    return jnp.concatenate([rows[k * LANES : (k + 1) * LANES] for k in range(count)], axis=1)
+
+
+def unpack(take, layout):
+    count, late_rows, in_rows, outer_rows, small_rows = layout
     blocks, at = [], 0
     for _ in range(6):
         blocks.append(take(at, at + count).reshape(-1, LANES))
         at = at + count
     late = take(at, at + late_rows).reshape(-1, LANES)
     at = at + late_rows
-    pair = take(at, at + half_rows)
-    small = jnp.sum(take(at + half_rows, at + half_rows + small_rows), axis=0)
-    lower, upper = pair[: every // 2], pair[every // 2 :]
+    small = jnp.sum(take(at, at + small_rows), axis=0)
+    return blocks, (late[in_rows : in_rows + outer_rows], across(late[:in_rows])), small
+
+
+def unpack_pair(pair, part_up, part_z):
+    devices, half_rows, _ = pair.shape
+    lower, upper = pair[: devices // 2], pair[devices // 2 :]
     over = 2 * part_up - half_rows
     g_up = jnp.concatenate([lower[:, part_up:], upper[:, :over]], axis=1).reshape(-1, LANES)
-    across = lambda g: jnp.concatenate(
-        [g[k * LANES : (k + 1) * LANES] for k in range(g.shape[0] // LANES)], axis=1
-    )
-    g_in = across(late[: in_blocks * LANES])
-    g_outer = late[in_blocks * LANES : in_blocks * LANES + outer_rows]
     g_down = lower[:, :part_up].reshape(-1, LANES)
-    g_z = upper[:, over : over + part_z].reshape(-1, LANES)
-    return blocks, (g_outer, g_in, g_z, across(g_up), g_down), small
+    return upper[:, over : over + part_z].reshape(-1, LANES), across(g_up), g_down
 
 
 def final_kernel(
     layout, dgate_ref, norm_ref, both_ref, dmid_ref, gain_ref, w_ref, *refs
 ):
-    n_got = 1 if layout else 12
+    n_got = 1 if layout else 9
     got, refs = refs[:n_got], refs[n_got:]
-    olds, refs = refs[:18], refs[18:]
-    news, (dnode_ref, gaina_ref, small_ref, grad_ref), sums = refs[:18], refs[18:22], refs[22:]
+    olds, refs = refs[:9], refs[9:]
+    news, (dnode_ref, gaina_ref, small_ref, grad_ref), sums = refs[:9], refs[9:13], refs[13:]
     width = dmid_ref.shape[1]
 
     @pl.when(pl.program_id(0) == 0)
     def _():
         if layout:
             take = lambda start, stop: got[0][:, start:stop].astype(F32)
-            blocks, grads, small = unpack(take, got[0].shape[0], layout)
+            blocks, grads, small = unpack(take, layout)
         else:
             values = [ref[...] for ref in got]
-            blocks, grads, small = values[:6], values[6:11], values[11]
+            blocks, grads, small = values[:6], values[6:8], values[8]
         small_ref[...] = small
         for ref, grad in zip(sums[1:], grads):
             ref[...] = grad
@@ -660,7 +739,7 @@
             dnode_ref[rows] = dmid_ref[rows] + norm_lanes_back(back * gain_ref[...], hat, inv)
         gaina_ref[...] = total
 
-    for k in range(6):
+    for k in range(3):
         height = olds[3 * k].shape[0]
         start = pl.multiple_of(pl.program_id(0) * height, height)
         adam_refs(*olds[3 * k : 3 * k + 3], sums[k][pl.ds(start, height), :], news[3 * k : 3 * k + 3])
@@ -674,13 +753,21 @@
     return pl.BlockSpec((step,) + shape, lambda i: (i,) + (0,) * len(shape))
 
 
-def pair_call(kernel, steps, ins, outs, args, scratch=(), flops=0, moved=0):
+def pair_call(kernel, steps, ins, outs, args, scratch=(), flops=0, moved=0, free=(), near=()):
+    args = [
+        arg if at in free else pltpu.with_memory_space_constraint(arg, pltpu.HBM)
+        for at, arg in enumerate(args)
+    ]
+    shapes = [
+        shape if at in near else pltpu.HBM(shape.shape, shape.dtype)
+        for at, (_, shape) in enumerate(outs)
+    ]
     return pl.pallas_call(
         kernel,
         grid=(steps,),
         in_specs=ins,
         out_specs=[spec for spec, _ in outs],
-        out_shape=[shape for _, shape in outs],
+        out_shape=shapes,
         scratch_shapes=list(scratch),
         compiler_params=pltpu.CompilerParams(vmem_limit_bytes=48 * 1024 * 1024),
         cost_estimate=pl.CostEstimate(flops=flops, bytes_accessed=moved, transcendentals=0),
@@ -725,7 +812,7 @@
     bias_wt, in_wt, z_wt, up_wt, down_wt = bias_wb.T, in_wb.T, z_wb.T, up_wb.T, down_wb.T
 
     direct = count % 16 == 0
-    step = 2 if count % 2 == 0 else 1
+    step = next(size for size in (4, 2, 1) if count % size == 0)
     steps = count // step
     pairs = count * residues
 
@@ -737,19 +824,20 @@
         [(by_row(step, (width_z, residues)), shape_of((count, width_z, residues), BF)),
          (by_row(step, (width_z, residues)), shape_of((count, width_z, residues), BF)),
          (by_row(step, (heads, residues)), shape_of((count, heads, residues), F32))],
-        [pair_x, column(gain_b), bias_wt],
+        [pair_x, column(gain_b), bias_wt], free=(0, 1, 2), near=(2,),
         flops=2 * pairs * width_z * heads, moved=4 * pairs * width_z,
     )
 
     def own_rows(values):
         return lax.dynamic_slice_in_dim(values, crop_index * residues + first_row, count, 0)
 
-    def single(kernel, outs, args, scratch=(), flops=0):
+    def single(kernel, outs, args, scratch=(), flops=0, far=(), apart=False):
         moved = sum(arg.size * 4 for arg in args)
         return pair_call(
             kernel, 1, [whole(arg.shape) for arg in args],
             [(whole(shape), shape_of(shape, kind)) for shape, kind in outs],
-            args, scratch, flops, moved,
+            args, scratch, flops, moved, (0,) if apart else range(len(args)),
+            [at for at in range(len(outs)) if at not in far],
         )
 
     columns = [column(gain) for gain in (gain_x, gain_t, gain_h)]
@@ -763,7 +851,7 @@
          ((count * heads, residues), F32), ((count * heads, residues), BF),
          ((count, width_s), BF)],
         [node_both, node_feats[:, 0], line(gain_a), att_wb, pair_bias, mask],
-        flops=8 * nodes * width_s * width_s,
+        flops=8 * nodes * width_s * width_s, far=(0, 1, 2, 3),
     )
     weights_cut = weights_low.reshape(count, heads, row_devices, count).transpose(2, 0, 1, 3)
     if direct:
@@ -776,7 +864,7 @@
         [(square, F32), (square, F32), ((nodes, 2 * outer_dim), BF), ((outer_dim, residues), BF)],
         [node_both, gated, line(gain_n), line(gain_s), attout_wb, nodeup_wb, nodedown_wb, node_wb,
          node_wb[:, outer_dim:].T],
-        scratch=[pltpu.VMEM(square, BF)], flops=18 * nodes * width_s * width_s,
+        scratch=[pltpu.VMEM(square, BF)], flops=18 * nodes * width_s * width_s, far=(0, 1),
     )
     node_out = own_rows(node_next).astype(BF)[:, None]
     left_vec = own_rows(node_proj[:, :outer_dim])
@@ -834,6 +922,7 @@
         flops=16 * pairs * width_z * hidden, moved=12 * pairs * width_z,
     )
 
+    tri_steps = lambda channels: channels // 2 if direct and channels % 2 == 0 else channels
     chain_specs = [whole((residues, 1)), whole((1, residues))]
     product = 2 * share * residues**3
     ready = [in_wb, z_wb, up_wb, down_wb, z_wt, up_wt, down_wt] + columns
@@ -841,8 +930,8 @@
     weights_col = acts[:, 6 * share * count :] if direct else swap(weights_cut)
     weights_col = weights_col.reshape(residues, heads * count)
     (tri,) = pair_call(
-        functools.partial(tri_kernel, dims), share, chain_specs + [tri_block(6, extra)[0]],
-        [tri_block(3)], [chain_col, chain_row, acts],
+        functools.partial(tri_kernel, dims), tri_steps(share), chain_specs + [tri_block(6, extra)[0]],
+        [tri_block(3)], [chain_col, chain_row, acts], free=(2,),
         flops=2 * product, moved=share * residues * 9 * 256,
     )
     tri_rows = to_rows(tri)
@@ -876,7 +965,7 @@
          (slab, shape_of((count, width_z, residues), BF)),
          sent_block(3, carried)]
         + [(whole(s), shape_of(s, F32)) for s in acc_shapes],
-        [arg for _, arg in second_args],
+        [arg for _, arg in second_args], free=(1,),
         scratch=[pltpu.VMEM((2 * hidden, residues), F32), pltpu.VMEM((width_z, residues), F32)]
         + stage(3) + stage(3),
         flops=12 * pairs * width_z * expand, moved=20 * pairs * width_z,
@@ -896,44 +985,41 @@
     theirs = lax.ppermute(jnp.where(low_crop, upper, lower), "crop", [(0, 1), (1, 0)])
     pair_own = (jnp.where(low_crop, lower, upper) + theirs).astype(BF)
     (dacts,) = pair_call(
-        functools.partial(tri_back_kernel, dims), share,
+        functools.partial(tri_back_kernel, dims), tri_steps(share),
         chain_specs + [tri_block(6, extra)[0], tri_block(3, carried)[0]],
-        [tri_block(6)], [chain_col, chain_row, acts, dtri],
+        [tri_block(6)], [chain_col, chain_row, acts, dtri], free=(2,),
         flops=4 * product, moved=share * residues * 15 * 256,
     )
     dacts_rows = after(to_rows(dacts), pair_own)
 
-    first_grad, d_mix, d_right, g_in_blocks, gains_x = pair_call(
+    right_rows = residues // LANES * outer_dim
+    left_rows = -(-count // 16) * 16
+    carry = pair_own if direct else jnp.zeros((1, LANES), BF)
+    packed_rows = right_rows + left_rows + (half_rows if direct else 0)
+    in_rows, outer_rows = in_wt.shape[0], w_outer.shape[0]
+    late_rows = -(-(in_rows + outer_rows) // (every * 16)) * every * 16
+    first_grad, packed, late, gains_x = pair_call(
         functools.partial(third_kernel, share, count), steps,
         [slab, sent_block(6)[0], slab, slab, by_row(step, (1, residues)),
          by_row(step, (outer_dim, width_z)), whole((outer_dim, residues)), whole((width_z, 1)),
-         whole(in_wt.shape), whole(in_wb.shape)],
+         whole(in_wt.shape), whole(in_wb.shape), whole(left_vec.shape), whole(w_outer.shape),
+         whole(carry.shape)],
         [(slab, shape_of((count, width_z, residues), F32)),
-         (by_row(step, (outer_dim, width_z)), shape_of((count, outer_dim, width_z), BF)),
-         (whole((residues // LANES, outer_dim, LANES)),
-          shape_of((residues // LANES, outer_dim, LANES), F32)),
-         (whole(in_wt.shape), shape_of(in_wt.shape, BF)),
+         (whole((packed_rows, LANES)), shape_of((packed_rows, LANES), BF)),
+         (whole((late_rows, LANES)), shape_of((late_rows, LANES), BF)),
          (whole((width_z // LANES, LANES)), shape_of((width_z // LANES, LANES), F32))],
-        [first_sum, dacts_rows, d_second, d_logit, mask, outer_mix, right_t, column(gain_x),
-         in_wt, in_wb],
-        scratch=[pltpu.VMEM((width_z, residues), F32), pltpu.VMEM((9 * hidden, residues), BF),
-                 pltpu.VMEM(in_wt.shape, F32)] + stage(6),
+        [first_sum, dacts_rows, d_second, d_logit, mask, outer_mix, right_t, columns[0],
+         in_wt, in_wb, left_vec, w_outer, carry],
+        free=(1,), near=(1, 2),
+        scratch=[pltpu.VMEM((width_z, residues), F32), pltpu.VMEM((9 * hidden, step * residues), BF),
+                 pltpu.VMEM(in_wt.shape, F32), pltpu.VMEM((count * outer_dim, LANES), F32),
+                 pltpu.VMEM((residues // LANES, outer_dim, LANES), F32),
+                 pltpu.VMEM(w_outer.shape, F32)] + stage(6),
         flops=54 * pairs * width_z * hidden, moved=20 * pairs * width_z,
     )
-
-    mix_flat = d_mix.reshape(count, outer_dim * width_z)
-    d_left = mm(mix_flat, outer_wb, NT)
-    right_rows = d_right.shape[0] * outer_dim
-    left_rows = jnp.pad(d_left, ((0, 0), (0, LANES - outer_dim)))
-    packed = jnp.concatenate([d_right.reshape(right_rows, LANES), left_rows]).astype(BF)
-
-    g_outer = mm(left_vec, mix_flat, TN).reshape(outer_dim * outer_dim, width_z).astype(BF)
-    late_rows = g_in_blocks.shape[0] + g_outer.shape[0]
-    spare = jnp.zeros((-late_rows % (every * 16), LANES), BF)
-    late = jnp.concatenate([g_in_blocks, g_outer, spare]).reshape(every, -1, LANES)
     got = gather_all(packed, row_devices, late)
-    late_own = scatter_sum(after(late, got))
-    left_all = left_rows
+    late_own = scatter_sum(after(late, got).reshape(every, -1, LANES))
+    left_all = left_vec
     if not direct:
         left_all = got[:, right_rows : right_rows + count].reshape(nodes, LANES)
 
@@ -949,7 +1035,7 @@
          line(gain_n), line(gain_s), attout_wb, nodeup_wb, nodedown_wb, wide_node],
         scratch=[pltpu.VMEM((nodes, LANES), BF), low_square, pltpu.VMEM(tall, BF), low_square,
                  low_square, pltpu.VMEM(tall, BF), low_square],
-        flops=50 * nodes * width_s * width_s,
+        flops=50 * nodes * width_s * width_s, apart=True,
     )
 
     values_own = lax.dynamic_slice(qkv_crop, (first_row, 2 * width_s), (count, width_s))
@@ -964,11 +1050,8 @@
 
     small = jnp.concatenate([g_bias_t, gains_x, gains_th]).astype(BF)
     small = jnp.pad(small, ((0, -small.shape[0] % 16), (0, 0)))
-    pieces = [qkv_grad.reshape(-1, LANES), late_own, pair_own, small]
-    layout = (
-        count, late_own.shape[0], half_rows, part_up, part_z,
-        in_wb.shape[1] // LANES, g_outer.shape[0], small.shape[0],
-    )
+    pieces = [qkv_grad.reshape(-1, LANES), late_own, small]
+    layout = (count, late_own.shape[0], in_rows, outer_rows, small.shape[0])
 
     (pair_grad,) = pair_call(
         last_kernel, steps,
@@ -978,7 +1061,7 @@
         flops=4 * pairs * width_z * heads, moved=10 * pairs * width_z,
     )
 
-    parts = 8
+    parts = 2
     split = lambda k: pl.BlockSpec((olds[k].shape[0] // parts, olds[k].shape[1]), lambda i: (i, 0))
     updated = {}
 
@@ -990,18 +1073,36 @@
         specs += [spec] * 4
         args += [turned(k, old[k]) for old in (masters, firsts, seconds)] + [grad]
         outs += [(spec, shape_of(grad.shape, F32))] * 3
+    pair_keys = (8, 9, 10)
+    for k in pair_keys:
+        height, width = masters[k].shape
+        spec = pl.BlockSpec((height // parts, width), lambda i: (i, 0))
+        specs += [spec] * 3
+        args += [masters[k], firsts[k], seconds[k]]
+        outs += [(spec, shape_of((height, width), F32))] * 3
+    if direct:
+        pair_got, pair_layout = [got], (right_rows + left_rows, part_up, part_z)
+    else:
+        pair_all = gather_all(pair_own, row_devices)
+        pair_got, pair_layout = list(unpack_pair(pair_all.astype(F32), part_up, part_z)), None
+    specs += [whole(arg.shape) for arg in pair_got]
+    args += pair_got
     found = pair_call(
-        functools.partial(adam_kernel, len(early)), parts, specs, outs, args,
+        functools.partial(adam_kernel, len(early), pair_layout), parts, specs, outs, args,
+        scratch=[pltpu.VMEM(masters[k].shape, F32) for k in pair_keys],
         moved=sum(7 * arg.size for arg in args),
     )
-    last = gather_all(jnp.concatenate(pieces), row_devices, (pair_grad, found[0]))
+    beside = (pair_grad, found[0], node_out)
+    last = gather_all(jnp.concatenate(pieces), row_devices, beside)
     for at, k in enumerate(early):
         updated[k] = [turned(k, value) for value in found[3 * at : 3 * at + 3]]
-
-    late_keys = (0, 6, 7, 8, 9, 10)
+    for at, k in enumerate(pair_keys, len(early)):
+        updated[k] = found[3 * at : 3 * at + 3]
+
+    late_keys = (0, 6, 7)
     got_last = [last]
     if not direct:
-        blocks, sums, small = unpack(lambda a, b: last[:, a:b].astype(F32), every, layout)
+        blocks, sums, small = unpack(lambda a, b: last[:, a:b].astype(F32), layout)
         got_last = blocks + list(sums) + [small]
     fixed = [d_gate, att_norm, node_both, grad_mid, line(gain_a), att_wb] + got_last
     olds, specs = [], [whole(arg.shape) for arg in fixed]
@@ -1019,7 +1120,7 @@
     )
     for at, k in enumerate(late_keys):
         updated[k] = found[3 * at : 3 * at + 3]
-    d_nodes, gain_a_grad, small = found[18:]
+    d_nodes, gain_a_grad, small = found[9:]
     node_grad = own_rows(d_nodes)[:, None]
 
     g_bias = small[:heads].T

time: 471 us -> 437 us (0.928)
  blocking collectives: 54.3 us -> 85.4 us
  local copies, waits for them, and re-layouts: 53.6 us -> 26 us
  starting transfers between devices: 64.1 us -> 45.1 us
  Pallas kernels: 106 us -> 98.3 us
    all_to_all x0 -> x1, blocking collectives: none -> 31.1 us  [gather_all(): lax.all_to_all(spread, BOTH, split_axis=0, concat_axis=0, tiled=True, axi...]
    unnamed x241 -> x103, local copies, waits for them, and re-layouts: 32.7 us -> 5.64 us
    all_to_all x4 -> x3, starting transfers between devices: 35.5 us -> 16.3 us  [gather_all(): lax.all_to_all(spread, BOTH, split_axis=0, concat_axis=0, tiled=True, axi...]
    pallas_call x13, Pallas kernels: 106 us -> 98.3 us  [pair_call(): pl.pallas_call(kernel, grid=(steps,), in_specs=ins, out_specs=[spec for s...]
    all_to_all x4 -> x3, waiting for transfers between devices: 17.2 us -> 13.1 us  [gather_all(): lax.all_to_all(spread, BOTH, split_axis=0, concat_axis=0, tiled=True, axi...]
  transfers between devices with their start and end apart: 13 -> 12, of which waited for: 12 -> 11; matrix products, arithmetic and copies ran while one was open for 7% -> 7% of each run, Pallas kernels for 5% -> 5%
where the time goes in v3:
time: 437 us; the launch traced here: 435 us
  waiting for transfers between devices  158 us (36%)
  Pallas kernels  98.3 us (22%)
  blocking collectives  85.4 us (20%)
  starting transfers between devices  45.1 us (10%)
  local copies, waits for them, and re-layouts  26 us (6%)
  other arithmetic  20.9 us (5%)
    all_to_all x3, waiting for transfers between devices, swap(): return lax.all_to_all(block, 'row', split_axis=0, concat_axis=0, tiled=True)  131 us
    pallas_call x13, Pallas kernels, pair_call(): pl.pallas_call(kernel, grid=(steps,), in_specs=ins, out_specs=[spec for s...  98.3 us
    all_to_all x1, blocking collectives, swap(): return lax.all_to_all(block, 'row', split_axis=0, concat_axis=0, tiled=True)  54.3 us
    all_to_all x1, blocking collectives, gather_all(): lax.all_to_all(spread, BOTH, split_axis=0, concat_axis=0, tiled=True, axi...  31.1 us
    all_to_all x3, starting transfers between devices, swap(): return lax.all_to_all(block, 'row', split_axis=0, concat_axis=0, tiled=True)  24.3 us
    all_to_all x3, starting transfers between devices, gather_all(): lax.all_to_all(spread, BOTH, split_axis=0, concat_axis=0, tiled=True, axi...  16.3 us
    all_to_all x3, waiting for transfers between devices, gather_all(): lax.all_to_all(spread, BOTH, split_axis=0, concat_axis=0, tiled=True, axi...  13.1 us
  transfers between devices with their start and end apart: 12, of which 11 were waited for; matrix products, arithmetic and copies ran while one was open for 7% of the time, Pallas kernels for 5%

profile of v3, /device:TPU:0, one launch (start us, length us, event | category | flops | bytes accessed | tf_op | source)
XLA Modules:
  0.0 435.4 jit_solution(10738775511498940521)
XLA Ops:
  2.2 8.4 %all-to-all-start = ((bf16[16,16,512]{2,1,0:T(8,128)(2,1)}), bf16[16,16,512]{2,1,0:T(8,128)(2,1)}, u32[]{:S(2)}, u32[]{:S(2)}) async-start(bf16[16,16,512]{2,1,0:T(8,128)(2,1)} %broadcast_in_dim.16), calls=%async_computation | async-start | bytes 524288 | tf_op jit(solution)/shard_map/all_to_all | solution.py:42
  26.2 4.3 all-to-all-start.1
  33.0 5.6 %all-to-all-done.1 = bf16[16,16,256]{2,1,0:T(8,128)(2,1)S(1)} async-done(((bf16[16,16,256]{2,1,0:T(8,128)(2,1)}), bf16[16,16,256]{2,1,0:T(8,128)(2,1)S(1)}, u32[]{:S(2)}, u32[]{:S(2)}) %all-to-all-start.1) | async-done | bytes 131104 | tf_op jit(solution)/shard_map/all_to_all | solution.py:42
  40.1 4.6 %shard_map.701 = (f32[512,256]{1,0:T(8,128)}, f32[512,256]{1,0:T(8,128)}, bf16[512,64]{1,0:T(8,128)(2,1)S(1)}, bf16[32,256]{1,0:T(8,128)(2,1)S(1)}) custom-call(bf16[512,512]{1,0:T(8,128)(2,1)S(1)} %bitcast.103, bf16[512,256]{1,0:T(8,128)(2,1)S(1)} %bitcast.111, f32[1,256]{1,0:T(1,128)S(1)} %bitcast.123, f32[1,256]{1,0:T(1,128)S(1)} %bitcast.121, ...), custom_call_target="tpu_custom_call" | custom-call | flops 603979776 | bytes 4032512 | tf_op jit(solution)/shard_map/pallas_call | solution.py:765
  45.6 9.6 %shard_map.702 = (f32[16,128,256]{2,1,0:T(8,128)}, bf16[16,784,128]{2,1,0:T(8,128)(2,1)}) custom-call(bf16[16,128,256]{2,1,0:T(8,128)(2,1)} %get-tuple-element.117.xt_ref, bf16[16,32,128]{2,1,0:T(8,128)(2,1)} %bitcast.130, bf16[32,256]{1,0:T(8,128)(2,1)} %copy-done.25, f32[16,1,256]{2,1,0:T(1,128)} %copy-done.20, f32[128,1]{1,0:T(8,128)} %copy.109.gain_ref.gx_ref, ...), custom_call_target="tpu_custom_call" | custom-call | flops 1073741824 | bytes 6291456 | tf_op jit(solution)/shard_map/pallas_call | solution.py:765
  55.2 3.9 all-to-all-start.2
  68.5 51.0 %all-to-all-done.2.acts_ref = bf16[16,784,128]{2,1,0:T(8,128)(2,1)S(1)} async-done(((bf16[16,784,128]{2,1,0:T(8,128)(2,1)}), bf16[16,784,128]{2,1,0:T(8,128)(2,1)S(1)}, u32[]{:S(2)}, u32[]{:S(2)}) %all-to-all-start.2) | async-done | bytes 3211296 | tf_op jit(solution)/shard_map/all_to_all | solution.py:886
  119.6 4.5 %shard_map.703 = bf16[16,384,128]{2,1,0:T(8,128)(2,1)} custom-call(s32[256,1]{1,0:T(8,128)} %copy.111.col_ref, s32[1,256]{1,0:T(1,128)} %row_ref.3, bf16[16,784,128]{2,1,0:T(8,128)(2,1)S(1)} %all-to-all-done.2.acts_ref), custom_call_target="tpu_custom_call" | custom-call | flops 536870912 | bytes 4718592 | tf_op jit(solution)/shard_map/pallas_call | solution.py:765
  124.1 15.9 %all-to-all-start.3 = ((bf16[16,384,128]{2,1,0:T(8,128)(2,1)}), bf16[16,384,128]{2,1,0:T(8,128)(2,1)}, u32[]{:S(2)}, u32[]{:S(2)}) async-start(bf16[16,384,128]{2,1,0:T(8,128)(2,1)} %shard_map.703), calls=%async_computation.3 | async-start | bytes 3145728 | tf_op jit(solution)/shard_map/all_to_all | solution.py:886
  145.4 26.6 %all-to-all-done.3.tri_ref = bf16[16,384,128]{2,1,0:T(8,128)(2,1)} async-done(((bf16[16,384,128]{2,1,0:T(8,128)(2,1)}), bf16[16,384,128]{2,1,0:T(8,128)(2,1)}, u32[]{:S(2)}, u32[]{:S(2)}) %all-to-all-start.3) | async-done | bytes 1572896 | tf_op jit(solution)/shard_map/all_to_all | solution.py:886
  172.0 22.6 %shard_map.704 = (bf16[16,256,128]{2,1,0:T(8,128)(2,1)}, f32[16,128,256]{2,1,0:T(8,128)}, bf16[16,128,256]{2,1,0:T(8,128)(2,1)}, bf16[16,480,128]{2,1,0:T(8,128)...) custom-call(f32[16,128,256]{2,1,0:T(8,128)} %get-tuple-element.125.sum_ref, ...), custom_call_target="tpu_custom_call" | custom-call | flops 3221225472 | bytes 10485760 | tf_op jit(solution)/shard_map/pallas_call | solution.py:765
  194.7 54.3 %all_to_all.45.grad_ref = bf16[16,480,128]{2,1,0:T(8,128)(2,1)} all-to-all(bf16[16,480,128]{2,1,0:T(8,128)(2,1)} %get-tuple-element.130), channel_id=1, replica_groups=mesh['crop'=2,'row'=16] {'row'}, dimensions={0} | all-to-all | bytes 3932160 | tf_op jit(solution)/shard_map/all_to_all | solution.py:886
  248.9 6.7 %shard_map.705 = bf16[16,768,128]{2,1,0:T(8,128)(2,1)} custom-call(s32[256,1]{1,0:T(8,128)} %copy.111.col_ref, s32[1,256]{1,0:T(1,128)} %row_ref.3, bf16[16,784,128]{2,1,0:T(8,128)(2,1)S(1)} %all-to-all-done.2.acts_ref, bf16[16,480,128]{2,1,0:T(8,128)(2,1)} %all_to_all.45.grad_ref), custom_call_target="tpu_custom_call" | custom-call | flops 1073741824 | bytes 7864320 | tf_op jit(solution)/shard_map/pallas_call | solution.py:765
  255.6 4.6 %all-to-all-start.5 = ((bf16[16,768,128]{2,1,0:T(8,128)(2,1)}), bf16[16,768,128]{2,1,0:T(8,128)(2,1)}, u32[]{:S(2)}, u32[]{:S(2)}) async-start(bf16[16,768,128]{2,1,0:T(8,128)(2,1)} %shard_map.705), calls=%async_computation.5 | async-start | bytes 6291456 | tf_op jit(solution)/shard_map/all_to_all | solution.py:886
  265.8 53.8 %all-to-all-done.5.acts_ref = bf16[16,768,128]{2,1,0:T(8,128)(2,1)} async-done(((bf16[16,768,128]{2,1,0:T(8,128)(2,1)}), bf16[16,768,128]{2,1,0:T(8,128)(2,1)}, u32[]{:S(2)}, u32[]{:S(2)}) %all-to-all-start.5) | async-done | bytes 3145760 | tf_op jit(solution)/shard_map/all_to_all | solution.py:886
  319.6 16.1 %shard_map.706 = (f32[16,128,256]{2,1,0:T(8,128)}, bf16[128,128]{1,0:T(8,128)(2,1)S(1)}, bf16[2560,128]{1,0:T(8,128)(2,1)S(1)}, f32[1,128]{1,0:T(1,128)}) custom-call(f32[16,128,256]{2,1,0:T(8,128)} %get-tuple-element.125.sum_ref, bf16[16,768,128]{2,1,0:T(8,128)(2,1)} %all-to-all-done.5.acts_ref, f32[16,128,256]{2,1,0:T(8,128)} %get-tuple-element.132.ds_ref, ...), custom_call_target="tpu_custom_call" | custom-call | flops 3623878656 | bytes 10485760 | tf_op jit(solution)/shard_map/pallas_call | solution.py:765
  335.8 31.1 %all_to_all.46 = bf16[16,128,128]{2,1,0:T(8,128)(2,1)S(1)} all-to-all(bf16[16,128,128]{2,1,0:T(8,128)(2,1)S(1)} %broadcast_in_dim.20), channel_id=1, replica_groups={{0,2,4,6,8,10,12,14,16,18,20,22,24,26,28,30},{1,3,5,7,9,11,13,15,17,19,..., dimensions={0} | all-to-all | bytes 1048576 | tf_op jit(solution)/shard_map/all_to_all | solution.py:42
  376.2 7.1 %shard_map.707 = (f32[64,256]{1,0:T(8,128)S(1)}, f32[1024,256]{1,0:T(8,128)S(1)}, f32[256,1024]{1,0:T(8,128)S(1)}, f32[256,256]{1,0:T(8,128)S(1)}, f32[1,256]{1,...) custom-call(bf16[32,128,128]{2,1,0:T(8,128)(2,1)S(1)} %bitcast.107, ...), custom_call_target="tpu_custom_call" | custom-call | flops 1677721600 | bytes 7737344 | tf_op jit(solution)/shard_map/pallas_call | solution.py:765
  386.9 5.2 %all-to-all-done.7 = bf16[32,80,128]{2,1,0:T(8,128)(2,1)} async-done(((bf16[32,80,128]{2,1,0:T(8,128)(2,1)}), bf16[32,80,128]{2,1,0:T(8,128)(2,1)}, u32[]{:S(2)}, u32[]{:S(2)}) %all-to-all-start.7) | async-done | bytes 655392 | tf_op jit(solution)/shard_map/all_to_all | solution.py:53
  394.3 3.6 all-to-all-start.8
  400.0 8.4 %shard_map.710 = (f32[256,256]{1,0:T(8,128)}, f32[256,256]{1,0:T(8,128)}, f32[256,256]{1,0:T(8,128)}, f32[256,1024]{1,0:T(8,128)}, f32[256,1024]{1,0:T(8,128)}, ...) custom-call(f32[256,256]{1,0:T(8,128)} %refs_0_.1, ...), custom_call_target="tpu_custom_call" | custom-call | bytes 24084480 | tf_op jit(solution)/shard_map/pallas_call | solution.py:765
  408.4 5.1 %shard_map.709 = f32[16,256,128]{2,1,0:T(8,128)} custom-call(bf16[16,128,256]{2,1,0:T(8,128)(2,1)} %get-tuple-element.117.xt_ref, f32[16,128,256]{2,1,0:T(8,128)} %get-tuple-element.134.fg_ref, bf16[16,8,256]{2,1,0:T(8,128)(2,1)} %bitcast.113, f32[128,1]{1,0:T(8,128)} %copy-done.8, bf16[128,8]{1,0:T(8,128)(2,1)} %copy.124.w_ref), custom_call_target="tpu_custom_call" | custom-call | flops 16777216 | bytes 5242880 | tf_op jit(solution)/shard_map/pallas_call | solution.py:765
  413.4 4.9 %all-to-all-done.8 = bf16[16,192,128]{2,1,0:T(8,128)(2,1)S(1)} async-done(((bf16[16,192,128]{2,1,0:T(8,128)(2,1)}), bf16[16,192,128]{2,1,0:T(8,128)(2,1)S(1)}, u32[]{:S(2)}, u32[]{:S(2)}) %all-to-all-start.8) | async-done | bytes 786464 | tf_op jit(solution)/shard_map/all_to_all | solution.py:42
  422.0 8.6 %shard_map.711 = (f32[256,1024]{1,0:T(8,128)}, f32[256,1024]{1,0:T(8,128)}, f32[256,1024]{1,0:T(8,128)}, f32[1024,128]{1,0:T(8,128)}, f32[1024,128]{1,0:T(8,128)...) custom-call(bf16[512,256]{1,0:T(8,128)(2,1)} %copy-done.15, ...), custom_call_target="tpu_custom_call" | custom-call | flops 536870912 | bytes 11354112 | tf_op jit(solution)/shard_map/pallas_call | solution.py:765
  (192 shorter events, 67.5 us)
Async XLA Ops:
  2.2 18.3 %all-to-all-start = ((bf16[16,16,512]{2,1,0:T(8,128)(2,1)}), bf16[16,16,512]{2,1,0:T(8,128)(2,1)}, u32[]{:S(2)}, u32[]{:S(2)}) async-start(bf16[16,16,512]{2,1,0:T(8,128)(2,1)} %broadcast_in_dim.16), calls=%async_computation | async-start | bytes 524288 | tf_op jit(solution)/shard_map/all_to_all | solution.py:42
  13.1 26.9 %copy-start.16 = (bf16[256,256]{1,0:T(8,128)(2,1)}, bf16[256,256]{1,0:T(8,128)(2,1)S(1)}, u32[]{:S(2)}) copy-start(bf16[256,256]{1,0:T(8,128)(2,1)S(1)} %convert_element_type.67.wo_ref) | copy-start | bytes 393220
  13.5 26.6 %copy-start.9 = (bf16[256,1024]{1,0:T(8,128)(2,1)}, bf16[256,1024]{1,0:T(8,128)(2,1)S(1)}, u32[]{:S(2)}) copy-start(bf16[256,1024]{1,0:T(8,128)(2,1)S(1)} %convert_element_type.68.wu_ref) | copy-start | bytes 1572868
  15.2 24.8 %copy-start.10 = (bf16[1024,256]{1,0:T(8,128)(2,1)}, bf16[1024,256]{1,0:T(8,128)(2,1)S(1)}, u32[]{:S(2)}) copy-start(bf16[1024,256]{1,0:T(8,128)(2,1)S(1)} %convert_element_type.69.wd_ref) | copy-start | bytes 1572868
  20.5 2.3 collective-permute-start
  22.8 17.3 %copy-start.23 = (f32[256]{0:T(256)}, f32[256]{0:T(256)S(1)}, u32[]{:S(2)}) copy-start(f32[256]{0:T(256)S(1)} %get-tuple-element.293) | copy-start | bytes 3076
  22.8 17.3 %copy-start.24 = (f32[256]{0:T(256)}, f32[256]{0:T(256)S(1)}, u32[]{:S(2)}) copy-start(f32[256]{0:T(256)S(1)} %get-tuple-element.294) | copy-start | bytes 3076
  23.9 16.2 %copy-start.1 = (bf16[16,2,16,512]{3,2,1,0:T(8,128)(2,1)}, bf16[16,2,16,512]{3,2,1,0:T(8,128)(2,1)S(1)}, u32[]{:S(2)}) copy-start(bf16[16,2,16,512]{3,2,1,0:T(8,128)(2,1)S(1)} %pad_maximum_fusion.2) | copy-start | bytes 1572868
  26.2 12.4 %all-to-all-start.1 = ((bf16[16,16,256]{2,1,0:T(8,128)(2,1)}), bf16[16,16,256]{2,1,0:T(8,128)(2,1)S(1)}, u32[]{:S(2)}, u32[]{:S(2)}) async-start(bf16[16,16,256]{2,1,0:T(8,128)(2,1)} %broadcast_in_dim.17), calls=%async_computation.1 | async-start | bytes 262144 | tf_op jit(solution)/shard_map/all_to_all | solution.py:42
  38.6 1.3 collective-permute-start.1
  55.2 64.3 %all-to-all-start.2 = ((bf16[16,784,128]{2,1,0:T(8,128)(2,1)}), bf16[16,784,128]{2,1,0:T(8,128)(2,1)S(1)}, u32[]{:S(2)}, u32[]{:S(2)}) async-start(bf16[16,784,128]{2,1,0:T(8,128)(2,1)} %get-tuple-element.126), calls=%async_computation.2 | async-start | bytes 6422528 | tf_op jit(solution)/shard_map/all_to_all | solution.py:886
  124.1 15.9 %copy-start.35 = (bf16[128,256]{0,1:T(8,128)(2,1)S(1)}, bf16[128,256]{0,1:T(8,128)(2,1)}, u32[]{:S(2)}) copy-start(bf16[128,256]{0,1:T(8,128)(2,1)} %convert_bitcast_fusion.3) | copy-start | bytes 196612
  124.1 16.7 %copy-start.46 = (f32[128,1]{0,1:T(1,128)S(1)}, f32[128,1]{0,1:T(1,128)}, u32[]{:S(2)}) copy-start(f32[128,1]{0,1:T(1,128)} %get-tuple-element.289) | copy-start | bytes 1540
  124.1 19.1 %copy-start.33 = (bf16[512,128]{0,1:T(8,128)(2,1)S(1)}, bf16[512,128]{0,1:T(8,128)(2,1)}, u32[]{:S(2)}) copy-start(bf16[512,128]{0,1:T(8,128)(2,1)} %convert_bitcast_fusion.2) | copy-start | bytes 393220
  124.1 19.8 %copy-start.43 = (f32[256]{0:T(256)S(1)}, f32[256]{0:T(256)}, u32[]{:S(2)}) copy-start(f32[256]{0:T(256)} %get-tuple-element.292) | copy-start | bytes 3076
  124.1 20.6 %slice-start = ((bf16[1152,128]{0,1:T(8,128)(2,1)}), bf16[128,128]{0,1:T(8,128)(2,1)S(1)}, s32[]{:S(2)}) async-start(bf16[1152,128]{0,1:T(8,128)(2,1)} %copy-done.32), calls=%async_computation.9 | async-start | bytes 65536 | tf_op jit(solution)/shard_map/slice | solution.py:950
  124.1 47.9 %all-to-all-start.3 = ((bf16[16,384,128]{2,1,0:T(8,128)(2,1)}), bf16[16,384,128]{2,1,0:T(8,128)(2,1)}, u32[]{:S(2)}, u32[]{:S(2)}) async-start(bf16[16,384,128]{2,1,0:T(8,128)(2,1)} %shard_map.703), calls=%async_computation.3 | async-start | bytes 3145728 | tf_op jit(solution)/shard_map/all_to_all | solution.py:886
  255.6 64.0 %all-to-all-start.5 = ((bf16[16,768,128]{2,1,0:T(8,128)(2,1)}), bf16[16,768,128]{2,1,0:T(8,128)(2,1)}, u32[]{:S(2)}, u32[]{:S(2)}) async-start(bf16[16,768,128]{2,1,0:T(8,128)(2,1)} %shard_map.705), calls=%async_computation.5 | async-start | bytes 6291456 | tf_op jit(solution)/shard_map/all_to_all | solution.py:886
  261.3 3.9 collective-permute-start.2
  335.7 34.3 %copy-start.7 = (bf16[2560,128]{1,0:T(8,128)(2,1)}, bf16[2560,128]{1,0:T(8,128)(2,1)S(1)}, u32[]{:S(2)}) copy-start(bf16[2560,128]{1,0:T(8,128)(2,1)S(1)} %get-tuple-element.150) | copy-start | bytes 1966084
  366.9 1.9 collective-permute-start.3
  370.0 22.0 %all-to-all-start.7 = ((bf16[32,80,128]{2,1,0:T(8,128)(2,1)}), bf16[32,80,128]{2,1,0:T(8,128)(2,1)}, u32[]{:S(2)}, u32[]{:S(2)}) async-start(bf16[32,80,128]{2,1,0:T(8,128)(2,1)} %bitcast.109), calls=%async_computation.7 | async-start | bytes 1310720 | tf_op jit(solution)/shard_map/all_to_all | solution.py:53
  394.3 24.0 %all-to-all-start.8 = ((bf16[16,192,128]{2,1,0:T(8,128)(2,1)}), bf16[16,192,128]{2,1,0:T(8,128)(2,1)S(1)}, u32[]{:S(2)}, u32[]{:S(2)}) async-start(bf16[16,192,128]{2,1,0:T(8,128)(2,1)} %broadcast_in_dim.44), calls=%async_computation.8 | async-start | bytes 1572864 | tf_op jit(solution)/shard_map/all_to_all | solution.py:42
  418.3 2.3 collective-permute-start.4
  (38 other events, 228.4 us)

commit v4 on v3

--- a/solution.py
+++ b/solution.py
@@ -35,23 +35,29 @@
     return lax.optimization_barrier((value, event))[0]
 
 
-def gather_all(part, row_devices, during=()):
+def spread_over(part, row_devices):
+    return jnp.broadcast_to(part[None], (row_devices,) + part.shape)
+
+
+def same_core_exchange(block, row_devices):
+    groups = [[d for d in range(2 * row_devices) if d % 2 == k] for k in range(2)]
+    return lax.all_to_all(
+        block, BOTH, split_axis=0, concat_axis=0, tiled=True, axis_index_groups=groups
+    )
+
+
+def core_exchange(block, row_devices):
+    return lax.ppermute(block, "row", [(d, d ^ 1) for d in range(row_devices)])
+
+
+def gather_all(spread, row_devices, during=()):
     every = 2 * row_devices
-    groups = [[d for d in range(every) if d % 2 == k] for k in range(2)]
-    spread = jnp.broadcast_to(part[None], (every // 2,) + part.shape)
-    got = lax.all_to_all(
-        spread, BOTH, split_axis=0, concat_axis=0, tiled=True, axis_index_groups=groups
-    )
-    got = after(got, during)
-    other = lax.ppermute(got, "row", [(d, d ^ 1) for d in range(row_devices)])
+    first = same_core_exchange(spread, row_devices)
+    got = after(first, during)
+    other = core_exchange(got, row_devices)
     odd = lax.axis_index("row") % 2 == 1
     pair = [jnp.where(odd, other, got), jnp.where(odd, got, other)]
-    return jnp.stack(pair, axis=1).reshape((every,) + part.shape)
-
-
-def scatter_sum(sent):
-    parts = lax.all_to_all(sent, BOTH, split_axis=0, concat_axis=0, tiled=True)
-    return jnp.sum(parts.astype(F32), axis=0).astype(BF)
+    return jnp.stack(pair, axis=1).reshape((every,) + spread.shape[1:]), first
 
 
 def norm_rows(values):
@@ -122,6 +128,11 @@
     count = ref.shape[0] // LANES
     cut = [ref[k * LANES : (k + 1) * LANES].T for k in range(count)]
     return jnp.concatenate([jnp.sum(part, axis=0, keepdims=True) for part in cut], axis=0)
+
+
+def spread_rows(ref, at, rows):
+    shape = (ref.shape[0],) + rows.shape
+    ref[:, at : at + rows.shape[0]] = jnp.broadcast_to(rows[None], shape)
 
 
 def turn_blocks(ref):
@@ -413,12 +424,11 @@
             gout_ref[pl.ds(b, outer_dim, stride=outer_dim), :] = mm(left_ref[...], mixed, TN)
         at = 0
         for half in range(dright_ref.shape[0]):
-            packed_ref[at : at + outer_dim] = dright_ref[half].astype(BF)
+            spread_rows(packed_ref, at, dright_ref[half].astype(BF))
             at = at + outer_dim
-        packed_ref[at : at + count] = d_left.astype(BF)
+        spread_rows(packed_ref, at, d_left.astype(BF))
         if carry_ref.shape[0] > 1:
-            start = packed_ref.shape[0] - carry_ref.shape[0]
-            packed_ref[start:] = carry_ref[...]
+            spread_rows(packed_ref, packed_ref.shape[1] - carry_ref.shape[0], carry_ref[...])
         in_rows, outer_rows = acc_ref.shape[0], gout_ref.shape[0]
         late_ref[:in_rows] = turn_blocks(acc_ref).astype(BF)
         late_ref[in_rows : in_rows + outer_rows] = gout_ref[...].astype(BF)
@@ -498,7 +508,7 @@
     low_ref[...] = low
     attn = mm(low, values).reshape(rows, heads, width)
     attn = jnp.sum(attn * lanes[None], axis=1)
-    gated_ref[...] = (gate * attn).astype(BF)
+    gated_ref[...] = jnp.broadcast_to((gate * attn).astype(BF)[None], gated_ref.shape)
 
 
 def node_chunks(rows):
@@ -648,10 +658,26 @@
             at = at + 1
 
 
-def adam_refs(master_ref, first_ref, second_ref, grad, outs):
-    for ref, value in zip(
-        outs, adam_step(master_ref[...], first_ref[...], second_ref[...], grad, 0.1, 0.1)
-    ):
+def layout_kernel(parts_ref, qkv_ref, bias_ref, gainx_ref, gains_ref, out_ref):
+    total = jnp.zeros(parts_ref.shape[1:], F32)
+    for d in range(parts_ref.shape[0]):
+        total += parts_ref[d].astype(F32)
+    at = 0
+    for k in range(qkv_ref.shape[0]):
+        spread_rows(out_ref, at, qkv_ref[k])
+        at = at + qkv_ref.shape[1]
+    spread_rows(out_ref, at, total.astype(BF))
+    at = at + total.shape[0]
+    small = [bias_ref[...], gainx_ref[...], gains_ref[...]]
+    filled = sum(part.shape[0] for part in small)
+    spare = out_ref.shape[1] - at - filled
+    small = jnp.concatenate(small + [jnp.zeros((spare, LANES), F32)], axis=0)
+    spread_rows(out_ref, at, small.astype(BF))
+
+
+def adam_refs(master_ref, first_ref, second_ref, grad, outs, rate=0.1, decay=0.1):
+    found = adam_step(master_ref[...], first_ref[...], second_ref[...], grad, rate, decay)
+    for ref, value in zip(outs, found):
         ref[...] = value
 
 
@@ -692,7 +718,9 @@
     for _ in range(6):
         blocks.append(take(at, at + count).reshape(-1, LANES))
         at = at + count
-    late = take(at, at + late_rows).reshape(-1, LANES)
+    late = take(at, at + late_rows)
+    late = late.reshape((-1, 2) + late.shape[1:])
+    late = jnp.concatenate([late[:, 0], late[:, 1]], axis=0).reshape(-1, LANES)
     at = at + late_rows
     small = jnp.sum(take(at, at + small_rows), axis=0)
     return blocks, (late[in_rows : in_rows + outer_rows], across(late[:in_rows])), small
@@ -708,12 +736,13 @@
 
 
 def final_kernel(
-    layout, dgate_ref, norm_ref, both_ref, dmid_ref, gain_ref, w_ref, *refs
+    layout, dgate_ref, norm_ref, both_ref, dmid_ref, gain_ref, w_ref, gainn_ref, gains_ref, *refs
 ):
     n_got = 1 if layout else 9
+    minor, refs = refs[:6], refs[6:]
     got, refs = refs[:n_got], refs[n_got:]
     olds, refs = refs[:9], refs[9:]
-    news, (dnode_ref, gaina_ref, small_ref, grad_ref), sums = refs[:9], refs[9:13], refs[13:]
+    news, minor_new, (dnode_ref, grad_ref, full_ref), sums = refs[:9], refs[9:15], refs[15:18], refs[18:]
     width = dmid_ref.shape[1]
 
     @pl.when(pl.program_id(0) == 0)
@@ -724,7 +753,6 @@
         else:
             values = [ref[...] for ref in got]
             blocks, grads, small = values[:6], values[6:8], values[8]
-        small_ref[...] = small
         for ref, grad in zip(sums[1:], grads):
             ref[...] = grad
         for k, block in enumerate(blocks):
@@ -736,8 +764,26 @@
             hat, inv = norm_lanes(both_ref[rows, :width].astype(F32))
             back = mm(grad_ref[rows], w_ref[...], NT)
             total += sublane_sum(back * hat)
-            dnode_ref[rows] = dmid_ref[rows] + norm_lanes_back(back * gain_ref[...], hat, inv)
-        gaina_ref[...] = total
+            full_ref[rows] = dmid_ref[rows] + norm_lanes_back(back * gain_ref[...], hat, inv)
+        if dnode_ref.shape[0] == full_ref.shape[0]:
+            dnode_ref[...] = full_ref[...]
+        else:
+            count = dnode_ref.shape[0]
+            first = lax.axis_index("crop") * (full_ref.shape[0] // 2)
+            first = pl.multiple_of(first + lax.axis_index("row") * count, count)
+            dnode_ref[:, 0] = full_ref[pl.ds(first, count), :]
+        heads = minor[0].shape[0]
+        bias = small[:heads]
+        adam_refs(*minor[:3], bias, minor_new[:3])
+        spots = width // LANES
+        rows_of = lambda line: [line[:, k * LANES : (k + 1) * LANES] for k in range(spots)]
+        gain_b = minor[3][spots : spots + 1]
+        weight = minor[0][...].astype(BF).astype(F32)
+        grad_b = jnp.sum(weight * bias, axis=0, keepdims=True) / gain_b
+        lines = rows_of(total) + [grad_b] + rows_of(gainn_ref[...]) + rows_of(gains_ref[...])
+        rest = minor[3].shape[0] - len(lines)
+        lines.append(small[heads : heads + rest])
+        adam_refs(*minor[3:], jnp.concatenate(lines, axis=0), minor_new[3:], 1.0, 0.0)
 
     for k in range(3):
         height = olds[3 * k].shape[0]
@@ -842,14 +888,16 @@
 
     columns = [column(gain) for gain in (gain_x, gain_t, gain_h)]
     ready = [att_wb, attout_wb, nodeup_wb, nodedown_wb, mask]
-    node_both = gather_all(node_both, row_devices, [xt, pair_bias] + ready)
+    node_both, _ = gather_all(
+        spread_over(node_both, row_devices), row_devices, [xt, pair_bias] + ready
+    )
     node_both = node_both.reshape(nodes, 2 * width_s)
     square = (nodes, width_s)
     att_norm, gate_all, qkv_crop, att_weights, weights_low, gated_own = single(
         attend_kernel,
         [(square, BF), (square, F32), ((residues, 3 * width_s), BF),
          ((count * heads, residues), F32), ((count * heads, residues), BF),
-         ((count, width_s), BF)],
+         ((row_devices, count, width_s), BF)],
         [node_both, node_feats[:, 0], line(gain_a), att_wb, pair_bias, mask],
         flops=8 * nodes * width_s * width_s, far=(0, 1, 2, 3),
     )
@@ -857,7 +905,8 @@
     if direct:
         weights_cut = weights_cut.reshape(row_devices, -1, LANES)
     ready = [weights_cut, node_wb, outer_wb, in_wt, chain_col, columns[0]]
-    gated = gather_all(gated_own, row_devices, ready).reshape(nodes, width_s)
+    gated, _ = gather_all(gated_own, row_devices, ready)
+    gated = gated.reshape(nodes, width_s)
 
     node_mid, node_next, node_proj, right_t = single(
         node_kernel,
@@ -1005,20 +1054,26 @@
          whole(in_wt.shape), whole(in_wb.shape), whole(left_vec.shape), whole(w_outer.shape),
          whole(carry.shape)],
         [(slab, shape_of((count, width_z, residues), F32)),
-         (whole((packed_rows, LANES)), shape_of((packed_rows, LANES), BF)),
+         (whole((row_devices, packed_rows, LANES)),
+          shape_of((row_devices, packed_rows, LANES), BF)),
          (whole((late_rows, LANES)), shape_of((late_rows, LANES), BF)),
          (whole((width_z // LANES, LANES)), shape_of((width_z // LANES, LANES), F32))],
         [first_sum, dacts_rows, d_second, d_logit, mask, outer_mix, right_t, columns[0],
          in_wt, in_wb, left_vec, w_outer, carry],
-        free=(1,), near=(1, 2),
+        free=(1,),
         scratch=[pltpu.VMEM((width_z, residues), F32), pltpu.VMEM((9 * hidden, step * residues), BF),
                  pltpu.VMEM(in_wt.shape, F32), pltpu.VMEM((count * outer_dim, LANES), F32),
                  pltpu.VMEM((residues // LANES, outer_dim, LANES), F32),
                  pltpu.VMEM(w_outer.shape, F32)] + stage(6),
         flops=54 * pairs * width_z * hidden, moved=20 * pairs * width_z,
     )
-    got = gather_all(packed, row_devices, late)
-    late_own = scatter_sum(after(late, got).reshape(every, -1, LANES))
+    late = late.reshape(2, late_rows // 2, LANES)
+    odd = row_index % 2 == 1
+    theirs = core_exchange(jnp.where(odd, late[0], late[1]), row_devices)
+    late = jnp.where(odd, late[1], late[0]).astype(F32) + theirs.astype(F32)
+    late = late.astype(BF).reshape(row_devices, -1, LANES)
+    got, first_got = gather_all(packed, row_devices, late)
+    late_parts = same_core_exchange(after(late, first_got), row_devices)
     left_all = left_vec
     if not direct:
         left_all = got[:, right_rows : right_rows + count].reshape(nodes, LANES)
@@ -1035,7 +1090,7 @@
          line(gain_n), line(gain_s), attout_wb, nodeup_wb, nodedown_wb, wide_node],
         scratch=[pltpu.VMEM((nodes, LANES), BF), low_square, pltpu.VMEM(tall, BF), low_square,
                  low_square, pltpu.VMEM(tall, BF), low_square],
-        flops=50 * nodes * width_s * width_s, apart=True,
+        flops=50 * nodes * width_s * width_s, far=(0, 1, 2, 3, 4, 5, 6, 8), apart=True,
     )
 
     values_own = lax.dynamic_slice(qkv_crop, (first_row, 2 * width_s), (count, width_s))
@@ -1048,10 +1103,20 @@
         flops=12 * count * heads * residues * width_s,
     )
 
-    small = jnp.concatenate([g_bias_t, gains_x, gains_th]).astype(BF)
-    small = jnp.pad(small, ((0, -small.shape[0] % 16), (0, 0)))
-    pieces = [qkv_grad.reshape(-1, LANES), late_own, small]
-    layout = (count, late_own.shape[0], in_rows, outer_rows, small.shape[0])
+    qkv_rows, share_rows = qkv_grad.size // LANES, late_parts.shape[1]
+    small_rows = heads + gains_x.shape[0] + gains_th.shape[0]
+    small_rows = small_rows + -small_rows % 16
+    layout = (count, share_rows, in_rows, outer_rows, small_rows)
+    last_shape = (row_devices, qkv_rows + share_rows + small_rows, LANES)
+    pieces = [late_parts, qkv_grad, g_bias_t, gains_x, gains_th]
+    if direct:
+        (last_own,) = single(layout_kernel, [(last_shape, BF)], pieces)
+    else:
+        small = jnp.concatenate(pieces[2:])
+        small = jnp.pad(small, ((0, small_rows - small.shape[0]), (0, 0)))
+        late_own = jnp.sum(late_parts.astype(F32), axis=0)
+        last_own = [qkv_grad.reshape(-1, LANES).astype(F32), late_own, small]
+        last_own = spread_over(jnp.concatenate(last_own).astype(BF), row_devices)
 
     (pair_grad,) = pair_call(
         last_kernel, steps,
@@ -1083,7 +1148,7 @@
     if direct:
         pair_got, pair_layout = [got], (right_rows + left_rows, part_up, part_z)
     else:
-        pair_all = gather_all(pair_own, row_devices)
+        pair_all, _ = gather_all(spread_over(pair_own, row_devices), row_devices)
         pair_got, pair_layout = list(unpack_pair(pair_all.astype(F32), part_up, part_z)), None
     specs += [whole(arg.shape) for arg in pair_got]
     args += pair_got
@@ -1093,7 +1158,7 @@
         moved=sum(7 * arg.size for arg in args),
     )
     beside = (pair_grad, found[0], node_out)
-    last = gather_all(jnp.concatenate(pieces), row_devices, beside)
+    last, _ = gather_all(last_own, row_devices, beside)
     for at, k in enumerate(early):
         updated[k] = [turned(k, value) for value in found[3 * at : 3 * at + 3]]
     for at, k in enumerate(pair_keys, len(early)):
@@ -1104,7 +1169,11 @@
     if not direct:
         blocks, sums, small = unpack(lambda a, b: last[:, a:b].astype(F32), layout)
         got_last = blocks + list(sums) + [small]
-    fixed = [d_gate, att_norm, node_both, grad_mid, line(gain_a), att_wb] + got_last
+    node_shape = (count, 1, width_s) if direct else square
+    minor = [old[1].T for old in (masters, firsts, seconds)]
+    minor += [old[11].reshape(-1, LANES) for old in (masters, firsts, seconds)]
+    fixed = [d_gate, att_norm, node_both, grad_mid, line(gain_a), att_wb, gain_n_grad, gain_s_grad]
+    fixed = fixed + minor + got_last
     olds, specs = [], [whole(arg.shape) for arg in fixed]
     for k in late_keys:
         olds += [masters[k], firsts[k], seconds[k]]
@@ -1112,25 +1181,18 @@
     found = pair_call(
         functools.partial(final_kernel, layout if direct else None), parts, specs + blocked,
         [(spec, shape_of(old.shape, F32)) for spec, old in zip(blocked, olds)]
-        + [(whole(shape), shape_of(shape, F32)) for shape in (square, (1, width_s), small.shape)],
+        + [(whole(value.shape), shape_of(value.shape, F32)) for value in minor]
+        + [(whole(node_shape), shape_of(node_shape, F32))],
         fixed + olds,
-        scratch=[pltpu.VMEM((nodes, 4 * width_s), BF)]
+        scratch=[pltpu.VMEM((nodes, 4 * width_s), BF), pltpu.VMEM(square, F32)]
         + [pltpu.VMEM(masters[k].shape, F32) for k in late_keys],
         flops=16 * nodes * width_s * width_s, moved=sum(7 * old.size for old in olds),
     )
     for at, k in enumerate(late_keys):
         updated[k] = found[3 * at : 3 * at + 3]
-    d_nodes, gain_a_grad, small = found[9:]
-    node_grad = own_rows(d_nodes)[:, None]
-
-    g_bias = small[:heads].T
-    gain_b_grad = jnp.sum(bias_wb.astype(F32) * g_bias, axis=1) / gain_b
-    pair_gains = small[heads : heads + gains_x.shape[0] + gains_th.shape[0]].reshape(-1)
-    gain_grad = jnp.concatenate(
-        [gain_a_grad[0], gain_b_grad, gain_n_grad[0], gain_s_grad[0], pair_gains]
-    )
-    updated[1] = adam_step(masters[1], firsts[1], seconds[1], g_bias, 0.1, 0.1)
-    updated[11] = adam_step(masters[11], firsts[11], seconds[11], gain_grad, 1.0, 0.0)
+    updated[1] = [value.T for value in found[9:12]]
+    updated[11] = [value.reshape(-1) for value in found[12:15]]
+    node_grad = found[15] if direct else own_rows(found[15])[:, None]
     results = [pair_out[:, None], node_out, pair_grad[:, None], node_grad]
     for k in range(12):
         results.extend(updated[k])

time: 437 us -> 427 us (0.977)
  blocking collectives: 85.4 us -> 54.3 us
  starting transfers between devices: 45.1 us -> 65 us
  local copies, waits for them, and re-layouts: 26 us -> 19.4 us
  waiting for transfers between devices: 158 us -> 164 us
    all_to_all x1 -> x0, blocking collectives: 31.1 us -> none  [gather_all(): lax.all_to_all(spread, BOTH, split_axis=0, concat_axis=0, tiled=True, axi...]
    all_to_all x4 -> x5, starting transfers between devices: 19.9 us -> 39.7 us  [same_core_exchange(): lax.all_to_all(block, BOTH, split_axis=0, concat_axis=0, tiled=True, axis...]
    all_to_all x4 -> x5, waiting for transfers between devices: 18.3 us -> 24.4 us  [same_core_exchange(): lax.all_to_all(block, BOTH, split_axis=0, concat_axis=0, tiled=True, axis...]
    pallas_call x13 -> x14, Pallas kernels: 98.3 us -> 101 us  [pair_call(): pl.pallas_call(kernel, grid=(steps,), in_specs=ins, out_specs=[spec for s...]
  transfers between devices with their start and end apart: 12 -> 14, of which waited for: 11 -> 11; matrix products, arithmetic and copies ran while one was open for 7% -> 8% of each run, Pallas kernels for 5% -> 6%
where the time goes in v4:
time: 427 us; the launch traced here: 426 us
  waiting for transfers between devices  164 us (38%)
  Pallas kernels  101 us (24%)
  starting transfers between devices  65 us (15%)
  blocking collectives  54.3 us (13%)
  other arithmetic  20 us (5%)
  local copies, waits for them, and re-layouts  19.4 us (5%)
    all_to_all x3, waiting for transfers between devices, swap(): return lax.all_to_all(block, 'row', split_axis=0, concat_axis=0, tiled=True)  131 us
    pallas_call x14, Pallas kernels, pair_call(): pl.pallas_call(kernel, grid=(steps,), in_specs=ins, out_specs=[spec for s...  101 us
    all_to_all x1, blocking collectives, swap(): return lax.all_to_all(block, 'row', split_axis=0, concat_axis=0, tiled=True)  54.3 us
    all_to_all x5, starting transfers between devices, same_core_exchange(): lax.all_to_all(block, BOTH, split_axis=0, concat_axis=0, tiled=True, axis...  39.7 us
    all_to_all x5, waiting for transfers between devices, same_core_exchange(): lax.all_to_all(block, BOTH, split_axis=0, concat_axis=0, tiled=True, axis...  24.4 us
    all_to_all x3, starting transfers between devices, swap(): return lax.all_to_all(block, 'row', split_axis=0, concat_axis=0, tiled=True)  24.3 us
  transfers between devices with their start and end apart: 14, of which 11 were waited for; matrix products, arithmetic and copies ran while one was open for 8% of the time, Pallas kernels for 6%

profile of v4, /device:TPU:0, one launch (start us, length us, event | category | flops | bytes accessed | tf_op | source)
XLA Modules:
  0.0 425.7 jit_solution(15822889372426721265)
XLA Ops:
  2.2 8.4 %all-to-all-start = ((bf16[16,16,512]{2,1,0:T(8,128)(2,1)}), bf16[16,16,512]{2,1,0:T(8,128)(2,1)}, u32[]{:S(2)}, u32[]{:S(2)}) async-start(bf16[16,16,512]{2,1,0:T(8,128)(2,1)} %broadcast_in_dim.8), calls=%async_computation | async-start | bytes 524288 | tf_op jit(solution)/shard_map/all_to_all | solution.py:44
  25.2 5.2 %all-to-all-start.1 = ((bf16[16,16,256]{2,1,0:T(8,128)(2,1)}), bf16[16,16,256]{2,1,0:T(8,128)(2,1)S(1)}, u32[]{:S(2)}, u32[]{:S(2)}) async-start(bf16[16,16,256]{2,1,0:T(8,128)(2,1)} %get-tuple-element.124), calls=%async_computation.1 | async-start | bytes 262144 | tf_op jit(solution)/shard_map/all_to_all | solution.py:44
  32.8 5.6 %all-to-all-done.1 = bf16[16,16,256]{2,1,0:T(8,128)(2,1)S(1)} async-done(((bf16[16,16,256]{2,1,0:T(8,128)(2,1)}), bf16[16,16,256]{2,1,0:T(8,128)(2,1)S(1)}, u32[]{:S(2)}, u32[]{:S(2)}) %all-to-all-start.1) | async-done | bytes 131104 | tf_op jit(solution)/shard_map/all_to_all | solution.py:44
  40.0 4.6 %shard_map.701 = (f32[512,256]{1,0:T(8,128)}, f32[512,256]{1,0:T(8,128)}, bf16[512,64]{1,0:T(8,128)(2,1)S(1)}, bf16[32,256]{1,0:T(8,128)(2,1)S(1)}) custom-call(bf16[512,512]{1,0:T(8,128)(2,1)S(1)} %bitcast.92, bf16[512,256]{1,0:T(8,128)(2,1)S(1)} %bitcast.99, f32[1,256]{1,0:T(1,128)S(1)} %bitcast.108, f32[1,256]{1,0:T(1,128)S(1)} %bitcast.106, ...), custom_call_target="tpu_custom_call" | custom-call | flops 603979776 | bytes 4032512 | tf_op jit(solution)/shard_map/pallas_call | solution.py:811
  45.4 9.6 %shard_map.702 = (f32[16,128,256]{2,1,0:T(8,128)}, bf16[16,784,128]{2,1,0:T(8,128)(2,1)}) custom-call(bf16[16,128,256]{2,1,0:T(8,128)(2,1)} %get-tuple-element.121.xt_ref, bf16[16,32,128]{2,1,0:T(8,128)(2,1)} %bitcast.117, bf16[32,256]{1,0:T(8,128)(2,1)} %copy-done.20, f32[16,1,256]{2,1,0:T(1,128)} %copy-done.13, f32[128,1]{1,0:T(8,128)} %copy.112.gain_ref.gx_ref, ...), custom_call_target="tpu_custom_call" | custom-call | flops 1073741824 | bytes 6291456 | tf_op jit(solution)/shard_map/pallas_call | solution.py:811
  55.1 3.9 all-to-all-start.2
  68.4 51.1 %all-to-all-done.2.acts_ref = bf16[16,784,128]{2,1,0:T(8,128)(2,1)S(1)} async-done(((bf16[16,784,128]{2,1,0:T(8,128)(2,1)}), bf16[16,784,128]{2,1,0:T(8,128)(2,1)S(1)}, u32[]{:S(2)}, u32[]{:S(2)}) %all-to-all-start.2) | async-done | bytes 3211296 | tf_op jit(solution)/shard_map/all_to_all | solution.py:935
  119.4 4.6 %shard_map.703 = bf16[16,384,128]{2,1,0:T(8,128)(2,1)} custom-call(s32[256,1]{1,0:T(8,128)} %copy.114.col_ref, s32[1,256]{1,0:T(1,128)} %row_ref.3, bf16[16,784,128]{2,1,0:T(8,128)(2,1)S(1)} %all-to-all-done.2.acts_ref), custom_call_target="tpu_custom_call" | custom-call | flops 536870912 | bytes 4718592 | tf_op jit(solution)/shard_map/pallas_call | solution.py:811
  124.0 15.9 %all-to-all-start.3 = ((bf16[16,384,128]{2,1,0:T(8,128)(2,1)}), bf16[16,384,128]{2,1,0:T(8,128)(2,1)}, u32[]{:S(2)}, u32[]{:S(2)}) async-start(bf16[16,384,128]{2,1,0:T(8,128)(2,1)} %shard_map.703), calls=%async_computation.3 | async-start | bytes 3145728 | tf_op jit(solution)/shard_map/all_to_all | solution.py:935
  145.3 26.6 %all-to-all-done.3.tri_ref = bf16[16,384,128]{2,1,0:T(8,128)(2,1)} async-done(((bf16[16,384,128]{2,1,0:T(8,128)(2,1)}), bf16[16,384,128]{2,1,0:T(8,128)(2,1)}, u32[]{:S(2)}, u32[]{:S(2)}) %all-to-all-start.3) | async-done | bytes 1572896 | tf_op jit(solution)/shard_map/all_to_all | solution.py:935
  171.9 22.6 %shard_map.704 = (bf16[16,256,128]{2,1,0:T(8,128)(2,1)}, f32[16,128,256]{2,1,0:T(8,128)}, bf16[16,128,256]{2,1,0:T(8,128)(2,1)}, bf16[16,480,128]{2,1,0:T(8,128)...) custom-call(f32[16,128,256]{2,1,0:T(8,128)} %get-tuple-element.129.sum_ref, ...), custom_call_target="tpu_custom_call" | custom-call | flops 3221225472 | bytes 10485760 | tf_op jit(solution)/shard_map/pallas_call | solution.py:811
  194.5 54.3 %all_to_all.45.grad_ref = bf16[16,480,128]{2,1,0:T(8,128)(2,1)} all-to-all(bf16[16,480,128]{2,1,0:T(8,128)(2,1)} %get-tuple-element.134), channel_id=1, replica_groups=mesh['crop'=2,'row'=16] {'row'}, dimensions={0} | all-to-all | bytes 3932160 | tf_op jit(solution)/shard_map/all_to_all | solution.py:935
  248.8 6.7 %shard_map.705 = bf16[16,768,128]{2,1,0:T(8,128)(2,1)} custom-call(s32[256,1]{1,0:T(8,128)} %copy.114.col_ref, s32[1,256]{1,0:T(1,128)} %row_ref.3, bf16[16,784,128]{2,1,0:T(8,128)(2,1)S(1)} %all-to-all-done.2.acts_ref, bf16[16,480,128]{2,1,0:T(8,128)(2,1)} %all_to_all.45.grad_ref), custom_call_target="tpu_custom_call" | custom-call | flops 1073741824 | bytes 7864320 | tf_op jit(solution)/shard_map/pallas_call | solution.py:811
  255.5 4.6 %all-to-all-start.5 = ((bf16[16,768,128]{2,1,0:T(8,128)(2,1)}), bf16[16,768,128]{2,1,0:T(8,128)(2,1)}, u32[]{:S(2)}, u32[]{:S(2)}) async-start(bf16[16,768,128]{2,1,0:T(8,128)(2,1)} %shard_map.705), calls=%async_computation.5 | async-start | bytes 6291456 | tf_op jit(solution)/shard_map/all_to_all | solution.py:935
  265.6 53.8 %all-to-all-done.5.acts_ref = bf16[16,768,128]{2,1,0:T(8,128)(2,1)} async-done(((bf16[16,768,128]{2,1,0:T(8,128)(2,1)}), bf16[16,768,128]{2,1,0:T(8,128)(2,1)}, u32[]{:S(2)}, u32[]{:S(2)}) %all-to-all-start.5) | async-done | bytes 3145760 | tf_op jit(solution)/shard_map/all_to_all | solution.py:935
  319.5 16.5 %shard_map.706 = (f32[16,128,256]{2,1,0:T(8,128)}, bf16[16,128,128]{2,1,0:T(8,128)(2,1)}, bf16[2560,128]{1,0:T(8,128)(2,1)}, f32[1,128]{1,0:T(1,128)}) custom-call(f32[16,128,256]{2,1,0:T(8,128)} %get-tuple-element.129.sum_ref, bf16[16,768,128]{2,1,0:T(8,128)(2,1)} %all-to-all-done.5.acts_ref, f32[16,128,256]{2,1,0:T(8,128)} %get-tuple-element.136.ds_ref, ...), custom_call_target="tpu_custom_call" | custom-call | flops 3623878656 | bytes 10485760 | tf_op jit(solution)/shard_map/pallas_call | solution.py:811
  336.0 15.7 %all-to-all-start.6 = ((bf16[16,128,128]{2,1,0:T(8,128)(2,1)}), bf16[16,128,128]{2,1,0:T(8,128)(2,1)}, u32[]{:S(2)}, u32[]{:S(2)}) async-start(bf16[16,128,128]{2,1,0:T(8,128)(2,1)} %get-tuple-element.139), calls=%async_computation.6 | async-start | bytes 1048576 | tf_op jit(solution)/shard_map/all_to_all | solution.py:44
  356.5 10.9 %all-to-all-done.6 = bf16[16,128,128]{2,1,0:T(8,128)(2,1)} async-done(((bf16[16,128,128]{2,1,0:T(8,128)(2,1)}), bf16[16,128,128]{2,1,0:T(8,128)(2,1)}, u32[]{:S(2)}, u32[]{:S(2)}) %all-to-all-start.6) | async-done | bytes 524320 | tf_op jit(solution)/shard_map/all_to_all | solution.py:44
  374.1 8.6 %shard_map.707 = (f32[64,256]{1,0:T(8,128)}, f32[1024,256]{1,0:T(8,128)}, f32[256,1024]{1,0:T(8,128)}, f32[256,256]{1,0:T(8,128)}, f32[1,256]{1,0:T(1,128)}, /*i...) custom-call(bf16[32,128,128]{2,1,0:T(8,128)(2,1)S(1)} %bitcast.95, ...), custom_call_target="tpu_custom_call" | custom-call | flops 1677721600 | bytes 7737344 | tf_op jit(solution)/shard_map/pallas_call | solution.py:811
  385.4 6.7 %all-to-all-start.8 = ((bf16[16,192,128]{2,1,0:T(8,128)(2,1)}), bf16[16,192,128]{2,1,0:T(8,128)(2,1)S(1)}, u32[]{:S(2)}, u32[]{:S(2)}) async-start(bf16[16,192,128]{2,1,0:T(8,128)(2,1)} %shard_map.710), calls=%async_computation.8 | async-start | bytes 1572864 | tf_op jit(solution)/shard_map/all_to_all | solution.py:44
  393.4 8.4 %shard_map.711 = (f32[256,256]{1,0:T(8,128)}, f32[256,256]{1,0:T(8,128)}, f32[256,256]{1,0:T(8,128)}, f32[256,1024]{1,0:T(8,128)}, f32[256,1024]{1,0:T(8,128)}, ...) custom-call(f32[256,256]{1,0:T(8,128)} %refs_0_.1, ...), custom_call_target="tpu_custom_call" | custom-call | bytes 24084480 | tf_op jit(solution)/shard_map/pallas_call | solution.py:811
  401.8 5.1 %shard_map.709 = f32[16,256,128]{2,1,0:T(8,128)} custom-call(bf16[16,128,256]{2,1,0:T(8,128)(2,1)} %get-tuple-element.121.xt_ref, f32[16,128,256]{2,1,0:T(8,128)} %get-tuple-element.138.fg_ref, bf16[16,8,256]{2,1,0:T(8,128)(2,1)} %bitcast.101, f32[128,1]{1,0:T(8,128)} %copy-done.5, bf16[128,8]{1,0:T(8,128)(2,1)} %copy-done.29), custom_call_target="tpu_custom_call" | custom-call | flops 16777216 | bytes 5242880 | tf_op jit(solution)/shard_map/pallas_call | solution.py:811
  406.9 6.0 %all-to-all-done.8 = bf16[16,192,128]{2,1,0:T(8,128)(2,1)S(1)} async-done(((bf16[16,192,128]{2,1,0:T(8,128)(2,1)}), bf16[16,192,128]{2,1,0:T(8,128)(2,1)S(1)}, u32[]{:S(2)}, u32[]{:S(2)}) %all-to-all-start.8) | async-done | bytes 786464 | tf_op jit(solution)/shard_map/all_to_all | solution.py:44
  416.9 8.7 %shard_map.712 = (f32[256,1024]{1,0:T(8,128)}, f32[256,1024]{1,0:T(8,128)}, f32[256,1024]{1,0:T(8,128)}, f32[1024,128]{1,0:T(8,128)}, f32[1024,128]{1,0:T(8,128)...) custom-call(bf16[512,256]{1,0:T(8,128)(2,1)} %get-tuple-element.150., ...), custom_call_target="tpu_custom_call" | custom-call | flops 536870912 | bytes 11354112 | tf_op jit(solution)/shard_map/pallas_call | solution.py:811
  (153 shorter events, 60.2 us)
Async XLA Ops:
  2.2 18.3 %all-to-all-start = ((bf16[16,16,512]{2,1,0:T(8,128)(2,1)}), bf16[16,16,512]{2,1,0:T(8,128)(2,1)}, u32[]{:S(2)}, u32[]{:S(2)}) async-start(bf16[16,16,512]{2,1,0:T(8,128)(2,1)} %broadcast_in_dim.8), calls=%async_computation | async-start | bytes 524288 | tf_op jit(solution)/shard_map/all_to_all | solution.py:44
  14.0 25.9 %copy-start.10 = (bf16[256,256]{1,0:T(8,128)(2,1)}, bf16[256,256]{1,0:T(8,128)(2,1)S(1)}, u32[]{:S(2)}) copy-start(bf16[256,256]{1,0:T(8,128)(2,1)S(1)} %convert_element_type.68.wo_ref) | copy-start | bytes 393220
  14.3 25.6 %copy-start.6 = (bf16[256,1024]{1,0:T(8,128)(2,1)}, bf16[256,1024]{1,0:T(8,128)(2,1)S(1)}, u32[]{:S(2)}) copy-start(bf16[256,1024]{1,0:T(8,128)(2,1)S(1)} %convert_element_type.69.wu_ref) | copy-start | bytes 1572868
  16.1 23.9 %copy-start.7 = (bf16[1024,256]{1,0:T(8,128)(2,1)}, bf16[1024,256]{1,0:T(8,128)(2,1)S(1)}, u32[]{:S(2)}) copy-start(bf16[1024,256]{1,0:T(8,128)(2,1)S(1)} %convert_element_type.70.wd_ref) | copy-start | bytes 1572868
  20.5 1.9 collective-permute-start
  22.4 17.5 %copy-start.17 = (f32[256]{0:T(256)}, f32[256]{0:T(256)S(1)}, u32[]{:S(2)}) copy-start(f32[256]{0:T(256)S(1)} %get-tuple-element.294) | copy-start | bytes 3076
  22.4 17.5 %copy-start.18 = (f32[256]{0:T(256)}, f32[256]{0:T(256)S(1)}, u32[]{:S(2)}) copy-start(f32[256]{0:T(256)S(1)} %get-tuple-element.295) | copy-start | bytes 3076
  23.5 16.4 %copy-start.1 = (bf16[16,2,16,512]{3,2,1,0:T(8,128)(2,1)}, bf16[16,2,16,512]{3,2,1,0:T(8,128)(2,1)S(1)}, u32[]{:S(2)}) copy-start(bf16[16,2,16,512]{3,2,1,0:T(8,128)(2,1)S(1)} %pad_maximum_fusion.2) | copy-start | bytes 1572868
  25.2 13.3 %all-to-all-start.1 = ((bf16[16,16,256]{2,1,0:T(8,128)(2,1)}), bf16[16,16,256]{2,1,0:T(8,128)(2,1)S(1)}, u32[]{:S(2)}, u32[]{:S(2)}) async-start(bf16[16,16,256]{2,1,0:T(8,128)(2,1)} %get-tuple-element.124), calls=%async_computation.1 | async-start | bytes 262144 | tf_op jit(solution)/shard_map/all_to_all | solution.py:44
  38.5 1.3 collective-permute-start.1
  55.1 64.3 %all-to-all-start.2 = ((bf16[16,784,128]{2,1,0:T(8,128)(2,1)}), bf16[16,784,128]{2,1,0:T(8,128)(2,1)S(1)}, u32[]{:S(2)}, u32[]{:S(2)}) async-start(bf16[16,784,128]{2,1,0:T(8,128)(2,1)} %get-tuple-element.130), calls=%async_computation.2 | async-start | bytes 6422528 | tf_op jit(solution)/shard_map/all_to_all | solution.py:935
  124.0 15.9 %copy-start.30 = (bf16[128,256]{0,1:T(8,128)(2,1)S(1)}, bf16[128,256]{0,1:T(8,128)(2,1)}, u32[]{:S(2)}) copy-start(bf16[128,256]{0,1:T(8,128)(2,1)} %convert_bitcast_fusion.2) | copy-start | bytes 196612
  124.0 16.6 %copy-start.34 = (f32[128,1]{0,1:T(1,128)S(1)}, f32[128,1]{0,1:T(1,128)}, u32[]{:S(2)}) copy-start(f32[128,1]{0,1:T(1,128)} %get-tuple-element.290) | copy-start | bytes 1540
  124.0 19.0 %copy-start.28 = (bf16[512,128]{0,1:T(8,128)(2,1)S(1)}, bf16[512,128]{0,1:T(8,128)(2,1)}, u32[]{:S(2)}) copy-start(bf16[512,128]{0,1:T(8,128)(2,1)} %convert_bitcast_fusion.1) | copy-start | bytes 393220
  124.0 20.6 %slice-start = ((bf16[1152,128]{0,1:T(8,128)(2,1)}), bf16[128,128]{0,1:T(8,128)(2,1)S(1)}, s32[]{:S(2)}) async-start(bf16[1152,128]{0,1:T(8,128)(2,1)} %copy-done.27), calls=%async_computation.9 | async-start | bytes 65536 | tf_op jit(solution)/shard_map/slice | solution.py:999
  124.0 47.9 %all-to-all-start.3 = ((bf16[16,384,128]{2,1,0:T(8,128)(2,1)}), bf16[16,384,128]{2,1,0:T(8,128)(2,1)}, u32[]{:S(2)}, u32[]{:S(2)}) async-start(bf16[16,384,128]{2,1,0:T(8,128)(2,1)} %shard_map.703), calls=%async_computation.3 | async-start | bytes 3145728 | tf_op jit(solution)/shard_map/all_to_all | solution.py:935
  255.5 64.0 %all-to-all-start.5 = ((bf16[16,768,128]{2,1,0:T(8,128)(2,1)}), bf16[16,768,128]{2,1,0:T(8,128)(2,1)}, u32[]{:S(2)}, u32[]{:S(2)}) async-start(bf16[16,768,128]{2,1,0:T(8,128)(2,1)} %shard_map.705), calls=%async_computation.5 | async-start | bytes 6291456 | tf_op jit(solution)/shard_map/all_to_all | solution.py:935
  261.1 3.9 collective-permute-start.2
  336.0 31.4 %all-to-all-start.6 = ((bf16[16,128,128]{2,1,0:T(8,128)(2,1)}), bf16[16,128,128]{2,1,0:T(8,128)(2,1)}, u32[]{:S(2)}, u32[]{:S(2)}) async-start(bf16[16,128,128]{2,1,0:T(8,128)(2,1)} %get-tuple-element.139), calls=%async_computation.6 | async-start | bytes 1048576 | tf_op jit(solution)/shard_map/all_to_all | solution.py:44
  352.9 1.7 collective-permute-start.3
  367.4 5.1 %collective-permute-start.4 = (bf16[16,128,128]{2,1,0:T(8,128)(2,1)}, bf16[16,128,128]{2,1,0:T(8,128)(2,1)}, u32[]{:S(2)}, u32[]{:S(2)}) collective-permute-start(bf16[16,128,128]{2,1,0:T(8,128)(2,1)} %all-to-all-done.6), channel_id=1, source_target_pairs={{0,1},{1,0},{2,3},{3,2},{4,5},{5,4},{6,7},{7,6},{8,9},{9,8},{10,11... | collective-permute-start | bytes 1572872 | tf_op jit(solution)/shard_map/ppermute | solution.py:50
  368.8 15.6 %all-to-all-start.7 = ((bf16[16,80,128]{2,1,0:T(8,128)(2,1)}), bf16[16,80,128]{2,1,0:T(8,128)(2,1)S(1)}, u32[]{:S(2)}, u32[]{:S(2)}) async-start(bf16[16,80,128]{2,1,0:T(8,128)(2,1)} %bitcast.114), calls=%async_computation.7 | async-start | bytes 655360 | tf_op jit(solution)/shard_map/all_to_all | solution.py:44
  385.4 27.5 %all-to-all-start.8 = ((bf16[16,192,128]{2,1,0:T(8,128)(2,1)}), bf16[16,192,128]{2,1,0:T(8,128)(2,1)S(1)}, u32[]{:S(2)}, u32[]{:S(2)}) async-start(bf16[16,192,128]{2,1,0:T(8,128)(2,1)} %shard_map.710), calls=%async_computation.8 | async-start | bytes 1572864 | tf_op jit(solution)/shard_map/all_to_all | solution.py:44
  412.9 2.3 collective-permute-start.5
  (26 other events, 163.9 us)

commit v5 on v4

--- a/solution.py
+++ b/solution.py
@@ -226,18 +226,15 @@
     return jnp.where(same, wide, 0.0).astype(BF)
 
 
-def store_tiles(out_ref, pair, spot, tiles):
+def store_tiles(out_ref, pair, k, tiles):
     for t in range(3):
         block = tiles[t].astype(BF).reshape(out_ref.shape[0], -1, LANES)
-        if spot:
-            out_ref[:, spot(3 * pair + t)] = block
-        else:
-            out_ref[:, 3 * pair + t, 0] = block
+        out_ref[:, 3 * pair + t, k] = block
 
 
 def tri_kernel(dims, col_ref, row_ref, acts_ref, out_ref):
     same = chain_mask(col_ref, row_ref)
-    for spot in channel_spots(dims):
+    for k, spot in enumerate(channel_spots(dims)):
         left_out, right_out = slot_operands(acts_ref, 0, spot)
         left_in, right_in = slot_operands(acts_ref, 1, spot)
         outgoing = jnp.where(same, mm(left_out, right_out, NT), 0.0)
@@ -246,12 +243,12 @@
         o_lo, o_hi = outgoing[:, :LANES], outgoing[:, LANES:]
         main_o = o_lo + jnp.where(low, turn(o_hi), 0.0)
         tail = jnp.where(low, o_hi, turn(incoming[:, LANES:]))
-        store_tiles(out_ref, 0, spot, (main_o, incoming[:, :LANES], tail))
+        store_tiles(out_ref, 0, k, (main_o, incoming[:, :LANES], tail))
 
 
 def tri_back_kernel(dims, col_ref, row_ref, acts_ref, grad_ref, out_ref):
     same = chain_mask(col_ref, row_ref)
-    for spot in channel_spots(dims):
+    for k, spot in enumerate(channel_spots(dims)):
         left_out, right_out = slot_operands(acts_ref, 0, spot)
         left_in, right_in = slot_operands(acts_ref, 1, spot)
         grad_out, grad_in = slot_operands(grad_ref, 0, spot)
@@ -260,13 +257,13 @@
         d_right = mm(raw_out, left_out, TN)
         low = low_lanes((d_left.shape[0], LANES))
         tail = jnp.where(low, d_left[:, LANES:], turn(d_right[:, LANES:]))
-        store_tiles(out_ref, 0, spot, (d_left[:, :LANES], d_right[:, :LANES], tail))
+        store_tiles(out_ref, 0, k, (d_left[:, :LANES], d_right[:, :LANES], tail))
         d_left = jnp.where(same, mm(right_in, grad_in, NT), 0.0)
         d_right = mm(raw_columns(left_in, same), grad_in)
         l_lo, l_hi = d_left[:, :LANES], d_left[:, LANES:]
         main_l = l_lo + jnp.where(low, turn(l_hi), 0.0)
         tail = jnp.where(low, l_hi, turn(d_right[:, LANES:]))
-        store_tiles(out_ref, 1, spot, (main_l, d_right[:, :LANES], tail))
+        store_tiles(out_ref, 1, k, (main_l, d_right[:, :LANES], tail))
 
 
 def second_kernel(
@@ -350,8 +347,6 @@
                 block = turn_blocks(acc) if turned else acc[...]
                 send_ref[:, at : at + part] = block.reshape(devices, part, LANES).astype(BF)
                 at = at + part
-            spare = send_ref.shape[1] - at
-            send_ref[:, at:] = jnp.zeros((devices, spare, LANES), BF)
 
 
 def third_kernel(
@@ -815,7 +810,7 @@
         out_specs=[spec for spec, _ in outs],
         out_shape=shapes,
         scratch_shapes=list(scratch),
-        compiler_params=pltpu.CompilerParams(vmem_limit_bytes=48 * 1024 * 1024),
+        compiler_params=pltpu.CompilerParams(vmem_limit_bytes=40 * 1024 * 1024),
         cost_estimate=pl.CostEstimate(flops=flops, bytes_accessed=moved, transcendentals=0),
     )(*args)
 
@@ -897,7 +892,7 @@
         attend_kernel,
         [(square, BF), (square, F32), ((residues, 3 * width_s), BF),
          ((count * heads, residues), F32), ((count * heads, residues), BF),
-         ((row_devices, count, width_s), BF)],
+         ((every, count, width_s), BF)],
         [node_both, node_feats[:, 0], line(gain_a), att_wb, pair_bias, mask],
         flops=8 * nodes * width_s * width_s, far=(0, 1, 2, 3),
     )
@@ -905,8 +900,8 @@
     if direct:
         weights_cut = weights_cut.reshape(row_devices, -1, LANES)
     ready = [weights_cut, node_wb, outer_wb, in_wt, chain_col, columns[0]]
-    gated, _ = gather_all(gated_own, row_devices, ready)
-    gated = gated.reshape(nodes, width_s)
+    gated = lax.all_to_all(gated_own, BOTH, split_axis=0, concat_axis=0, tiled=True)
+    gated = after(gated, ready).reshape(nodes, width_s)
 
     node_mid, node_next, node_proj, right_t = single(
         node_kernel,
@@ -944,11 +939,19 @@
 
     def to_rows(block):
         if direct:
-            return swap(block)
+            return swap(block.reshape(row_devices, -1, LANES))
         tiles = block.shape[1]
         cut = block.reshape(tiles, share, row_devices, count, LANES)
         got = swap(cut.transpose(2, 0, 1, 3, 4))
         return got.transpose(3, 1, 0, 2, 4).reshape(count, tiles, hidden, LANES)
+
+    def tri_out(tiles):
+        if not direct:
+            return tri_block(tiles)
+        shape = (row_devices, tiles, share, count, LANES)
+        each = share // tri_steps(share)
+        block = (row_devices, tiles, each, count, LANES)
+        return pl.BlockSpec(block, lambda i: (0, 0, i, 0, 0)), shape_of(shape, BF)
 
     def tri_block(tiles, extra=0):
         if direct:
@@ -980,7 +983,7 @@
     weights_col = weights_col.reshape(residues, heads * count)
     (tri,) = pair_call(
         functools.partial(tri_kernel, dims), tri_steps(share), chain_specs + [tri_block(6, extra)[0]],
-        [tri_block(3)], [chain_col, chain_row, acts], free=(2,),
+        [tri_out(3)], [chain_col, chain_row, acts], free=(2,),
         flops=2 * product, moved=share * residues * 9 * 256,
     )
     tri_rows = to_rows(tri)
@@ -1001,7 +1004,7 @@
     ]
     part_up, part_z = expand // row_devices, 2 * hidden // row_devices
     half_rows = part_up + part_up // 2
-    carried = 2 * half_rows if direct else 0
+    carried = 2 * part_up + part_z if direct else 0
     acc_shapes = [
         (expand, width_z), (expand, width_z), (2 * hidden, width_z),
         ((2 * hidden + width_z) // LANES, LANES),
@@ -1026,9 +1029,9 @@
     else:
         turned = g_up_t.reshape(-1, LANES, LANES).transpose(0, 2, 1)
         parts = [g.reshape(row_devices, -1, LANES) for g in (g_down, turned, g_z)]
-        spare = jnp.zeros((row_devices, part_up - part_z, LANES), F32)
-        grad_parts = swap(jnp.concatenate(parts + [spare], axis=1).astype(BF))
+        grad_parts = swap(jnp.concatenate(parts, axis=1).astype(BF))
     row_sum = jnp.sum(grad_parts.astype(F32), axis=0)
+    row_sum = jnp.pad(row_sum, ((0, 2 * half_rows - row_sum.shape[0]), (0, 0)))
     lower, upper = row_sum[:half_rows], row_sum[half_rows:]
     low_crop = crop_index == 0
     theirs = lax.ppermute(jnp.where(low_crop, upper, lower), "crop", [(0, 1), (1, 0)])
@@ -1036,7 +1039,7 @@
     (dacts,) = pair_call(
         functools.partial(tri_back_kernel, dims), tri_steps(share),
         chain_specs + [tri_block(6, extra)[0], tri_block(3, carried)[0]],
-        [tri_block(6)], [chain_col, chain_row, acts, dtri], free=(2,),
+        [tri_out(6)], [chain_col, chain_row, acts, dtri], free=(2,),
         flops=4 * product, moved=share * residues * 15 * 256,
     )
     dacts_rows = after(to_rows(dacts), pair_own)

time: 427 us -> 424 us (level)
    all_to_all x5 -> x4, waiting for transfers between devices: 24.4 us -> 19 us  [same_core_exchange(): lax.all_to_all(block, BOTH, split_axis=0, concat_axis=0, tiled=True, axis...]
    all_to_all x5 -> x4, starting transfers between devices: 39.7 us -> 34.4 us  [same_core_exchange(): lax.all_to_all(block, BOTH, split_axis=0, concat_axis=0, tiled=True, axis...]
    all_to_all x0 -> x1, waiting for transfers between devices: none -> 5.02 us  [shards(): lax.all_to_all(gated_own, BOTH, split_axis=0, concat_axis=0, tiled=True)]
  transfers between devices with their start and end apart: 14 -> 13, of which waited for: 11 -> 11; matrix products, arithmetic and copies ran while one was open for 8% -> 8% of each run, Pallas kernels for 6% -> 6%
where the time goes in v5:
time: 424 us; the launch traced here: 423 us
  waiting for transfers between devices  165 us (39%)
  Pallas kernels  101 us (24%)
  starting transfers between devices  63.5 us (15%)
  blocking collectives  53.1 us (13%)
  other arithmetic  20 us (5%)
  local copies, waits for them, and re-layouts  19.1 us (5%)
    all_to_all x3, waiting for transfers between devices, swap(): return lax.all_to_all(block, 'row', split_axis=0, concat_axis=0, tiled=True)  132 us
    pallas_call x14, Pallas kernels, pair_call(): pl.pallas_call(kernel, grid=(steps,), in_specs=ins, out_specs=[spec for s...  101 us
    all_to_all x1, blocking collectives, swap(): return lax.all_to_all(block, 'row', split_axis=0, concat_axis=0, tiled=True)  53.1 us
    all_to_all x4, starting transfers between devices, same_core_exchange(): lax.all_to_all(block, BOTH, split_axis=0, concat_axis=0, tiled=True, axis...  34.4 us
    all_to_all x3, starting transfers between devices, swap(): return lax.all_to_all(block, 'row', split_axis=0, concat_axis=0, tiled=True)  24.2 us
    all_to_all x4, waiting for transfers between devices, same_core_exchange(): lax.all_to_all(block, BOTH, split_axis=0, concat_axis=0, tiled=True, axis...  19 us
  transfers between devices with their start and end apart: 13, of which 11 were waited for; matrix products, arithmetic and copies ran while one was open for 8% of the time, Pallas kernels for 6%

profile of v5, /device:TPU:0, one launch (start us, length us, event | category | flops | bytes accessed | tf_op | source)
XLA Modules:
  0.0 422.9 jit_solution(5750679406094627127)
XLA Ops:
  2.3 8.4 %all-to-all-start = ((bf16[16,16,512]{2,1,0:T(8,128)(2,1)}), bf16[16,16,512]{2,1,0:T(8,128)(2,1)}, u32[]{:S(2)}, u32[]{:S(2)}) async-start(bf16[16,16,512]{2,1,0:T(8,128)(2,1)} %broadcast_in_dim.8), calls=%async_computation | async-start | bytes 524288 | tf_op jit(solution)/shard_map/all_to_all | solution.py:44
  25.1 3.9 all-to-all-start.1
  34.4 5.0 %all-to-all-done.1 = bf16[32,16,256]{2,1,0:T(8,128)(2,1)S(1)} async-done(((bf16[32,16,256]{2,1,0:T(8,128)(2,1)}), bf16[32,16,256]{2,1,0:T(8,128)(2,1)S(1)}, u32[]{:S(2)}, u32[]{:S(2)}) %all-to-all-start.1) | async-done | bytes 262176 | tf_op jit(solution)/shard_map/all_to_all | solution.py:903
  39.4 4.6 %shard_map.701 = (f32[512,256]{1,0:T(8,128)}, f32[512,256]{1,0:T(8,128)}, bf16[512,64]{1,0:T(8,128)(2,1)S(1)}, bf16[32,256]{1,0:T(8,128)(2,1)S(1)}) custom-call(bf16[512,512]{1,0:T(8,128)(2,1)S(1)} %bitcast.90, bf16[512,256]{1,0:T(8,128)(2,1)S(1)} %bitcast.97, f32[1,256]{1,0:T(1,128)S(1)} %bitcast.106, f32[1,256]{1,0:T(1,128)S(1)} %bitcast.104, ...), custom_call_target="tpu_custom_call" | custom-call | flops 603979776 | bytes 4032512 | tf_op jit(solution)/shard_map/pallas_call | solution.py:806
  44.9 9.6 %shard_map.702 = (f32[16,128,256]{2,1,0:T(8,128)}, bf16[16,784,128]{2,1,0:T(8,128)(2,1)}) custom-call(bf16[16,128,256]{2,1,0:T(8,128)(2,1)} %get-tuple-element.121.xt_ref, bf16[16,32,128]{2,1,0:T(8,128)(2,1)} %bitcast.117, bf16[32,256]{1,0:T(8,128)(2,1)} %copy-done.20, f32[16,1,256]{2,1,0:T(1,128)} %copy-done.13, f32[128,1]{1,0:T(8,128)} %copy.110.gain_ref.gx_ref, ...), custom_call_target="tpu_custom_call" | custom-call | flops 1073741824 | bytes 6291456 | tf_op jit(solution)/shard_map/pallas_call | solution.py:806
  54.5 3.9 all-to-all-start.2
  66.9 51.9 %all-to-all-done.2.acts_ref = bf16[16,784,128]{2,1,0:T(8,128)(2,1)S(1)} async-done(((bf16[16,784,128]{2,1,0:T(8,128)(2,1)}), bf16[16,784,128]{2,1,0:T(8,128)(2,1)S(1)}, u32[]{:S(2)}, u32[]{:S(2)}) %all-to-all-start.2) | async-done | bytes 3211296 | tf_op jit(solution)/shard_map/all_to_all | solution.py:930
  118.9 4.3 %shard_map.703 = bf16[16,3,8,16,128]{4,3,2,1,0:T(8,128)(2,1)} custom-call(s32[256,1]{1,0:T(8,128)} %copy.112.col_ref, s32[1,256]{1,0:T(1,128)} %row_ref.3, bf16[16,784,128]{2,1,0:T(8,128)(2,1)S(1)} %all-to-all-done.2.acts_ref), custom_call_target="tpu_custom_call" | custom-call | flops 536870912 | bytes 4718592 | tf_op jit(solution)/shard_map/pallas_call | solution.py:806
  123.2 15.9 %all-to-all-start.3 = ((bf16[16,384,128]{2,1,0:T(8,128)(2,1)}), bf16[16,384,128]{2,1,0:T(8,128)(2,1)}, u32[]{:S(2)}, u32[]{:S(2)}) async-start(bf16[16,384,128]{2,1,0:T(8,128)(2,1)} %bitcast.110), calls=%async_computation.3 | async-start | bytes 3145728 | tf_op jit(solution)/shard_map/all_to_all | solution.py:930
  144.5 26.6 %all-to-all-done.3.tri_ref = bf16[16,384,128]{2,1,0:T(8,128)(2,1)} async-done(((bf16[16,384,128]{2,1,0:T(8,128)(2,1)}), bf16[16,384,128]{2,1,0:T(8,128)(2,1)}, u32[]{:S(2)}, u32[]{:S(2)}) %all-to-all-start.3) | async-done | bytes 1572896 | tf_op jit(solution)/shard_map/all_to_all | solution.py:930
  171.1 22.6 %shard_map.704 = (bf16[16,256,128]{2,1,0:T(8,128)(2,1)}, f32[16,128,256]{2,1,0:T(8,128)}, bf16[16,128,256]{2,1,0:T(8,128)(2,1)}, bf16[16,464,128]{2,1,0:T(8,128)...) custom-call(f32[16,128,256]{2,1,0:T(8,128)} %get-tuple-element.129.sum_ref, ...), custom_call_target="tpu_custom_call" | custom-call | flops 3221225472 | bytes 10485760 | tf_op jit(solution)/shard_map/pallas_call | solution.py:806
  193.7 53.1 %all_to_all.45.grad_ref = bf16[16,464,128]{2,1,0:T(8,128)(2,1)} all-to-all(bf16[16,464,128]{2,1,0:T(8,128)(2,1)} %get-tuple-element.134), channel_id=1, replica_groups=mesh['crop'=2,'row'=16] {'row'}, dimensions={0} | all-to-all | bytes 3801088 | tf_op jit(solution)/shard_map/all_to_all | solution.py:930
  246.8 6.0 %shard_map.705 = bf16[16,6,8,16,128]{4,3,2,1,0:T(8,128)(2,1)} custom-call(s32[256,1]{1,0:T(8,128)} %copy.112.col_ref, s32[1,256]{1,0:T(1,128)} %row_ref.3, bf16[16,784,128]{2,1,0:T(8,128)(2,1)S(1)} %all-to-all-done.2.acts_ref, bf16[16,464,128]{2,1,0:T(8,128)(2,1)} %all_to_all.45.grad_ref), custom_call_target="tpu_custom_call" | custom-call | flops 1073741824 | bytes 7864320 | tf_op jit(solution)/shard_map/pallas_call | solution.py:806
  252.8 4.5 %all-to-all-start.5 = ((bf16[16,768,128]{2,1,0:T(8,128)(2,1)}), bf16[16,768,128]{2,1,0:T(8,128)(2,1)}, u32[]{:S(2)}, u32[]{:S(2)}) async-start(bf16[16,768,128]{2,1,0:T(8,128)(2,1)} %bitcast.109), calls=%async_computation.5 | async-start | bytes 6291456 | tf_op jit(solution)/shard_map/all_to_all | solution.py:930
  262.9 53.8 %all-to-all-done.5.acts_ref = bf16[16,768,128]{2,1,0:T(8,128)(2,1)} async-done(((bf16[16,768,128]{2,1,0:T(8,128)(2,1)}), bf16[16,768,128]{2,1,0:T(8,128)(2,1)}, u32[]{:S(2)}, u32[]{:S(2)}) %all-to-all-start.5) | async-done | bytes 3145760 | tf_op jit(solution)/shard_map/all_to_all | solution.py:930
  316.7 16.5 %shard_map.706 = (f32[16,128,256]{2,1,0:T(8,128)}, bf16[16,128,128]{2,1,0:T(8,128)(2,1)}, bf16[2560,128]{1,0:T(8,128)(2,1)}, f32[1,128]{1,0:T(1,128)}) custom-call(f32[16,128,256]{2,1,0:T(8,128)} %get-tuple-element.129.sum_ref, bf16[16,768,128]{2,1,0:T(8,128)(2,1)} %all-to-all-done.5.acts_ref, f32[16,128,256]{2,1,0:T(8,128)} %get-tuple-element.136.ds_ref, ...), custom_call_target="tpu_custom_call" | custom-call | flops 3623878656 | bytes 10485760 | tf_op jit(solution)/shard_map/pallas_call | solution.py:806
  333.2 15.7 %all-to-all-start.6 = ((bf16[16,128,128]{2,1,0:T(8,128)(2,1)}), bf16[16,128,128]{2,1,0:T(8,128)(2,1)}, u32[]{:S(2)}, u32[]{:S(2)}) async-start(bf16[16,128,128]{2,1,0:T(8,128)(2,1)} %get-tuple-element.139), calls=%async_computation.6 | async-start | bytes 1048576 | tf_op jit(solution)/shard_map/all_to_all | solution.py:44
  353.6 10.9 %all-to-all-done.6 = bf16[16,128,128]{2,1,0:T(8,128)(2,1)} async-done(((bf16[16,128,128]{2,1,0:T(8,128)(2,1)}), bf16[16,128,128]{2,1,0:T(8,128)(2,1)}, u32[]{:S(2)}, u32[]{:S(2)}) %all-to-all-start.6) | async-done | bytes 524320 | tf_op jit(solution)/shard_map/all_to_all | solution.py:44
  371.2 8.6 %shard_map.707 = (f32[64,256]{1,0:T(8,128)}, f32[1024,256]{1,0:T(8,128)}, f32[256,1024]{1,0:T(8,128)}, f32[256,256]{1,0:T(8,128)}, f32[1,256]{1,0:T(1,128)}, /*i...) custom-call(bf16[32,128,128]{2,1,0:T(8,128)(2,1)S(1)} %bitcast.93, ...), custom_call_target="tpu_custom_call" | custom-call | flops 1677721600 | bytes 7737344 | tf_op jit(solution)/shard_map/pallas_call | solution.py:806
  382.5 6.7 %all-to-all-start.8 = ((bf16[16,192,128]{2,1,0:T(8,128)(2,1)}), bf16[16,192,128]{2,1,0:T(8,128)(2,1)S(1)}, u32[]{:S(2)}, u32[]{:S(2)}) async-start(bf16[16,192,128]{2,1,0:T(8,128)(2,1)} %shard_map.710), calls=%async_computation.8 | async-start | bytes 1572864 | tf_op jit(solution)/shard_map/all_to_all | solution.py:44
  390.5 8.4 %shard_map.711 = (f32[256,256]{1,0:T(8,128)}, f32[256,256]{1,0:T(8,128)}, f32[256,256]{1,0:T(8,128)}, f32[256,1024]{1,0:T(8,128)}, f32[256,1024]{1,0:T(8,128)}, ...) custom-call(f32[256,256]{1,0:T(8,128)} %refs_0_.1, ...), custom_call_target="tpu_custom_call" | custom-call | bytes 24084480 | tf_op jit(solution)/shard_map/pallas_call | solution.py:806
  398.9 5.1 %shard_map.709 = f32[16,256,128]{2,1,0:T(8,128)} custom-call(bf16[16,128,256]{2,1,0:T(8,128)(2,1)} %get-tuple-element.121.xt_ref, f32[16,128,256]{2,1,0:T(8,128)} %get-tuple-element.138.fg_ref, bf16[16,8,256]{2,1,0:T(8,128)(2,1)} %bitcast.99, f32[128,1]{1,0:T(8,128)} %copy-done.5, bf16[128,8]{1,0:T(8,128)(2,1)} %copy-done.30), custom_call_target="tpu_custom_call" | custom-call | flops 16777216 | bytes 5242880 | tf_op jit(solution)/shard_map/pallas_call | solution.py:806
  404.0 6.1 %all-to-all-done.8 = bf16[16,192,128]{2,1,0:T(8,128)(2,1)S(1)} async-done(((bf16[16,192,128]{2,1,0:T(8,128)(2,1)}), bf16[16,192,128]{2,1,0:T(8,128)(2,1)S(1)}, u32[]{:S(2)}, u32[]{:S(2)}) %all-to-all-start.8) | async-done | bytes 786464 | tf_op jit(solution)/shard_map/all_to_all | solution.py:44
  414.0 8.7 %shard_map.712 = (f32[256,1024]{1,0:T(8,128)}, f32[256,1024]{1,0:T(8,128)}, f32[256,1024]{1,0:T(8,128)}, f32[1024,128]{1,0:T(8,128)}, f32[1024,128]{1,0:T(8,128)...) custom-call(bf16[512,256]{1,0:T(8,128)(2,1)} %get-tuple-element.150., ...), custom_call_target="tpu_custom_call" | custom-call | flops 536870912 | bytes 11354112 | tf_op jit(solution)/shard_map/pallas_call | solution.py:806
  (152 shorter events, 60.6 us)
Async XLA Ops:
  2.3 18.3 %all-to-all-start = ((bf16[16,16,512]{2,1,0:T(8,128)(2,1)}), bf16[16,16,512]{2,1,0:T(8,128)(2,1)}, u32[]{:S(2)}, u32[]{:S(2)}) async-start(bf16[16,16,512]{2,1,0:T(8,128)(2,1)} %broadcast_in_dim.8), calls=%async_computation | async-start | bytes 524288 | tf_op jit(solution)/shard_map/all_to_all | solution.py:44
  14.0 25.4 %copy-start.10 = (bf16[256,256]{1,0:T(8,128)(2,1)}, bf16[256,256]{1,0:T(8,128)(2,1)S(1)}, u32[]{:S(2)}) copy-start(bf16[256,256]{1,0:T(8,128)(2,1)S(1)} %convert_element_type.70.wo_ref) | copy-start | bytes 393220
  14.2 25.2 %copy-start.6 = (bf16[256,1024]{1,0:T(8,128)(2,1)}, bf16[256,1024]{1,0:T(8,128)(2,1)S(1)}, u32[]{:S(2)}) copy-start(bf16[256,1024]{1,0:T(8,128)(2,1)S(1)} %convert_element_type.71.wu_ref) | copy-start | bytes 1572868
  15.9 23.4 %copy-start.7 = (bf16[1024,256]{1,0:T(8,128)(2,1)}, bf16[1024,256]{1,0:T(8,128)(2,1)S(1)}, u32[]{:S(2)}) copy-start(bf16[1024,256]{1,0:T(8,128)(2,1)S(1)} %convert_element_type.72.wd_ref) | copy-start | bytes 1572868
  20.6 1.7 collective-permute-start
  20.8 18.6 %copy-start.17 = (f32[256]{0:T(256)}, f32[256]{0:T(256)S(1)}, u32[]{:S(2)}) copy-start(f32[256]{0:T(256)S(1)} %get-tuple-element.292) | copy-start | bytes 3076
  20.8 18.6 %copy-start.18 = (f32[256]{0:T(256)}, f32[256]{0:T(256)S(1)}, u32[]{:S(2)}) copy-start(f32[256]{0:T(256)S(1)} %get-tuple-element.293) | copy-start | bytes 3076
  23.4 16.0 %copy-start.1 = (bf16[16,2,16,512]{3,2,1,0:T(8,128)(2,1)}, bf16[16,2,16,512]{3,2,1,0:T(8,128)(2,1)S(1)}, u32[]{:S(2)}) copy-start(bf16[16,2,16,512]{3,2,1,0:T(8,128)(2,1)S(1)} %pad_maximum_fusion.2) | copy-start | bytes 1572868
  25.1 14.2 %all-to-all-start.1 = ((bf16[32,16,256]{2,1,0:T(8,128)(2,1)}), bf16[32,16,256]{2,1,0:T(8,128)(2,1)S(1)}, u32[]{:S(2)}, u32[]{:S(2)}) async-start(bf16[32,16,256]{2,1,0:T(8,128)(2,1)} %get-tuple-element.124), calls=%async_computation.1 | async-start | bytes 524288 | tf_op jit(solution)/shard_map/all_to_all | solution.py:903
  39.4 15.2 %copy-start.9 = (bf16[32,16,256]{2,1,0:T(8,128)(2,1)}, bf16[32,16,256]{2,1,0:T(8,128)(2,1)S(1)}, u32[]{:S(2)}) copy-start(bf16[32,16,256]{2,1,0:T(8,128)(2,1)S(1)} %all-to-all-done.1) | copy-start | bytes 786436
  54.5 64.3 %all-to-all-start.2 = ((bf16[16,784,128]{2,1,0:T(8,128)(2,1)}), bf16[16,784,128]{2,1,0:T(8,128)(2,1)S(1)}, u32[]{:S(2)}, u32[]{:S(2)}) async-start(bf16[16,784,128]{2,1,0:T(8,128)(2,1)} %get-tuple-element.130), calls=%async_computation.2 | async-start | bytes 6422528 | tf_op jit(solution)/shard_map/all_to_all | solution.py:930
  123.2 15.9 %copy-start.32 = (bf16[128,256]{0,1:T(8,128)(2,1)S(1)}, bf16[128,256]{0,1:T(8,128)(2,1)}, u32[]{:S(2)}) copy-start(bf16[128,256]{0,1:T(8,128)(2,1)} %convert_bitcast_fusion.2) | copy-start | bytes 196612
  123.2 16.6 %copy-start.36 = (f32[128,1]{0,1:T(1,128)S(1)}, f32[128,1]{0,1:T(1,128)}, u32[]{:S(2)}) copy-start(f32[128,1]{0,1:T(1,128)} %get-tuple-element.288) | copy-start | bytes 1540
  123.2 19.0 %copy-start.29 = (bf16[512,128]{0,1:T(8,128)(2,1)S(1)}, bf16[512,128]{0,1:T(8,128)(2,1)}, u32[]{:S(2)}) copy-start(bf16[512,128]{0,1:T(8,128)(2,1)} %convert_bitcast_fusion.1) | copy-start | bytes 393220
  123.2 20.6 %slice-start = ((bf16[1152,128]{0,1:T(8,128)(2,1)}), bf16[128,128]{0,1:T(8,128)(2,1)S(1)}, s32[]{:S(2)}) async-start(bf16[1152,128]{0,1:T(8,128)(2,1)} %copy-done.26), calls=%async_computation.9 | async-start | bytes 65536 | tf_op jit(solution)/shard_map/slice | solution.py:1002
  123.2 47.9 %all-to-all-start.3 = ((bf16[16,384,128]{2,1,0:T(8,128)(2,1)}), bf16[16,384,128]{2,1,0:T(8,128)(2,1)}, u32[]{:S(2)}, u32[]{:S(2)}) async-start(bf16[16,384,128]{2,1,0:T(8,128)(2,1)} %bitcast.110), calls=%async_computation.3 | async-start | bytes 3145728 | tf_op jit(solution)/shard_map/all_to_all | solution.py:930
  252.8 63.8 %all-to-all-start.5 = ((bf16[16,768,128]{2,1,0:T(8,128)(2,1)}), bf16[16,768,128]{2,1,0:T(8,128)(2,1)}, u32[]{:S(2)}, u32[]{:S(2)}) async-start(bf16[16,768,128]{2,1,0:T(8,128)(2,1)} %bitcast.109), calls=%async_computation.5 | async-start | bytes 6291456 | tf_op jit(solution)/shard_map/all_to_all | solution.py:930
  258.4 3.9 collective-permute-start.1
  333.2 31.3 %all-to-all-start.6 = ((bf16[16,128,128]{2,1,0:T(8,128)(2,1)}), bf16[16,128,128]{2,1,0:T(8,128)(2,1)}, u32[]{:S(2)}, u32[]{:S(2)}) async-start(bf16[16,128,128]{2,1,0:T(8,128)(2,1)} %get-tuple-element.139), calls=%async_computation.6 | async-start | bytes 1048576 | tf_op jit(solution)/shard_map/all_to_all | solution.py:44
  350.0 1.7 collective-permute-start.2
  364.5 5.1 %collective-permute-start.3 = (bf16[16,128,128]{2,1,0:T(8,128)(2,1)}, bf16[16,128,128]{2,1,0:T(8,128)(2,1)}, u32[]{:S(2)}, u32[]{:S(2)}) collective-permute-start(bf16[16,128,128]{2,1,0:T(8,128)(2,1)} %all-to-all-done.6), channel_id=1, source_target_pairs={{0,1},{1,0},{2,3},{3,2},{4,5},{5,4},{6,7},{7,6},{8,9},{9,8},{10,11... | collective-permute-start | bytes 1572872 | tf_op jit(solution)/shard_map/ppermute | solution.py:50
  365.9 15.6 %all-to-all-start.7 = ((bf16[16,80,128]{2,1,0:T(8,128)(2,1)}), bf16[16,80,128]{2,1,0:T(8,128)(2,1)S(1)}, u32[]{:S(2)}, u32[]{:S(2)}) async-start(bf16[16,80,128]{2,1,0:T(8,128)(2,1)} %bitcast.114), calls=%async_computation.7 | async-start | bytes 655360 | tf_op jit(solution)/shard_map/all_to_all | solution.py:44
  382.5 27.5 %all-to-all-start.8 = ((bf16[16,192,128]{2,1,0:T(8,128)(2,1)}), bf16[16,192,128]{2,1,0:T(8,128)(2,1)S(1)}, u32[]{:S(2)}, u32[]{:S(2)}) async-start(bf16[16,192,128]{2,1,0:T(8,128)(2,1)} %shard_map.710), calls=%async_computation.8 | async-start | bytes 1572864 | tf_op jit(solution)/shard_map/all_to_all | solution.py:44
  410.0 2.3 collective-permute-start.4
  (27 other events, 172.4 us)

commit v6 on v5

--- a/solution.py
+++ b/solution.py
@@ -983,7 +983,7 @@
     weights_col = weights_col.reshape(residues, heads * count)
     (tri,) = pair_call(
         functools.partial(tri_kernel, dims), tri_steps(share), chain_specs + [tri_block(6, extra)[0]],
-        [tri_out(3)], [chain_col, chain_row, acts], free=(2,),
+        [tri_out(3)], [chain_col, chain_row, acts], free=(0, 1, 2),
         flops=2 * product, moved=share * residues * 9 * 256,
     )
     tri_rows = to_rows(tri)
@@ -1039,7 +1039,7 @@
     (dacts,) = pair_call(
         functools.partial(tri_back_kernel, dims), tri_steps(share),
         chain_specs + [tri_block(6, extra)[0], tri_block(3, carried)[0]],
-        [tri_out(6)], [chain_col, chain_row, acts, dtri], free=(2,),
+        [tri_out(6)], [chain_col, chain_row, acts, dtri], free=(0, 1, 2, 3),
         flops=4 * product, moved=share * residues * 15 * 256,
     )
     dacts_rows = after(to_rows(dacts), pair_own)

time: 424 us -> 423 us (level)
  no operation moved by 1% of the time
where the time goes in v6:
time: 423 us; the launch traced here: 421 us
  waiting for transfers between devices  164 us (39%)
  Pallas kernels  98 us (23%)
  starting transfers between devices  63.5 us (15%)
  blocking collectives  53 us (13%)
  local copies, waits for them, and re-layouts  20.9 us (5%)
  other arithmetic  20.1 us (5%)
    all_to_all x3, waiting for transfers between devices, swap(): return lax.all_to_all(block, 'row', split_axis=0, concat_axis=0, tiled=True)  132 us
    pallas_call x14, Pallas kernels, pair_call(): pl.pallas_call(kernel, grid=(steps,), in_specs=ins, out_specs=[spec for s...  98 us
    all_to_all x1, blocking collectives, swap(): return lax.all_to_all(block, 'row', split_axis=0, concat_axis=0, tiled=True)  53 us
    all_to_all x4, starting transfers between devices, same_core_exchange(): lax.all_to_all(block, BOTH, split_axis=0, concat_axis=0, tiled=True, axis...  34.4 us
    all_to_all x3, starting transfers between devices, swap(): return lax.all_to_all(block, 'row', split_axis=0, concat_axis=0, tiled=True)  24.2 us
    all_to_all x4, waiting for transfers between devices, same_core_exchange(): lax.all_to_all(block, BOTH, split_axis=0, concat_axis=0, tiled=True, axis...  19 us
  transfers between devices with their start and end apart: 13, of which 11 were waited for; matrix products, arithmetic and copies ran while one was open for 8% of the time, Pallas kernels for 6%

profile of v6, /device:TPU:0, one launch (start us, length us, event | category | flops | bytes accessed | tf_op | source)
XLA Modules:
  0.0 421.2 jit_solution(6391841855644322465)
XLA Ops:
  2.3 8.4 %all-to-all-start = ((bf16[16,16,512]{2,1,0:T(8,128)(2,1)}), bf16[16,16,512]{2,1,0:T(8,128)(2,1)}, u32[]{:S(2)}, u32[]{:S(2)}) async-start(bf16[16,16,512]{2,1,0:T(8,128)(2,1)} %broadcast_in_dim.8), calls=%async_computation | async-start | bytes 524288 | tf_op jit(solution)/shard_map/all_to_all | solution.py:44
  26.1 3.9 all-to-all-start.1
  35.3 5.0 %all-to-all-done.1 = bf16[32,16,256]{2,1,0:T(8,128)(2,1)S(1)} async-done(((bf16[32,16,256]{2,1,0:T(8,128)(2,1)}), bf16[32,16,256]{2,1,0:T(8,128)(2,1)S(1)}, u32[]{:S(2)}, u32[]{:S(2)}) %all-to-all-start.1) | async-done | bytes 262176 | tf_op jit(solution)/shard_map/all_to_all | solution.py:903
  40.4 4.6 %shard_map.701 = (f32[512,256]{1,0:T(8,128)}, f32[512,256]{1,0:T(8,128)}, bf16[512,64]{1,0:T(8,128)(2,1)S(1)}, bf16[32,256]{1,0:T(8,128)(2,1)S(1)}) custom-call(bf16[512,512]{1,0:T(8,128)(2,1)S(1)} %bitcast.90, bf16[512,256]{1,0:T(8,128)(2,1)S(1)} %bitcast.97, f32[1,256]{1,0:T(1,128)S(1)} %bitcast.108, f32[1,256]{1,0:T(1,128)S(1)} %bitcast.106, ...), custom_call_target="tpu_custom_call" | custom-call | flops 603979776 | bytes 4032512 | tf_op jit(solution)/shard_map/pallas_call | solution.py:806
  45.8 9.6 %shard_map.702 = (f32[16,128,256]{2,1,0:T(8,128)}, bf16[16,784,128]{2,1,0:T(8,128)(2,1)}) custom-call(bf16[16,128,256]{2,1,0:T(8,128)(2,1)} %get-tuple-element.121.xt_ref, bf16[16,32,128]{2,1,0:T(8,128)(2,1)} %bitcast.119, bf16[32,256]{1,0:T(8,128)(2,1)} %copy-done.23, f32[16,1,256]{2,1,0:T(1,128)} %copy-done.14, f32[128,1]{1,0:T(8,128)} %copy.110.gain_ref.gx_ref, ...), custom_call_target="tpu_custom_call" | custom-call | flops 1073741824 | bytes 6291456 | tf_op jit(solution)/shard_map/pallas_call | solution.py:806
  55.5 3.9 all-to-all-start.2
  67.3 52.5 %all-to-all-done.2.acts_ref = bf16[16,784,128]{2,1,0:T(8,128)(2,1)S(1)} async-done(((bf16[16,784,128]{2,1,0:T(8,128)(2,1)}), bf16[16,784,128]{2,1,0:T(8,128)(2,1)S(1)}, u32[]{:S(2)}, u32[]{:S(2)}) %all-to-all-start.2) | async-done | bytes 3211296 | tf_op jit(solution)/shard_map/all_to_all | solution.py:930
  123.2 15.9 %all-to-all-start.3 = ((bf16[16,384,128]{2,1,0:T(8,128)(2,1)}), bf16[16,384,128]{2,1,0:T(8,128)(2,1)}, u32[]{:S(2)}, u32[]{:S(2)}) async-start(bf16[16,384,128]{2,1,0:T(8,128)(2,1)} %bitcast.112), calls=%async_computation.3 | async-start | bytes 3145728 | tf_op jit(solution)/shard_map/all_to_all | solution.py:930
  145.5 25.7 %all-to-all-done.3.tri_ref = bf16[16,384,128]{2,1,0:T(8,128)(2,1)} async-done(((bf16[16,384,128]{2,1,0:T(8,128)(2,1)}), bf16[16,384,128]{2,1,0:T(8,128)(2,1)}, u32[]{:S(2)}, u32[]{:S(2)}) %all-to-all-start.3) | async-done | bytes 1572896 | tf_op jit(solution)/shard_map/all_to_all | solution.py:930
  171.1 22.6 %shard_map.704 = (bf16[16,256,128]{2,1,0:T(8,128)(2,1)}, f32[16,128,256]{2,1,0:T(8,128)}, bf16[16,128,256]{2,1,0:T(8,128)(2,1)}, bf16[16,464,128]{2,1,0:T(8,128)...) custom-call(f32[16,128,256]{2,1,0:T(8,128)} %get-tuple-element.129.sum_ref, ...), custom_call_target="tpu_custom_call" | custom-call | flops 3221225472 | bytes 10485760 | tf_op jit(solution)/shard_map/pallas_call | solution.py:806
  193.8 53.0 %all_to_all.45.grad_ref = bf16[16,464,128]{2,1,0:T(8,128)(2,1)S(1)} all-to-all(bf16[16,464,128]{2,1,0:T(8,128)(2,1)} %get-tuple-element.134), channel_id=1, replica_groups=mesh['crop'=2,'row'=16] {'row'}, dimensions={0} | all-to-all | bytes 3801088 | tf_op jit(solution)/shard_map/all_to_all | solution.py:930
  246.8 4.4 %shard_map.705 = bf16[16,6,8,16,128]{4,3,2,1,0:T(8,128)(2,1)} custom-call(s32[256,1]{1,0:T(8,128)S(1)} %copy.112.col_ref, s32[1,256]{1,0:T(1,128)S(1)} %copy-done.17, bf16[16,784,128]{2,1,0:T(8,128)(2,1)S(1)} %all-to-all-done.2.acts_ref, bf16[16,464,128]{2,1,0:T(8,128)(2,1)S(1)} %all_to_all.45.grad_ref), custom_call_target="tpu_custom_call" | custom-call | flops 1073741824 | bytes 7864320 | tf_op jit(solution)/shard_map/pallas_call | solution.py:806
  251.1 4.5 %all-to-all-start.5 = ((bf16[16,768,128]{2,1,0:T(8,128)(2,1)}), bf16[16,768,128]{2,1,0:T(8,128)(2,1)}, u32[]{:S(2)}, u32[]{:S(2)}) async-start(bf16[16,768,128]{2,1,0:T(8,128)(2,1)} %bitcast.111), calls=%async_computation.5 | async-start | bytes 6291456 | tf_op jit(solution)/shard_map/all_to_all | solution.py:930
  261.2 53.8 %all-to-all-done.5.acts_ref = bf16[16,768,128]{2,1,0:T(8,128)(2,1)} async-done(((bf16[16,768,128]{2,1,0:T(8,128)(2,1)}), bf16[16,768,128]{2,1,0:T(8,128)(2,1)}, u32[]{:S(2)}, u32[]{:S(2)}) %all-to-all-start.5) | async-done | bytes 3145760 | tf_op jit(solution)/shard_map/all_to_all | solution.py:930
  315.0 16.5 %shard_map.706 = (f32[16,128,256]{2,1,0:T(8,128)}, bf16[16,128,128]{2,1,0:T(8,128)(2,1)}, bf16[2560,128]{1,0:T(8,128)(2,1)}, f32[1,128]{1,0:T(1,128)}) custom-call(f32[16,128,256]{2,1,0:T(8,128)} %get-tuple-element.129.sum_ref, bf16[16,768,128]{2,1,0:T(8,128)(2,1)} %all-to-all-done.5.acts_ref, f32[16,128,256]{2,1,0:T(8,128)} %get-tuple-element.136.ds_ref, ...), custom_call_target="tpu_custom_call" | custom-call | flops 3623878656 | bytes 10485760 | tf_op jit(solution)/shard_map/pallas_call | solution.py:806
  331.5 15.7 %all-to-all-start.6 = ((bf16[16,128,128]{2,1,0:T(8,128)(2,1)}), bf16[16,128,128]{2,1,0:T(8,128)(2,1)}, u32[]{:S(2)}, u32[]{:S(2)}) async-start(bf16[16,128,128]{2,1,0:T(8,128)(2,1)} %get-tuple-element.139), calls=%async_computation.6 | async-start | bytes 1048576 | tf_op jit(solution)/shard_map/all_to_all | solution.py:44
  351.9 10.9 %all-to-all-done.6 = bf16[16,128,128]{2,1,0:T(8,128)(2,1)} async-done(((bf16[16,128,128]{2,1,0:T(8,128)(2,1)}), bf16[16,128,128]{2,1,0:T(8,128)(2,1)}, u32[]{:S(2)}, u32[]{:S(2)}) %all-to-all-start.6) | async-done | bytes 524320 | tf_op jit(solution)/shard_map/all_to_all | solution.py:44
  364.2 3.8 all-to-all-start.7
  369.5 8.6 %shard_map.707 = (f32[64,256]{1,0:T(8,128)}, f32[1024,256]{1,0:T(8,128)}, f32[256,1024]{1,0:T(8,128)}, f32[256,256]{1,0:T(8,128)}, f32[1,256]{1,0:T(1,128)}, /*i...) custom-call(bf16[32,128,128]{2,1,0:T(8,128)(2,1)S(1)} %bitcast.93, ...), custom_call_target="tpu_custom_call" | custom-call | flops 1677721600 | bytes 7737344 | tf_op jit(solution)/shard_map/pallas_call | solution.py:806
  380.8 6.7 %all-to-all-start.8 = ((bf16[16,192,128]{2,1,0:T(8,128)(2,1)}), bf16[16,192,128]{2,1,0:T(8,128)(2,1)S(1)}, u32[]{:S(2)}, u32[]{:S(2)}) async-start(bf16[16,192,128]{2,1,0:T(8,128)(2,1)} %shard_map.710), calls=%async_computation.8 | async-start | bytes 1572864 | tf_op jit(solution)/shard_map/all_to_all | solution.py:44
  388.8 8.4 %shard_map.711 = (f32[256,256]{1,0:T(8,128)}, f32[256,256]{1,0:T(8,128)}, f32[256,256]{1,0:T(8,128)}, f32[256,1024]{1,0:T(8,128)}, f32[256,1024]{1,0:T(8,128)}, ...) custom-call(f32[256,256]{1,0:T(8,128)} %refs_0_.1, ...), custom_call_target="tpu_custom_call" | custom-call | bytes 24084480 | tf_op jit(solution)/shard_map/pallas_call | solution.py:806
  397.2 5.1 %shard_map.709 = f32[16,256,128]{2,1,0:T(8,128)} custom-call(bf16[16,128,256]{2,1,0:T(8,128)(2,1)} %get-tuple-element.121.xt_ref, f32[16,128,256]{2,1,0:T(8,128)} %get-tuple-element.138.fg_ref, bf16[16,8,256]{2,1,0:T(8,128)(2,1)} %bitcast.99, f32[128,1]{1,0:T(8,128)} %copy-done.6, bf16[128,8]{1,0:T(8,128)(2,1)} %copy-done.32), custom_call_target="tpu_custom_call" | custom-call | flops 16777216 | bytes 5242880 | tf_op jit(solution)/shard_map/pallas_call | solution.py:806
  402.3 6.1 %all-to-all-done.8 = bf16[16,192,128]{2,1,0:T(8,128)(2,1)S(1)} async-done(((bf16[16,192,128]{2,1,0:T(8,128)(2,1)}), bf16[16,192,128]{2,1,0:T(8,128)(2,1)S(1)}, u32[]{:S(2)}, u32[]{:S(2)}) %all-to-all-start.8) | async-done | bytes 786464 | tf_op jit(solution)/shard_map/all_to_all | solution.py:44
  412.3 8.7 %shard_map.712 = (f32[256,1024]{1,0:T(8,128)}, f32[256,1024]{1,0:T(8,128)}, f32[256,1024]{1,0:T(8,128)}, f32[1024,128]{1,0:T(8,128)}, f32[1024,128]{1,0:T(8,128)...) custom-call(bf16[512,256]{1,0:T(8,128)(2,1)} %get-tuple-element.150., ...), custom_call_target="tpu_custom_call" | custom-call | flops 536870912 | bytes 11354112 | tf_op jit(solution)/shard_map/pallas_call | solution.py:806
  (158 shorter events, 61.5 us)
Async XLA Ops:
  2.3 18.3 %all-to-all-start = ((bf16[16,16,512]{2,1,0:T(8,128)(2,1)}), bf16[16,16,512]{2,1,0:T(8,128)(2,1)}, u32[]{:S(2)}, u32[]{:S(2)}) async-start(bf16[16,16,512]{2,1,0:T(8,128)(2,1)} %broadcast_in_dim.8), calls=%async_computation | async-start | bytes 524288 | tf_op jit(solution)/shard_map/all_to_all | solution.py:44
  14.0 26.3 %copy-start.11 = (bf16[256,256]{1,0:T(8,128)(2,1)}, bf16[256,256]{1,0:T(8,128)(2,1)S(1)}, u32[]{:S(2)}) copy-start(bf16[256,256]{1,0:T(8,128)(2,1)S(1)} %convert_element_type.70.wo_ref) | copy-start | bytes 393220
  14.2 26.1 %copy-start.7 = (bf16[256,1024]{1,0:T(8,128)(2,1)}, bf16[256,1024]{1,0:T(8,128)(2,1)S(1)}, u32[]{:S(2)}) copy-start(bf16[256,1024]{1,0:T(8,128)(2,1)S(1)} %convert_element_type.71.wu_ref) | copy-start | bytes 1572868
  16.0 24.4 %copy-start.8 = (bf16[1024,256]{1,0:T(8,128)(2,1)}, bf16[1024,256]{1,0:T(8,128)(2,1)S(1)}, u32[]{:S(2)}) copy-start(bf16[1024,256]{1,0:T(8,128)(2,1)S(1)} %convert_element_type.72.wd_ref) | copy-start | bytes 1572868
  20.6 1.7 collective-permute-start
  21.3 19.0 %copy-start.20 = (f32[256]{0:T(256)}, f32[256]{0:T(256)S(1)}, u32[]{:S(2)}) copy-start(f32[256]{0:T(256)S(1)} %get-tuple-element.292) | copy-start | bytes 3076
  21.3 19.0 %copy-start.21 = (f32[256]{0:T(256)}, f32[256]{0:T(256)S(1)}, u32[]{:S(2)}) copy-start(f32[256]{0:T(256)S(1)} %get-tuple-element.293) | copy-start | bytes 3076
  23.4 16.9 %copy-start.2 = (bf16[16,2,16,512]{3,2,1,0:T(8,128)(2,1)}, bf16[16,2,16,512]{3,2,1,0:T(8,128)(2,1)S(1)}, u32[]{:S(2)}) copy-start(bf16[16,2,16,512]{3,2,1,0:T(8,128)(2,1)S(1)} %pad_maximum_fusion.2) | copy-start | bytes 1572868
  26.1 14.2 %all-to-all-start.1 = ((bf16[32,16,256]{2,1,0:T(8,128)(2,1)}), bf16[32,16,256]{2,1,0:T(8,128)(2,1)S(1)}, u32[]{:S(2)}, u32[]{:S(2)}) async-start(bf16[32,16,256]{2,1,0:T(8,128)(2,1)} %get-tuple-element.124), calls=%async_computation.1 | async-start | bytes 524288 | tf_op jit(solution)/shard_map/all_to_all | solution.py:903
  40.3 15.2 %copy-start.10 = (bf16[32,16,256]{2,1,0:T(8,128)(2,1)}, bf16[32,16,256]{2,1,0:T(8,128)(2,1)S(1)}, u32[]{:S(2)}) copy-start(bf16[32,16,256]{2,1,0:T(8,128)(2,1)S(1)} %all-to-all-done.1) | copy-start | bytes 786436
  55.5 64.3 %all-to-all-start.2 = ((bf16[16,784,128]{2,1,0:T(8,128)(2,1)}), bf16[16,784,128]{2,1,0:T(8,128)(2,1)S(1)}, u32[]{:S(2)}, u32[]{:S(2)}) async-start(bf16[16,784,128]{2,1,0:T(8,128)(2,1)} %get-tuple-element.130), calls=%async_computation.2 | async-start | bytes 6422528 | tf_op jit(solution)/shard_map/all_to_all | solution.py:930
  123.2 15.9 %copy-start.34 = (bf16[128,256]{0,1:T(8,128)(2,1)S(1)}, bf16[128,256]{0,1:T(8,128)(2,1)}, u32[]{:S(2)}) copy-start(bf16[128,256]{0,1:T(8,128)(2,1)} %convert_bitcast_fusion.2) | copy-start | bytes 196612
  123.2 16.6 %copy-start.38 = (f32[128,1]{0,1:T(1,128)S(1)}, f32[128,1]{0,1:T(1,128)}, u32[]{:S(2)}) copy-start(f32[128,1]{0,1:T(1,128)} %get-tuple-element.288) | copy-start | bytes 1540
  123.2 20.7 %copy-start.37 = (f32[256]{0:T(256)S(1)}, f32[256]{0:T(256)}, u32[]{:S(2)}) copy-start(f32[256]{0:T(256)} %get-tuple-element.291) | copy-start | bytes 3076
  123.2 21.5 %slice-start = ((bf16[1152,128]{0,1:T(8,128)(2,1)}), bf16[128,128]{0,1:T(8,128)(2,1)S(1)}, s32[]{:S(2)}) async-start(bf16[1152,128]{0,1:T(8,128)(2,1)} %copy-done.29), calls=%async_computation.9 | async-start | bytes 65536 | tf_op jit(solution)/shard_map/slice | solution.py:1002
  123.2 47.9 %all-to-all-start.3 = ((bf16[16,384,128]{2,1,0:T(8,128)(2,1)}), bf16[16,384,128]{2,1,0:T(8,128)(2,1)}, u32[]{:S(2)}, u32[]{:S(2)}) async-start(bf16[16,384,128]{2,1,0:T(8,128)(2,1)} %bitcast.112), calls=%async_computation.3 | async-start | bytes 3145728 | tf_op jit(solution)/shard_map/all_to_all | solution.py:930
  251.1 63.8 %all-to-all-start.5 = ((bf16[16,768,128]{2,1,0:T(8,128)(2,1)}), bf16[16,768,128]{2,1,0:T(8,128)(2,1)}, u32[]{:S(2)}, u32[]{:S(2)}) async-start(bf16[16,768,128]{2,1,0:T(8,128)(2,1)} %bitcast.111), calls=%async_computation.5 | async-start | bytes 6291456 | tf_op jit(solution)/shard_map/all_to_all | solution.py:930
  256.7 3.9 collective-permute-start.1
  331.5 31.3 %all-to-all-start.6 = ((bf16[16,128,128]{2,1,0:T(8,128)(2,1)}), bf16[16,128,128]{2,1,0:T(8,128)(2,1)}, u32[]{:S(2)}, u32[]{:S(2)}) async-start(bf16[16,128,128]{2,1,0:T(8,128)(2,1)} %get-tuple-element.139), calls=%async_computation.6 | async-start | bytes 1048576 | tf_op jit(solution)/shard_map/all_to_all | solution.py:44
  348.3 1.7 collective-permute-start.2
  362.8 5.1 %collective-permute-start.3 = (bf16[16,128,128]{2,1,0:T(8,128)(2,1)}, bf16[16,128,128]{2,1,0:T(8,128)(2,1)}, u32[]{:S(2)}, u32[]{:S(2)}) collective-permute-start(bf16[16,128,128]{2,1,0:T(8,128)(2,1)} %all-to-all-done.6), channel_id=1, source_target_pairs={{0,1},{1,0},{2,3},{3,2},{4,5},{5,4},{6,7},{7,6},{8,9},{9,8},{10,11... | collective-permute-start | bytes 1572872 | tf_op jit(solution)/shard_map/ppermute | solution.py:50
  364.2 15.6 %all-to-all-start.7 = ((bf16[16,80,128]{2,1,0:T(8,128)(2,1)}), bf16[16,80,128]{2,1,0:T(8,128)(2,1)S(1)}, u32[]{:S(2)}, u32[]{:S(2)}) async-start(bf16[16,80,128]{2,1,0:T(8,128)(2,1)} %bitcast.116), calls=%async_computation.7 | async-start | bytes 655360 | tf_op jit(solution)/shard_map/all_to_all | solution.py:44
  380.8 27.5 %all-to-all-start.8 = ((bf16[16,192,128]{2,1,0:T(8,128)(2,1)}), bf16[16,192,128]{2,1,0:T(8,128)(2,1)S(1)}, u32[]{:S(2)}, u32[]{:S(2)}) async-start(bf16[16,192,128]{2,1,0:T(8,128)(2,1)} %shard_map.710), calls=%async_computation.8 | async-start | bytes 1572864 | tf_op jit(solution)/shard_map/all_to_all | solution.py:44
  408.4 2.3 collective-permute-start.4
  (30 other events, 183.8 us)
